TPU v7x, 128 devices: a whole 4x4x4 slice. The times are simulated.
128 devices in a mesh: dom: 8 (over y, core), bulk: 16 (over x, z).
Axes of the slice: x: 4, y: 4, z: 4, core: 2. Of those that a mesh axis runs over, the one named last changes fastest.
Arguments:
- group_pos: float32 [32768, 3, 128], P(('dom', 'bulk')), may hold values from 0 to 1
- group_vel: float32 [32768, 3, 128], P(('dom', 'bulk')), may hold values from -6 to 6
- leaf_pos: float32 [65536, 3, 128], P(('dom', 'bulk')), may hold values from 0 to 1
- leaf_mass: float32 [65536, 128], P(('dom', 'bulk')), may hold values from 0.0002 to 0.002
- node_pos: float32 [3, 65536], P(None, ('dom', 'bulk')), may hold values from 0 to 1
- node_mass: float32 [65536], P(('dom', 'bulk')), may hold values from 0.002 to 0.02
- group_nodes: int32 [32768, 512], P(('dom', 'bulk')), may hold values from 0 to 511
- export_group: int32 [128, 128, 8], P(('dom', 'bulk')), may hold values from 0 to 255
- export_leaf: int32 [128, 128, 8, 2], P(('dom', 'bulk')), may hold values from 0 to 511
- export_count: int32 [128, 128], P(('dom', 'bulk')), may hold values from 0 to 8, as said below
- move_count: int32 [128], P(('dom', 'bulk')), may hold values from 0 to 16, as said below
Outputs:
- migrated: float32 [34816, 6, 128], P(('dom', 'bulk'))
Inputs may be any that keep to these rules, and one draw needn't show every extreme that they name: `export_count`: zero on the diagonal. For each receiver either every other device uses all 8 slots to it, or every sender uses at most 4; at least one receiver is full from every other device. `move_count`: the last device along the curve hands on nothing; some device hands on exactly 16.
All inputs are finite; a program needn't handle non-finite values.
Results may differ from a plain program's by a relative error of at most 0.0003.
Values sent between devices are 32-bit elements; how exact they have to be, the bound alone decides.
No kernel may reach another device: no remote copies, remote signals or barrier semaphores. Data moves between devices by JAX's collectives and lax.ppermute only.
A program may use at most 64 MiB of HBM per device.

v0:
```python
import math

import jax
import jax.numpy as jnp
from jax import lax
from jax.sharding import PartitionSpec as P

MOVE_MAX = 16


soft_sq = 0.001
kick_dt = 0.5


def shifted(value, axis, steps):
    count = lax.axis_size(axis)
    first, last = (max(0, -steps), min(count, count - steps))
    return lax.ppermute(value, axis, [(source, source + steps) for source in range(first, last)])


def attract(targets, src_pos, src_mass):
    offset = src_pos[:, :, None, :] - targets[:, :, :, None]
    dist_sq = jnp.sum(offset * offset, axis=1) + soft_sq
    weight = src_mass[:, None, :] / (dist_sq * jnp.sqrt(dist_sq))
    return jnp.sum(offset * weight[:, None], axis=3)


def blocked_attract(targets, src_pos, src_mass, block_size):
    item_count = targets.shape[0]
    block_size = math.gcd(item_count, block_size)
    rounds = item_count // block_size

    def blocked_one_block(members):
        return attract(members[0], members[1], members[2])

    pieces = (
        targets.reshape((rounds, block_size) + targets.shape[1:]),
        src_pos.reshape((rounds, block_size) + src_pos.shape[1:]),
        src_mass.reshape((rounds, block_size) + src_mass.shape[1:]),
    )
    return lax.map(blocked_one_block, pieces).reshape(targets.shape)


def node_attract(group_pos, node_table, group_nodes, block_size):
    item_count = group_pos.shape[0]
    block_size = math.gcd(item_count, block_size)
    rounds = item_count // block_size
    node_total = node_table.shape[1]
    node_ids = jnp.arange(node_total, dtype=jnp.int32)

    def node_one_block(members):
        targets, wanted = members
        selector = (node_ids[None, :, None] == wanted[:, None, :]).astype(jnp.float32)
        picked = jnp.einsum(
            "cn,bnk->bck",
            node_table,
            selector,
            precision=lax.Precision.HIGHEST,
            preferred_element_type=jnp.float32,
        )
        return attract(targets, picked[:, 0:3], picked[:, 3])

    pieces = (
        group_pos.reshape((rounds, block_size) + group_pos.shape[1:]),
        group_nodes.reshape((rounds, block_size) + group_nodes.shape[1:]),
    )
    return lax.map(node_one_block, pieces).reshape(group_pos.shape)


def opened_leaves(leaf_pos, leaf_mass, leaf_ids):
    total_slots = leaf_ids.shape[0] * leaf_ids.shape[1]
    part_count = leaf_pos.shape[2]
    leaf_count = leaf_ids.shape[2]
    src_pos = jnp.transpose(leaf_pos[leaf_ids], (0, 1, 3, 2, 4)).reshape(
        total_slots, 3, leaf_count * part_count
    )
    src_mass = leaf_mass[leaf_ids].reshape(total_slots, leaf_count * part_count)
    return (src_pos, src_mass)


def per_device(
    group_pos,
    group_vel,
    leaf_pos,
    leaf_mass,
    node_pos,
    node_mass,
    group_nodes,
    export_group,
    export_leaf,
    export_count,
    move_count,
):
    dom_count = lax.axis_size("dom")
    bulk_count = lax.axis_size("bulk")
    peer_count = dom_count * bulk_count
    group_count = group_pos.shape[0]
    part_count = group_pos.shape[2]
    slot_count = export_group.shape[2]
    node_table = jnp.concatenate([node_pos, node_mass[None, :]], axis=0)
    local_acc = node_attract(group_pos, node_table, group_nodes, 16)
    chosen = export_group[0]
    counts = export_count[0]
    wanted = export_leaf[0]
    usable = jnp.arange(slot_count)[None, :] < counts[:, None]
    aim_pos = group_pos[chosen.reshape(-1)]
    aim_rows = aim_pos.reshape(peer_count, slot_count, 3, part_count)
    limits = counts[:, None]
    got_aims, got_wanted, got_limits = (
        lax.all_to_all(aim_rows, ("dom", "bulk"), split_axis=0, concat_axis=0, tiled=True),
        lax.all_to_all(wanted, ("dom", "bulk"), split_axis=0, concat_axis=0, tiled=True),
        lax.all_to_all(limits, ("dom", "bulk"), split_axis=0, concat_axis=0, tiled=True),
    )
    src_pos, src_mass = opened_leaves(leaf_pos, leaf_mass, got_wanted)
    partial_value = blocked_attract(
        got_aims.reshape(peer_count * slot_count, 3, part_count), src_pos, src_mass, 64
    )
    alive_mask = (jnp.arange(slot_count)[None, :] < got_limits).astype(jnp.float32)
    partial_value = (
        partial_value.reshape(peer_count, slot_count, 3, part_count) * alive_mask[:, :, None, None]
    )
    forces = lax.all_to_all(partial_value, ("dom", "bulk"), split_axis=0, concat_axis=0, tiled=True)
    forces = forces.reshape(peer_count * slot_count, 3, part_count)
    selector = (
        (chosen.reshape(-1)[None, :] == jnp.arange(group_count)[:, None])
        & usable.reshape(-1)[None, :]
    ).astype(jnp.float32)
    remote_acc = jnp.dot(
        selector,
        forces.reshape(peer_count * slot_count, 3 * part_count),
        precision=lax.Precision.HIGHEST,
        preferred_element_type=jnp.float32,
    ).reshape(group_count, 3, part_count)
    kicked = jnp.concatenate([group_pos, group_vel + kick_dt * (local_acc + remote_acc)], axis=1)
    leaving = move_count[0]
    leaving_rows = kicked[group_count - MOVE_MAX :]
    arrived, before = shifted((leaving_rows, move_count), ("dom", "bulk"), 1)
    kept_mask = (jnp.arange(group_count) < group_count - leaving).astype(jnp.float32)
    stacked = jnp.concatenate(
        [
            arrived,
            kicked * kept_mask[:, None, None],
            jnp.zeros((MOVE_MAX, 6, part_count), jnp.float32),
        ],
        axis=0,
    )
    return lax.dynamic_slice_in_dim(
        stacked, (MOVE_MAX - before[0]).astype(jnp.int32), group_count + MOVE_MAX, 0
    )


def solution(mesh):
    in_specs = (
        P(("dom", "bulk"), None, None),
        P(("dom", "bulk"), None, None),
        P(("dom", "bulk"), None, None),
        P(("dom", "bulk"), None),
        P(None, ("dom", "bulk")),
        P(("dom", "bulk")),
        P(("dom", "bulk"), None),
        P(("dom", "bulk"), None, None),
        P(("dom", "bulk"), None, None, None),
        P(("dom", "bulk"), None),
        P(("dom", "bulk")),
    )
    out_specs = P(("dom", "bulk"), None, None)
    return jax.shard_map(
        per_device, mesh=mesh, in_specs=in_specs, out_specs=out_specs, check_vma=False
    )
```

profile of v0, /device:TPU:1, one launch (start us, length us, event | category | flops | bytes accessed | tf_op | source)
XLA Modules:
  0.0 628.7 jit_solution(9035773315846373959)
XLA Ops:
  1.5 11.5 %all-to-all-start.2 = ((s32[128,1,1]{2,1,0:T(1,128)}), s32[128,1,1]{2,1,0:T(1,128)S(1)}, u32[]{:S(2)}, u32[]{:S(2)}) async-start(s32[128,1,1]{2,1,0:T(1,128)} %copy.84), calls=%async_computation.2 | async-start | bytes 131072 | tf_op jit(solution)/shard_map/all_to_all | solution.py:112
  15.4 7.1 %all-to-all-done.2 = s32[128,1,1]{2,1,0:T(1,128)S(1)} async-done(((s32[128,1,1]{2,1,0:T(1,128)}), s32[128,1,1]{2,1,0:T(1,128)S(1)}, u32[]{:S(2)}, u32[]{:S(2)}) %all-to-all-start.2) | async-done | bytes 544 | tf_op jit(solution)/shard_map/all_to_all | solution.py:112
  22.5 4.5 all-to-all-start
  27.1 3.9 gather_fusion.1
  32.3 4.7 all-to-all-done
  37.0 5.1 all-to-all-start.1
  42.1 3.6 collective-permute-start.1
  50.5 16.7 %gather_fusion = f32[2048,3,128]{2,0,1:T(8,128)} fusion(f32[512,3,128]{2,0,1:T(8,128)S(1)} %copy-done, s32[2048]{0:T(1024)S(1)} %broadcast_clamp_fusion), kind=kCustom, calls=%fused_computation | custom fusion | bytes 6299648 | tf_op jit(solution)/shard_map/gather | solution.py:74
  67.1 5.5 reshape_reshape.15
  72.7 7.6 %gather_fusion.2 = f32[2048,128]{1,0:T(8,128)} fusion(f32[512,128]{1,0:T(8,128)S(1)} %copy-done.2, s32[2048]{0:T(1024)S(1)} %broadcast_clamp_fusion), kind=kCustom, calls=%fused_computation.2 | custom fusion | bytes 2105344 | tf_op jit(solution)/shard_map/gather | solution.py:77
  84.1 298.1 %while.21 = (s32[]{:T(128)}, f32[16,64,3,128]{3,1,0,2:T(8,128)}, f32[16,64,3,256]{3,1,0,2:T(8,128)}, f32[16,64,3,128]{3,1,0,2:T(8,128)}, f32[16,64,256]{2,1,0:T(8,128)}, /*index=5*/s32[]{:T(128)}) while((s32[]{:T(128)}, f32[16,64,3,128]{3,1,0,2:T(8,128)}, f32[16,64,3,256]{3,1,0,2:T(8,128)}, f32[16,64,3,128]{3,1,0,2:T(8,128)}, ...), condition=%wide.region_7.8_spmd, body=%wide.region_4.7_spmd.sunk | while | flops 41918464 | bytes 35816016 | solution.py:41
  86.2 4.6 fusion.33
  91.6 3.0 fusion.34
  94.6 7.4 %fusion.35 = f32[64,3,128]{2,1,0:T(4,128)S(1)} fusion(f32[64,128,256]{2,1,0:T(8,128)S(1)} %fusion.34, f32[64,3,128]{2,1,0:T(4,128)S(1)} %bitcast.75, f32[64,3,256]{2,1,0:T(4,128)S(1)} %bitcast.73), kind=kLoop, calls=%fused_computation.7.clone.1 | loop fusion | flops 18849792 | bytes 8781824 | tf_op jit(solution)/shard_map/while/body/eval_jaxpr/reduce_sum | solution.py:25
  104.8 4.6 fusion.33
  113.3 7.4 %fusion.35 = f32[64,3,128]{2,1,0:T(4,128)S(1)} fusion(f32[64,128,256]{2,1,0:T(8,128)S(1)} %fusion.34, f32[64,3,128]{2,1,0:T(4,128)S(1)} %bitcast.75, f32[64,3,256]{2,1,0:T(4,128)S(1)} %bitcast.73), kind=kLoop, calls=%fused_computation.7.clone.1 | loop fusion | flops 18849792 | bytes 8781824 | tf_op jit(solution)/shard_map/while/body/eval_jaxpr/reduce_sum | solution.py:25
  123.4 4.6 fusion.33
  131.9 7.4 %fusion.35 = f32[64,3,128]{2,1,0:T(4,128)S(1)} fusion(f32[64,128,256]{2,1,0:T(8,128)S(1)} %fusion.34, f32[64,3,128]{2,1,0:T(4,128)S(1)} %bitcast.75, f32[64,3,256]{2,1,0:T(4,128)S(1)} %bitcast.73), kind=kLoop, calls=%fused_computation.7.clone.1 | loop fusion | flops 18849792 | bytes 8781824 | tf_op jit(solution)/shard_map/while/body/eval_jaxpr/reduce_sum | solution.py:25
  142.1 4.6 fusion.33
  150.5 7.4 %fusion.35 = f32[64,3,128]{2,1,0:T(4,128)S(1)} fusion(f32[64,128,256]{2,1,0:T(8,128)S(1)} %fusion.34, f32[64,3,128]{2,1,0:T(4,128)S(1)} %bitcast.75, f32[64,3,256]{2,1,0:T(4,128)S(1)} %bitcast.73), kind=kLoop, calls=%fused_computation.7.clone.1 | loop fusion | flops 18849792 | bytes 8781824 | tf_op jit(solution)/shard_map/while/body/eval_jaxpr/reduce_sum | solution.py:25
  160.7 4.6 fusion.33
  169.2 7.4 %fusion.35 = f32[64,3,128]{2,1,0:T(4,128)S(1)} fusion(f32[64,128,256]{2,1,0:T(8,128)S(1)} %fusion.34, f32[64,3,128]{2,1,0:T(4,128)S(1)} %bitcast.75, f32[64,3,256]{2,1,0:T(4,128)S(1)} %bitcast.73), kind=kLoop, calls=%fused_computation.7.clone.1 | loop fusion | flops 18849792 | bytes 8781824 | tf_op jit(solution)/shard_map/while/body/eval_jaxpr/reduce_sum | solution.py:25
  179.3 4.6 fusion.33
  187.8 7.4 %fusion.35 = f32[64,3,128]{2,1,0:T(4,128)S(1)} fusion(f32[64,128,256]{2,1,0:T(8,128)S(1)} %fusion.34, f32[64,3,128]{2,1,0:T(4,128)S(1)} %bitcast.75, f32[64,3,256]{2,1,0:T(4,128)S(1)} %bitcast.73), kind=kLoop, calls=%fused_computation.7.clone.1 | loop fusion | flops 18849792 | bytes 8781824 | tf_op jit(solution)/shard_map/while/body/eval_jaxpr/reduce_sum | solution.py:25
  198.0 4.6 fusion.33
  206.4 7.4 %fusion.35 = f32[64,3,128]{2,1,0:T(4,128)S(1)} fusion(f32[64,128,256]{2,1,0:T(8,128)S(1)} %fusion.34, f32[64,3,128]{2,1,0:T(4,128)S(1)} %bitcast.75, f32[64,3,256]{2,1,0:T(4,128)S(1)} %bitcast.73), kind=kLoop, calls=%fused_computation.7.clone.1 | loop fusion | flops 18849792 | bytes 8781824 | tf_op jit(solution)/shard_map/while/body/eval_jaxpr/reduce_sum | solution.py:25
  216.6 4.6 fusion.33
  225.1 7.4 %fusion.35 = f32[64,3,128]{2,1,0:T(4,128)S(1)} fusion(f32[64,128,256]{2,1,0:T(8,128)S(1)} %fusion.34, f32[64,3,128]{2,1,0:T(4,128)S(1)} %bitcast.75, f32[64,3,256]{2,1,0:T(4,128)S(1)} %bitcast.73), kind=kLoop, calls=%fused_computation.7.clone.1 | loop fusion | flops 18849792 | bytes 8781824 | tf_op jit(solution)/shard_map/while/body/eval_jaxpr/reduce_sum | solution.py:25
  235.2 4.6 fusion.33
  243.7 7.4 %fusion.35 = f32[64,3,128]{2,1,0:T(4,128)S(1)} fusion(f32[64,128,256]{2,1,0:T(8,128)S(1)} %fusion.34, f32[64,3,128]{2,1,0:T(4,128)S(1)} %bitcast.75, f32[64,3,256]{2,1,0:T(4,128)S(1)} %bitcast.73), kind=kLoop, calls=%fused_computation.7.clone.1 | loop fusion | flops 18849792 | bytes 8781824 | tf_op jit(solution)/shard_map/while/body/eval_jaxpr/reduce_sum | solution.py:25
  253.9 4.6 fusion.33
  262.3 7.4 %fusion.35 = f32[64,3,128]{2,1,0:T(4,128)S(1)} fusion(f32[64,128,256]{2,1,0:T(8,128)S(1)} %fusion.34, f32[64,3,128]{2,1,0:T(4,128)S(1)} %bitcast.75, f32[64,3,256]{2,1,0:T(4,128)S(1)} %bitcast.73), kind=kLoop, calls=%fused_computation.7.clone.1 | loop fusion | flops 18849792 | bytes 8781824 | tf_op jit(solution)/shard_map/while/body/eval_jaxpr/reduce_sum | solution.py:25
  272.5 4.6 fusion.33
  281.0 7.4 %fusion.35 = f32[64,3,128]{2,1,0:T(4,128)S(1)} fusion(f32[64,128,256]{2,1,0:T(8,128)S(1)} %fusion.34, f32[64,3,128]{2,1,0:T(4,128)S(1)} %bitcast.75, f32[64,3,256]{2,1,0:T(4,128)S(1)} %bitcast.73), kind=kLoop, calls=%fused_computation.7.clone.1 | loop fusion | flops 18849792 | bytes 8781824 | tf_op jit(solution)/shard_map/while/body/eval_jaxpr/reduce_sum | solution.py:25
  291.1 4.6 fusion.33
  299.6 7.4 %fusion.35 = f32[64,3,128]{2,1,0:T(4,128)S(1)} fusion(f32[64,128,256]{2,1,0:T(8,128)S(1)} %fusion.34, f32[64,3,128]{2,1,0:T(4,128)S(1)} %bitcast.75, f32[64,3,256]{2,1,0:T(4,128)S(1)} %bitcast.73), kind=kLoop, calls=%fused_computation.7.clone.1 | loop fusion | flops 18849792 | bytes 8781824 | tf_op jit(solution)/shard_map/while/body/eval_jaxpr/reduce_sum | solution.py:25
  309.8 4.6 fusion.33
  318.2 7.4 %fusion.35 = f32[64,3,128]{2,1,0:T(4,128)S(1)} fusion(f32[64,128,256]{2,1,0:T(8,128)S(1)} %fusion.34, f32[64,3,128]{2,1,0:T(4,128)S(1)} %bitcast.75, f32[64,3,256]{2,1,0:T(4,128)S(1)} %bitcast.73), kind=kLoop, calls=%fused_computation.7.clone.1 | loop fusion | flops 18849792 | bytes 8781824 | tf_op jit(solution)/shard_map/while/body/eval_jaxpr/reduce_sum | solution.py:25
  328.4 4.6 fusion.33
  336.8 7.4 %fusion.35 = f32[64,3,128]{2,1,0:T(4,128)S(1)} fusion(f32[64,128,256]{2,1,0:T(8,128)S(1)} %fusion.34, f32[64,3,128]{2,1,0:T(4,128)S(1)} %bitcast.75, f32[64,3,256]{2,1,0:T(4,128)S(1)} %bitcast.73), kind=kLoop, calls=%fused_computation.7.clone.1 | loop fusion | flops 18849792 | bytes 8781824 | tf_op jit(solution)/shard_map/while/body/eval_jaxpr/reduce_sum | solution.py:25
  347.0 4.6 fusion.33
  355.5 7.4 %fusion.35 = f32[64,3,128]{2,1,0:T(4,128)S(1)} fusion(f32[64,128,256]{2,1,0:T(8,128)S(1)} %fusion.34, f32[64,3,128]{2,1,0:T(4,128)S(1)} %bitcast.75, f32[64,3,256]{2,1,0:T(4,128)S(1)} %bitcast.73), kind=kLoop, calls=%fused_computation.7.clone.1 | loop fusion | flops 18849792 | bytes 8781824 | tf_op jit(solution)/shard_map/while/body/eval_jaxpr/reduce_sum | solution.py:25
  365.7 4.6 fusion.33
  374.1 7.4 %fusion.35 = f32[64,3,128]{2,1,0:T(4,128)S(1)} fusion(f32[64,128,256]{2,1,0:T(8,128)S(1)} %fusion.34, f32[64,3,128]{2,1,0:T(4,128)S(1)} %bitcast.75, f32[64,3,256]{2,1,0:T(4,128)S(1)} %bitcast.73), kind=kLoop, calls=%fused_computation.7.clone.1 | loop fusion | flops 18849792 | bytes 8781824 | tf_op jit(solution)/shard_map/while/body/eval_jaxpr/reduce_sum | solution.py:25
  385.1 9.7 %all-to-all-start.3 = ((f32[128,8,3,128]{3,1,2,0:T(8,128)}), f32[128,8,3,128]{3,1,2,0:T(8,128)S(1)}, u32[]{:S(2)}, u32[]{:S(2)}) async-start(f32[128,8,3,128]{3,1,2,0:T(8,128)} %copy.85), calls=%async_computation.3 | async-start | bytes 3145728 | tf_op jit(solution)/shard_map/all_to_all | solution.py:122
  394.8 216.4 %while.22 = (s32[]{:T(128)}, f32[16,16,3,128]{3,1,0,2:T(8,128)}, s32[16,16,512]{2,1,0:T(8,128)}, f32[4,512]{1,0:T(4,128)S(1)}, f32[16,16,3,128]{3,2,1,0:T(4,128)}, /*index=5*/s32[]{:T(128)}) while((s32[]{:T(128)}, f32[16,16,3,128]{3,1,0,2:T(8,128)}, s32[16,16,512]{2,1,0:T(8,128)}, f32[4,512]{1,0:T(4,128)S(1)}, ...), condition=%wide.region_3.4_spmd.clone, body=%wide.region_0.3_spmd.clone.sunk | while | flops 226486272 | bytes 17547852 | solution.py:67
  395.6 5.2 fusion.37
  409.2 5.2 fusion.37
  422.7 5.2 fusion.37
  436.2 5.2 fusion.37
  449.7 5.2 fusion.37
  463.2 5.2 fusion.37
  476.8 5.2 fusion.37
  490.3 5.2 fusion.37
  503.8 5.2 fusion.37
  517.3 5.2 fusion.37
  530.8 5.2 fusion.37
  544.4 5.2 fusion.37
  557.9 5.2 fusion.37
  571.4 5.2 fusion.37
  584.9 5.2 fusion.37
  598.4 5.2 fusion.37
  618.0 3.4 collective-permute-start
  621.5 6.1 collective-permute-done
  (288 shorter events, 256.9 us)
Async XLA Ops:
  0.0 50.4 %copy-start = (f32[512,3,128]{2,0,1:T(8,128)S(1)}, f32[512,3,128]{2,0,1:T(8,128)}, u32[]{:S(2)}) copy-start(f32[512,3,128]{2,0,1:T(8,128)} %param.17) | copy-start | bytes 2359300
  0.0 27.1 %copy-start.1 = (f32[256,3,128]{2,0,1:T(8,128)S(1)}, f32[256,3,128]{2,0,1:T(8,128)}, u32[]{:S(2)}) copy-start(f32[256,3,128]{2,0,1:T(8,128)} %param.15) | copy-start | bytes 1179652
  1.5 21.0 %all-to-all-start.2 = ((s32[128,1,1]{2,1,0:T(1,128)}), s32[128,1,1]{2,1,0:T(1,128)S(1)}, u32[]{:S(2)}, u32[]{:S(2)}) async-start(s32[128,1,1]{2,1,0:T(1,128)} %copy.84), calls=%async_computation.2 | async-start | bytes 131072 | tf_op jit(solution)/shard_map/all_to_all | solution.py:112
  22.5 14.5 %all-to-all-start = ((s32[128,8,2]{1,2,0:T(2,128)}), s32[128,8,2]{1,2,0:T(2,128)S(1)}, u32[]{:S(2)}, u32[]{:S(2)}) async-start(s32[128,8,2]{1,2,0:T(2,128)} %bitcast.10), calls=%async_computation | async-start | bytes 262144 | tf_op jit(solution)/shard_map/all_to_all | solution.py:111
  31.0 15.9 %copy-start.4 = (f32[3,512]{1,0:T(4,128)S(1)}, f32[3,512]{1,0:T(4,128)}, u32[]{:S(2)}) copy-start(f32[3,512]{1,0:T(4,128)} %param.19) | copy-start | bytes 18436
  31.0 15.8 %copy-start.6 = (f32[512]{0:T(512)S(1)}, f32[512]{0:T(512)}, u32[]{:S(2)}) copy-start(f32[512]{0:T(512)} %param.20) | copy-start | bytes 6148
  37.0 45.9 %all-to-all-start.1 = ((f32[128,8,3,128]{3,1,2,0:T(8,128)}), f32[128,8,3,128]{3,1,2,0:T(8,128)S(1)}, u32[]{:S(2)}, u32[]{:S(2)}) async-start(f32[128,8,3,128]{3,1,2,0:T(8,128)} %copy.79), calls=%async_computation.1 | async-start | bytes 3145728 | tf_op jit(solution)/shard_map/all_to_all | solution.py:110
  42.1 570.0 %collective-permute-start.1 = (s32[1]{0:T(128)}, s32[1]{0:T(128)}, u32[]{:S(2)}, u32[]{:S(2)}) collective-permute-start(s32[1]{0:T(128)} %param.25), channel_id=1, source_target_pairs={{0,1},{1,2},{2,3},{3,4},{4,5},{5,6},{6,7},{7,8},{8,9},{9,10},{10,1... | collective-permute-start | bytes 20 | tf_op jit(solution)/shard_map/ppermute | solution.py:18
  67.1 5.5 copy-start.2
  385.1 228.6 %all-to-all-start.3 = ((f32[128,8,3,128]{3,1,2,0:T(8,128)}), f32[128,8,3,128]{3,1,2,0:T(8,128)S(1)}, u32[]{:S(2)}, u32[]{:S(2)}) async-start(f32[128,8,3,128]{3,1,2,0:T(8,128)} %copy.85), calls=%async_computation.3 | async-start | bytes 3145728 | tf_op jit(solution)/shard_map/all_to_all | solution.py:122
  394.8 217.1 %copy-start.5 = (s32[1,128]{1,0:T(1,128)S(1)}, s32[1,128]{1,0:T(1,128)}, u32[]{:S(2)}) copy-start(s32[1,128]{1,0:T(1,128)} %param.24) | copy-start | bytes 1540
  394.8 220.5 %copy-start.3 = (f32[256,3,128]{2,0,1:T(8,128)S(1)}, f32[256,3,128]{2,0,1:T(8,128)}, u32[]{:S(2)}) copy-start(f32[256,3,128]{2,0,1:T(8,128)} %param.16) | copy-start | bytes 1179652
  618.0 9.7 %collective-permute-start = (f32[16,6,128]{2,0,1:T(8,128)S(1)}, f32[16,6,128]{2,0,1:T(8,128)S(1)}, u32[]{:S(2)}, u32[]{:S(2)}) collective-permute-start(f32[16,6,128]{2,0,1:T(8,128)S(1)} %fusion.23), channel_id=1, source_target_pairs={{0,1},{1,2},{2,3},{3,4},{4,5},{5,6},{6,7},{7,8},{8,9},{9,10},{10,1... | collective-permute-start | bytes 147464 | tf_op jit(solution)/shard_map/ppermute | solution.py:18
where the time goes:
time: 633 us; the launch traced here: 629 us
  other arithmetic  343 us (54%)
  local copies, waits for them, and re-layouts  140 us (22%)
  matrix products  86 us (14%)
  starting transfers between devices  37.9 us (6%)
  waiting for transfers between devices  17.9 us (3%)
    reduce_sum x32, other arithmetic, attract(): return jnp.sum(offset * weight[:, None], axis=3)  159 us
    reduce_sum x32, other arithmetic, attract(): dist_sq = jnp.sum(offset * offset, axis=1) + soft_sq  106 us
    dot_general x16, matrix products, node_one_block(): jnp.einsum('cn,bnk->bck', node_table, selector, precision=lax.Precision.H...  83.3 us
    div x32, other arithmetic, attract(): weight = src_mass[:, None, :] / (dist_sq * jnp.sqrt(dist_sq))  72.1 us
    dynamic_slice x64, local copies, waits for them, and re-layouts, blocked_attract(): return lax.map(blocked_one_block, pieces).reshape(targets.shape)  32.9 us
    gather x1, local copies, waits for them, and re-layouts, opened_leaves(): leaf_pos[leaf_ids]  16.7 us
    div x16, local copies, waits for them, and re-layouts, attract(): weight = src_mass[:, None, :] / (dist_sq * jnp.sqrt(dist_sq))  13.6 us
  transfers between devices with their start and end apart: 6, of which 3 were waited for; matrix products, arithmetic and copies ran while one was open for 89% of the time, Pallas kernels for 0%

commit v1 on v0

v1 whole, which is shorter than its diff:
```python
import functools

import jax
import jax.numpy as jnp
from jax import lax
from jax.experimental import pallas as pl
from jax.experimental.pallas import tpu as pltpu
from jax.sharding import PartitionSpec as P

AXES = ("dom", "bulk")
MOVE_MAX = 16
SOFT_SQ = 0.001
KICK = 0.5
MID = 0.5
LANES = 128
ROWS = 32

f32 = jnp.float32
bf16 = jnp.bfloat16


def dot(a, b):
    return lax.dot_general(a, b, (((1,), (0,)), ((), ())), preferred_element_type=f32)


def dot_t(a, b):
    return lax.dot_general(a, b, (((1,), (1,)), ((), ())), preferred_element_type=f32)


def split3(v):
    a = v.astype(bf16).astype(f32)
    r = v - a
    b = r.astype(bf16).astype(f32)
    return a, b, r - b


def split2(w):
    hi = w.astype(bf16)
    return hi, (w - hi.astype(f32)).astype(bf16)


def target_rows(x):
    rows = []
    for c in range(3):
        a, b, d = split3(x[c])
        rows += [a, a, b, b, a, d]
    rows += list(split3(x[0] * x[0] + x[1] * x[1] + x[2] * x[2]))
    one = jnp.ones_like(x[0])
    return rows + [one, one, one]


def source_rows(y, scale):
    rows = []
    for c in range(3):
        a, b, d = split3(y[c] * (-2.0 * scale))
        rows += [a, b, a, b, d, a]
    one = jnp.ones_like(y[0]) * scale
    rows += [one, one, one]
    rows += list(split3((y[0] * y[0] + y[1] * y[1] + y[2] * y[2] + SOFT_SQ) * scale))
    return rows


def inv_cube(r2):
    rs = lax.rsqrt(r2)
    return rs * rs * rs


def open_kernel(ids_ref, pos_ref, mass_ref, out_ref, table):
    leaf_count = pos_ref.shape[1]

    def build(b, carry):
        first = pl.multiple_of(b * 8, 8)
        for c in range(4):
            v = pos_ref[c, pl.ds(first, 8), :] if c < 3 else mass_ref[pl.ds(first, 8), :]
            table[pl.ds(first * 8 + c, 8, stride=8), :] = v
            table[pl.ds(first * 8 + 4 + c, 8, stride=8), :] = v
        return carry

    lax.fori_loop(0, leaf_count // 8, build, 0)
    upper = lax.broadcasted_iota(jnp.int32, (8, LANES), 0) < 4

    def one_peer(p, carry):
        for s in range(8):
            i0 = pl.multiple_of(ids_ref[p, 2 * s] * 8, 8)
            i1 = pl.multiple_of(ids_ref[p, 2 * s + 1] * 8, 8)
            out_ref[p, pl.ds(s * 8, 8), :] = jnp.where(
                upper, table[pl.ds(i0, 8), :], table[pl.ds(i1, 8), :]
            )
        return carry

    lax.fori_loop(0, out_ref.shape[0], one_peer, 0)


def open_leaves(ids, leaf_pos, leaf_mass):
    peers = ids.shape[0]
    return pl.pallas_call(
        open_kernel,
        out_shape=jax.ShapeDtypeStruct((peers, 64, LANES), f32),
        in_specs=[
            pl.BlockSpec(memory_space=pltpu.SMEM),
            pl.BlockSpec(memory_space=pltpu.VMEM),
            pl.BlockSpec(memory_space=pltpu.VMEM),
        ],
        out_specs=pl.BlockSpec(memory_space=pltpu.VMEM),
        scratch_shapes=[pltpu.VMEM((leaf_pos.shape[1] * 8, LANES), f32)],
        compiler_params=pltpu.CompilerParams(vmem_limit_bytes=24 << 20),
        name="open_leaves",
    )(ids, leaf_pos, leaf_mass)


def local_kernel(pos_ref, node_ref, mass_ref, list_ref, acc_ref, xt_ref, ynt, xk, raw):
    nodes = node_ref.shape[1]
    y = [node_ref[c : c + 1, :] - MID for c in range(3)]
    mass = mass_ref[...]
    yk = jnp.concatenate(source_rows(y, 1.0) + [jnp.zeros((8, nodes), f32)], axis=0)
    ynt[...] = jnp.transpose(yk).astype(bf16)
    tab = jnp.concatenate([mass * y[0], mass * y[1], mass * y[2], mass], axis=0)
    tab = jnp.concatenate([tab, tab], axis=0)
    xk[...] = jnp.zeros_like(xk)
    row128 = lax.broadcasted_iota(jnp.int32, (LANES, nodes), 0)
    row16 = lax.broadcasted_iota(jnp.int32, (16, nodes), 0)
    eye = (
        lax.broadcasted_iota(jnp.int32, (LANES, LANES), 0)
        == lax.broadcasted_iota(jnp.int32, (LANES, LANES), 1)
    ).astype(f32).astype(bf16)
    upper = lax.broadcasted_iota(jnp.int32, (8, LANES), 0) < 4
    raw[...] = jnp.zeros_like(raw)

    def one_block(b, carry):
        first = pl.multiple_of(b * 8, 8)
        x = [pos_ref[c, pl.ds(first, 8), :] - MID for c in range(3)]
        for r, v in enumerate(target_rows(x)):
            xk[pl.ds(r, 8, stride=ROWS), :] = v
        lists = list_ref[pl.ds(first, 8), :]
        counts = []
        for g in range(8):
            wanted = lists[g : g + 1, :]
            low = jnp.where(row128 == (wanted & 127), 1.0, 0.0).astype(bf16)
            high = jnp.where(row16 == (wanted >> 7), 1.0, 0.0).astype(bf16)
            counts.append(dot_t(high, low))
        for p in range(4):
            parts = []
            for h in range(nodes // LANES):
                both = jnp.where(
                    upper, counts[2 * p][h : h + 1, :], counts[2 * p + 1][h : h + 1, :]
                )
                parts.append(tab[:, h * LANES : (h + 1) * LANES] * both)
            a, d, e = split3(jnp.concatenate(parts, axis=1))
            weights = jnp.concatenate([a, d, e, jnp.zeros_like(a)], axis=0).astype(bf16)
            xa = xk[pl.ds(2 * p * ROWS, ROWS), :]
            xb = xk[pl.ds((2 * p + 1) * ROWS, ROWS), :]
            rhs = jnp.concatenate([xa, xb], axis=1).astype(bf16)
            total = jnp.zeros((32, 2 * LANES), f32)
            for h in range(nodes // 256):
                hi, lo = split2(inv_cube(dot(ynt[pl.ds(h * 256, 256), :], rhs)))
                part = weights[:, h * 256 : (h + 1) * 256]
                total = total + dot(part, hi) + dot(part, lo)
            total = total[0:8] + total[8:16] + total[16:24]
            raw[pl.ds(2 * p * 8, 4), :] = total[0:4, :LANES]
            raw[pl.ds((2 * p + 1) * 8, 4), :] = total[4:8, LANES:]
        weight = raw[pl.ds(3, 8, stride=8), :]
        for c in range(3):
            acc_ref[c, pl.ds(first, 8), :] = raw[pl.ds(c, 8, stride=8), :] - x[c] * weight
        xt = dot_t(eye, xk[...].astype(bf16)).astype(bf16)
        xt_ref[2 * b] = xt[:, :LANES]
        xt_ref[2 * b + 1] = xt[:, LANES:]
        return carry

    lax.fori_loop(0, pos_ref.shape[1] // 8, one_block, 0)


def local_pull(pos, node_pos, node_mass, lists):
    groups = pos.shape[1]
    nodes = node_pos.shape[1]
    pairs = groups * LANES * nodes
    return pl.pallas_call(
        local_kernel,
        out_shape=(
            jax.ShapeDtypeStruct(pos.shape, f32),
            jax.ShapeDtypeStruct((groups // 4, LANES, LANES), bf16),
        ),
        in_specs=[pl.BlockSpec(memory_space=pltpu.VMEM)] * 4,
        out_specs=[pl.BlockSpec(memory_space=pltpu.VMEM)] * 2,
        scratch_shapes=[
            pltpu.VMEM((nodes, ROWS), bf16),
            pltpu.VMEM((8 * ROWS, LANES), f32),
            pltpu.VMEM((64, LANES), f32),
        ],
        compiler_params=pltpu.CompilerParams(vmem_limit_bytes=16 << 20),
        cost_estimate=pl.CostEstimate(
            flops=pairs * 2000, bytes_accessed=4 << 20, transcendentals=pairs
        ),
        name="local_pull",
    )(pos, node_pos, node_mass, lists)


def remote_kernel(
    eg_ref, ec_ref, recv_ref, xt_ref, pos_ref, vel_ref, local_ref, out_ref, todo, xt, tile, yk, tk, acc
):
    peers = ec_ref.shape[0]
    groups = pos_ref.shape[1]

    def unpack(q, carry):
        v = xt_ref[q]
        for j in range(4):
            xt[4 * q + j] = v[:, j * ROWS : (j + 1) * ROWS]
        return carry

    lax.fori_loop(0, groups // 4, unpack, 0)

    def clear(i, carry):
        acc[pl.ds(pl.multiple_of(i * 64, 64), 64), :] = jnp.zeros((64, LANES), f32)
        return carry

    lax.fori_loop(0, groups * 16 // 64, clear, 0)
    yk[...] = jnp.zeros_like(yk)
    tk[...] = jnp.zeros_like(tk)

    def enlist(p, count):
        for s in range(8):
            todo[count + s] = p * 8 + s
        return count + ec_ref[p]

    count = lax.fori_loop(0, peers, enlist, 0)
    for s in range(8):
        todo[count + s] = 0

    lane = lax.broadcasted_iota(jnp.int32, (8, LANES), 1).astype(f32)
    scale = 1.0 + lane * (1.0 / LANES)
    lift = scale * jnp.sqrt(scale)

    def one_block(b, carry):
        slots = []
        for s in range(8):
            k = todo[b * 8 + s]
            slots.append(k)
            tile[pl.ds(s * 8, 8), :] = recv_ref[pl.ds(pl.multiple_of(k * 8, 8), 8), :]
        live = (lax.broadcasted_iota(jnp.int32, (8, LANES), 0) + b * 8) < count
        for h in range(2):
            y = [tile[pl.ds(4 * h + c, 8, stride=8), :] - MID for c in range(3)]
            m = tile[pl.ds(4 * h + 3, 8, stride=8), :]
            m = jnp.where(live, m * lift, 0.0)
            for r, v in enumerate(source_rows(y, scale)):
                yk[pl.ds(h * 8 * ROWS + r, 8, stride=ROWS), :] = v
            for c, v in enumerate([m * y[0], m * y[1], m * y[2], m]):
                for j, part in enumerate(split3(v)):
                    tk[pl.ds(h * 128 + 4 * j + c, 8, stride=16), :] = part
        for s in range(8):
            g = eg_ref[slots[s] & 7, slots[s] >> 3]
            rhs = [yk[pl.ds((h * 8 + s) * ROWS, ROWS), :] for h in range(2)]
            r2 = dot(xt[g], jnp.concatenate(rhs, axis=1).astype(bf16))
            hi, lo = split2(inv_cube(r2))
            part = [tk[pl.ds((h * 8 + s) * 16, 16), :] for h in range(2)]
            part = jnp.concatenate(part, axis=1).astype(bf16)
            rows = pl.ds(pl.multiple_of(g * 16, 16), 16)
            acc[rows, :] += dot_t(part, hi) + dot_t(part, lo)
        return carry

    lax.fori_loop(0, (count + 7) // 8, one_block, 0)

    def finish(b, carry):
        first = pl.multiple_of(b * 8, 8)
        rows = pl.ds(first, 8)
        total = []
        for c in range(4):
            v = acc[pl.ds(first * 16 + c, 8, stride=16), :]
            v = v + acc[pl.ds(first * 16 + 4 + c, 8, stride=16), :]
            total.append(v + acc[pl.ds(first * 16 + 8 + c, 8, stride=16), :])
        for c in range(3):
            x = pos_ref[c, rows, :]
            pull = total[c] - (x - MID) * total[3]
            out_ref[c, rows, :] = x
            out_ref[3 + c, rows, :] = vel_ref[c, rows, :] + KICK * (local_ref[c, rows, :] + pull)
        return carry

    lax.fori_loop(0, groups // 8, finish, 0)


def remote_pull(export_group, export_count, recv, xt, pos, vel, local_acc):
    groups = pos.shape[1]
    peers = export_count.shape[0]
    slots = export_group.shape[0]
    smem = pl.BlockSpec(memory_space=pltpu.SMEM)
    vmem = pl.BlockSpec(memory_space=pltpu.VMEM)
    return pl.pallas_call(
        remote_kernel,
        out_shape=jax.ShapeDtypeStruct((6, groups, LANES), f32),
        in_specs=[smem, smem] + [vmem] * 5,
        out_specs=vmem,
        scratch_shapes=[
            pltpu.SMEM((peers * slots + 8,), jnp.int32),
            pltpu.VMEM((groups, LANES, ROWS), bf16),
            pltpu.VMEM((64, LANES), f32),
            pltpu.VMEM((2 * 8 * ROWS, LANES), f32),
            pltpu.VMEM((2 * 8 * 16, LANES), f32),
            pltpu.VMEM((groups * 16, LANES), f32),
        ],
        compiler_params=pltpu.CompilerParams(vmem_limit_bytes=40 << 20),
        name="remote_pull",
    )(export_group, export_count, recv, xt, pos, vel, local_acc)


def shifted(value, axis, steps):
    count = lax.axis_size(axis)
    return lax.ppermute(value, axis, [(source, source + steps) for source in range(count - steps)])


def per_device(
    group_pos,
    group_vel,
    leaf_pos,
    leaf_mass,
    node_pos,
    node_mass,
    group_nodes,
    export_group,
    export_leaf,
    export_count,
    move_count,
):
    peers = export_group.shape[1]
    groups = group_pos.shape[0]
    before = shifted(move_count, AXES, 1)
    ids = lax.all_to_all(
        export_leaf[0].reshape(peers, 16), AXES, split_axis=0, concat_axis=0, tiled=True
    )
    pos = jnp.transpose(group_pos, (1, 0, 2))
    vel = jnp.transpose(group_vel, (1, 0, 2))
    opened = open_leaves(ids, jnp.transpose(leaf_pos, (1, 0, 2)), leaf_mass)
    recv = lax.all_to_all(opened, AXES, split_axis=0, concat_axis=0, tiled=True)
    local_acc, xt = local_pull(pos, node_pos, node_mass[None, :], group_nodes)
    kicked = remote_pull(
        jnp.transpose(export_group[0]),
        export_count[0],
        recv.reshape(peers * 64, LANES),
        xt,
        pos,
        vel,
        local_acc,
    )
    leaving = move_count[0]
    arrived = shifted(kicked[:, groups - MOVE_MAX :], AXES, 1)
    keep = (jnp.arange(groups) < groups - leaving).astype(f32)
    stacked = jnp.concatenate(
        [arrived, kicked * keep[None, :, None], jnp.zeros((6, MOVE_MAX, LANES), f32)], axis=1
    )
    moved = lax.dynamic_slice_in_dim(stacked, MOVE_MAX - before[0], groups + MOVE_MAX, 1)
    return jnp.transpose(moved, (1, 0, 2))


def solution(mesh):
    in_specs = (
        P(AXES, None, None),
        P(AXES, None, None),
        P(AXES, None, None),
        P(AXES, None),
        P(None, AXES),
        P(AXES),
        P(AXES, None),
        P(AXES, None, None),
        P(AXES, None, None, None),
        P(AXES, None),
        P(AXES),
    )
    return jax.shard_map(
        per_device,
        mesh=mesh,
        in_specs=in_specs,
        out_specs=P(AXES, None, None),
        check_vma=False,
    )
```

time: 633 us -> 183 us (0.29)
  the two profiles are of different devices: /device:TPU:1 before, /device:TPU:14 now
where the time goes in v1:
time: 183 us; the launch traced here: 180 us
  Pallas kernels  128 us (70%)
  starting transfers between devices  18.7 us (10%)
  blocking collectives  17.3 us (9%)
  waiting for transfers between devices  7.4 us (4%)
  local copies, waits for them, and re-layouts  5.99 us (3%)
  between operations  1.92 us (1%)
    pallas_call x1, Pallas kernels, remote_pull(): pl.pallas_call(remote_kernel, out_shape=jax.ShapeDtypeStruct((6, groups,...  76.4 us
    pallas_call x1, Pallas kernels, local_pull(): pl.pallas_call(local_kernel, out_shape=(jax.ShapeDtypeStruct(pos.shape, f...  46.2 us
    all_to_all x1, blocking collectives, per_device(): lax.all_to_all(export_leaf[0].reshape(peers, 16), AXES, split_axis=0, con...  17.3 us
    ppermute x2, starting transfers between devices, shifted(): lax.ppermute(value, axis, [(source, source + steps) for source in range(c...  10.5 us
    all_to_all x1, starting transfers between devices, per_device(): recv = lax.all_to_all(opened, AXES, split_axis=0, concat_axis=0, tiled=True)  8.25 us
    ppermute x2, waiting for transfers between devices, shifted(): lax.ppermute(value, axis, [(source, source + steps) for source in range(c...  7.4 us
    unnamed x20, local copies, waits for them, and re-layouts  5.1 us
    pallas_call x1, Pallas kernels, open_leaves(): pl.pallas_call(open_kernel, out_shape=jax.ShapeDtypeStruct((peers, 64, LA...  4.94 us
  transfers between devices with their start and end apart: 3, of which 1 were waited for; matrix products, arithmetic and copies ran while one was open for 0% of the time, Pallas kernels for 26%

profile of v1, /device:TPU:14, one launch (start us, length us, event | category | flops | bytes accessed | tf_op | source)
XLA Modules:
  0.0 180.0 jit_solution(8302075202094617472)
XLA Ops:
  0.0 0.8 copy.14
  0.8 17.3 %all_to_all.16 = s32[128,1,16]{2,1,0:T(1,128)S(1)} all-to-all(s32[128,1,16]{2,1,0:T(1,128)S(1)} %copy.14), channel_id=1, replica_groups=mesh['dom'=8,'bulk'=16] {'dom','bulk'}, dimensions={0} | all-to-all | bytes 16384 | tf_op jit(solution)/shard_map/all_to_all | solution.py:324
  18.1 0.0 copy-start.1
  18.1 1.1 copy-done.1
  19.2 0.0 copy-start.4
  19.2 0.9 copy-done.4
  20.1 4.9 %open_leaves.1 = f32[128,64,128]{2,1,0:T(8,128)S(1)} custom-call(s32[128,16]{1,0:T(8,128)S(1)} %bitcast.20, f32[3,512,128]{2,1,0:T(8,128)S(1)} %bitcast.16, f32[512,128]{1,0:T(8,128)S(1)} %copy-done.4), custom_call_target="tpu_custom_call" | custom-call | tf_op jit(solution)/shard_map/open_leaves/pallas_call | solution.py:96
  25.1 0.0 copy-start
  25.1 2.0 %copy-done = f32[128,64,128]{2,1,0:T(8,128)} copy-done((f32[128,64,128]{2,1,0:T(8,128)}, f32[128,64,128]{2,1,0:T(8,128)S(1)}, u32[]{:S(2)}) %copy-start) | copy-done | bytes 4194328
  27.1 0.0 copy-start.2
  27.1 0.0 copy-start.8
  27.1 0.0 copy-start.9
  27.1 8.2 %all-to-all-start.1 = ((f32[128,64,128]{2,1,0:T(8,128)}), f32[128,64,128]{2,1,0:T(8,128)}, u32[]{:S(2)}, u32[]{:S(2)}) async-start(f32[128,64,128]{2,1,0:T(8,128)} %copy-done), calls=%async_computation.1 | async-start | bytes 8388608 | tf_op jit(solution)/shard_map/all_to_all | solution.py:330
  35.3 3.6 %collective-permute-start.1 = (s32[1]{0:T(128)}, s32[1]{0:T(128)}, u32[]{:S(2)}, u32[]{:S(2)}) collective-permute-start(s32[1]{0:T(128)} %param.21), channel_id=1, source_target_pairs={{0,1},{1,2},{2,3},{3,4},{4,5},{5,6},{6,7},{7,8},{8,9},{9,10},{10,1... | collective-permute-start | bytes 20 | tf_op jit(solution)/shard_map/ppermute | solution.py:305
  39.6 0.0 copy-done.2
  39.7 0.0 copy-done.8
  39.7 0.0 copy-done.9
  39.7 0.0 copy-start.7
  39.7 1.0 copy-done.7
  40.7 0.0 copy-start.3
  40.7 0.0 copy-start.5
  40.7 0.0 copy-start.6
  40.7 46.2 %local_pull.1 = (f32[3,256,128]{2,1,0:T(8,128)S(1)}, bf16[64,128,128]{2,1,0:T(8,128)(2,1)S(1)}) custom-call(f32[3,256,128]{2,1,0:T(8,128)S(1)} %bitcast.17, f32[3,512]{1,0:T(4,128)S(1)} %copy-done.8, f32[1,512]{1,0:T(1,128)S(1)} %bitcast.23, s32[256,512]{1,0:T(8,128)S(1)} %copy-done.7), custom_call_target="tpu_custom_call" | custom-call | flops 33554432000 | bytes 4194304 | tf_op jit(solution)/shard_map/local_pull/pallas_call | solution.py:176
  87.0 0.0 collective-permute-done.1
  88.1 0.1 pad_dynamic-slice_fusion.2
  88.2 0.0 all-to-all-done.1
  88.2 0.0 copy-done.3
  88.2 0.0 copy-done.5
  88.2 0.0 copy-done.6
  88.2 76.4 %remote_pull.1 = f32[6,256,128]{2,1,0:T(8,128)S(1)} custom-call(s32[8,128]{1,0:T(8,128)S(1)} %bitcast.21, s32[128]{0:T(128)S(1)} %bitcast.22, f32[8192,128]{1,0:T(8,128)} %bitcast.6.recv_ref, bf16[64,128,128]{2,1,0:T(8,128)(2,1)S(1)} %get-tuple-element.7.xt_ref, f32[3,256,128]{2,1,0:T(8,128)S(1)} %bitcast.18, f32[3,256,128]{2,1,0:T(8,128)S(1)} %bitcast.19, ...), custom_call_target="tpu_custom_call" | custom-call | tf_op jit(solution)/shard_map/remote_pull/pallas_call | solution.py:285
  164.6 6.8 %collective-permute-start = (f32[6,16,128]{2,1,0:T(8,128)S(1)}, f32[6,16,128]{2,1,0:T(8,128)S(1)}, u32[]{:S(2)}, u32[]{:S(2)}) collective-permute-start(f32[6,16,128]{2,1,0:T(8,128)S(1)} %slice.4), channel_id=1, source_target_pairs={{0,1},{1,2},{2,3},{3,4},{4,5},{5,6},{6,7},{7,8},{8,9},{9,10},{10,1... | collective-permute-start | bytes 147464 | tf_op jit(solution)/shard_map/ppermute | solution.py:305
  171.4 0.1 broadcast_multiply_fusion
  171.5 7.4 %collective-permute-done = f32[6,16,128]{2,1,0:T(8,128)S(1)} collective-permute-done((f32[6,16,128]{2,1,0:T(8,128)S(1)}, f32[6,16,128]{2,1,0:T(8,128)S(1)}, u32[]{:S(2)}, u32[]{:S(2)}) %collective-permute-start) | collective-permute-done | bytes 49184 | tf_op jit(solution)/shard_map/ppermute | solution.py:305
  178.9 1.0 fusion.2
  (3 shorter events, 0.0 us)
Async XLA Ops:
  18.1 1.1 copy-start.1
  19.2 0.9 copy-start.4
  25.1 2.0 %copy-start = (f32[128,64,128]{2,1,0:T(8,128)}, f32[128,64,128]{2,1,0:T(8,128)S(1)}, u32[]{:S(2)}) copy-start(f32[128,64,128]{2,1,0:T(8,128)S(1)} %open_leaves.1) | copy-start | bytes 12582916
  27.1 12.6 %copy-start.2 = (f32[256,3,128]{2,0,1:T(8,128)S(1)}, f32[256,3,128]{2,0,1:T(8,128)}, u32[]{:S(2)}) copy-start(f32[256,3,128]{2,0,1:T(8,128)} %param.11) | copy-start | bytes 1179652
  27.1 12.6 %copy-start.8 = (f32[3,512]{1,0:T(4,128)S(1)}, f32[3,512]{1,0:T(4,128)}, u32[]{:S(2)}) copy-start(f32[3,512]{1,0:T(4,128)} %node_ref.1) | copy-start | bytes 18436
  27.1 12.6 %copy-start.9 = (f32[512]{0:T(512)S(1)}, f32[512]{0:T(512)}, u32[]{:S(2)}) copy-start(f32[512]{0:T(512)} %param.16) | copy-start | bytes 6148
  27.1 61.1 %all-to-all-start.1 = ((f32[128,64,128]{2,1,0:T(8,128)}), f32[128,64,128]{2,1,0:T(8,128)}, u32[]{:S(2)}, u32[]{:S(2)}) async-start(f32[128,64,128]{2,1,0:T(8,128)} %copy-done), calls=%async_computation.1 | async-start | bytes 8388608 | tf_op jit(solution)/shard_map/all_to_all | solution.py:330
  35.3 51.7 %collective-permute-start.1 = (s32[1]{0:T(128)}, s32[1]{0:T(128)}, u32[]{:S(2)}, u32[]{:S(2)}) collective-permute-start(s32[1]{0:T(128)} %param.21), channel_id=1, source_target_pairs={{0,1},{1,2},{2,3},{3,4},{4,5},{5,6},{6,7},{7,8},{8,9},{9,10},{10,1... | collective-permute-start | bytes 20 | tf_op jit(solution)/shard_map/ppermute | solution.py:305
  39.7 1.0 copy-start.7
  40.7 47.5 %copy-start.3 = (f32[256,3,128]{2,0,1:T(8,128)S(1)}, f32[256,3,128]{2,0,1:T(8,128)}, u32[]{:S(2)}) copy-start(f32[256,3,128]{2,0,1:T(8,128)} %param.12) | copy-start | bytes 1179652
  40.7 47.5 %copy-start.5 = (s32[1,128,8]{1,2,0:T(8,128)S(1)}, s32[1,128,8]{1,2,0:T(8,128)}, u32[]{:S(2)}) copy-start(s32[1,128,8]{1,2,0:T(8,128)} %param.18) | copy-start | bytes 12292
  40.7 47.5 %copy-start.6 = (s32[1,128]{1,0:T(1,128)S(1)}, s32[1,128]{1,0:T(1,128)}, u32[]{:S(2)}) copy-start(s32[1,128]{1,0:T(1,128)} %param.20) | copy-start | bytes 1540
  164.6 14.4 %collective-permute-start = (f32[6,16,128]{2,1,0:T(8,128)S(1)}, f32[6,16,128]{2,1,0:T(8,128)S(1)}, u32[]{:S(2)}, u32[]{:S(2)}) collective-permute-start(f32[6,16,128]{2,1,0:T(8,128)S(1)} %slice.4), channel_id=1, source_target_pairs={{0,1},{1,2},{2,3},{3,4},{4,5},{5,6},{6,7},{7,8},{8,9},{9,10},{10,1... | collective-permute-start | bytes 147464 | tf_op jit(solution)/shard_map/ppermute | solution.py:305

commit v2 on v1

--- a/solution.py
+++ b/solution.py
@@ -108,7 +108,7 @@
     )(ids, leaf_pos, leaf_mass)
 
 
-def local_kernel(pos_ref, node_ref, mass_ref, list_ref, acc_ref, xt_ref, ynt, xk, raw):
+def local_kernel(begin, pos_ref, node_ref, mass_ref, list_ref, acc_ref, xt_ref, ynt, xk, raw):
     nodes = node_ref.shape[1]
     y = [node_ref[c : c + 1, :] - MID for c in range(3)]
     mass = mass_ref[...]
@@ -128,10 +128,11 @@
 
     def one_block(b, carry):
         first = pl.multiple_of(b * 8, 8)
-        x = [pos_ref[c, pl.ds(first, 8), :] - MID for c in range(3)]
+        place = pl.multiple_of(begin + b * 8, 8)
+        x = [pos_ref[c, pl.ds(place, 8), :] - MID for c in range(3)]
         for r, v in enumerate(target_rows(x)):
             xk[pl.ds(r, 8, stride=ROWS), :] = v
-        lists = list_ref[pl.ds(first, 8), :]
+        lists = list_ref[pl.ds(place, 8), :]
         counts = []
         for g in range(8):
             wanted = lists[g : g + 1, :]
@@ -166,17 +167,17 @@
         xt_ref[2 * b + 1] = xt[:, LANES:]
         return carry
 
-    lax.fori_loop(0, pos_ref.shape[1] // 8, one_block, 0)
-
-
-def local_pull(pos, node_pos, node_mass, lists):
-    groups = pos.shape[1]
+    lax.fori_loop(0, acc_ref.shape[1] // 8, one_block, 0)
+
+
+def local_pull(pos, node_pos, node_mass, lists, begin, end):
+    groups = end - begin
     nodes = node_pos.shape[1]
     pairs = groups * LANES * nodes
     return pl.pallas_call(
-        local_kernel,
+        functools.partial(local_kernel, begin),
         out_shape=(
-            jax.ShapeDtypeStruct(pos.shape, f32),
+            jax.ShapeDtypeStruct((3, groups, LANES), f32),
             jax.ShapeDtypeStruct((groups // 4, LANES, LANES), bf16),
         ),
         in_specs=[pl.BlockSpec(memory_space=pltpu.VMEM)] * 4,
@@ -195,18 +196,36 @@
 
 
 def remote_kernel(
-    eg_ref, ec_ref, recv_ref, xt_ref, pos_ref, vel_ref, local_ref, out_ref, todo, xt, tile, yk, tk, acc
+    eg_ref,
+    ec_ref,
+    recv_ref,
+    xt0_ref,
+    xt1_ref,
+    pos_ref,
+    vel_ref,
+    local0_ref,
+    local1_ref,
+    out_ref,
+    todo,
+    xt,
+    tile,
+    yk,
+    tk,
+    acc,
 ):
     peers = ec_ref.shape[0]
     groups = pos_ref.shape[1]
 
-    def unpack(q, carry):
-        v = xt_ref[q]
-        for j in range(4):
-            xt[4 * q + j] = v[:, j * ROWS : (j + 1) * ROWS]
-        return carry
-
-    lax.fori_loop(0, groups // 4, unpack, 0)
+    def unpack(ref, base, q, carry):
+        for i in range(4):
+            v = ref[4 * q + i]
+            for j in range(4):
+                xt[base + 16 * q + 4 * i + j] = v[:, j * ROWS : (j + 1) * ROWS]
+        return carry
+
+    early = local0_ref.shape[1]
+    lax.fori_loop(0, early // 16, functools.partial(unpack, xt0_ref, 0), 0)
+    lax.fori_loop(0, (groups - early) // 16, functools.partial(unpack, xt1_ref, early), 0)
 
     def clear(i, carry):
         acc[pl.ds(pl.multiple_of(i * 64, 64), 64), :] = jnp.zeros((64, LANES), f32)
@@ -249,18 +268,18 @@
             g = eg_ref[slots[s] & 7, slots[s] >> 3]
             rhs = [yk[pl.ds((h * 8 + s) * ROWS, ROWS), :] for h in range(2)]
             r2 = dot(xt[g], jnp.concatenate(rhs, axis=1).astype(bf16))
-            hi, lo = split2(inv_cube(r2))
             part = [tk[pl.ds((h * 8 + s) * 16, 16), :] for h in range(2)]
             part = jnp.concatenate(part, axis=1).astype(bf16)
             rows = pl.ds(pl.multiple_of(g * 16, 16), 16)
-            acc[rows, :] += dot_t(part, hi) + dot_t(part, lo)
+            acc[rows, :] += dot_t(part, inv_cube(r2).astype(bf16))
         return carry
 
     lax.fori_loop(0, (count + 7) // 8, one_block, 0)
 
-    def finish(b, carry):
-        first = pl.multiple_of(b * 8, 8)
+    def finish(ref, base, b, carry):
+        first = pl.multiple_of(base + b * 8, 8)
         rows = pl.ds(first, 8)
+        near = pl.ds(pl.multiple_of(b * 8, 8), 8)
         total = []
         for c in range(4):
             v = acc[pl.ds(first * 16 + c, 8, stride=16), :]
@@ -270,13 +289,14 @@
             x = pos_ref[c, rows, :]
             pull = total[c] - (x - MID) * total[3]
             out_ref[c, rows, :] = x
-            out_ref[3 + c, rows, :] = vel_ref[c, rows, :] + KICK * (local_ref[c, rows, :] + pull)
-        return carry
-
-    lax.fori_loop(0, groups // 8, finish, 0)
-
-
-def remote_pull(export_group, export_count, recv, xt, pos, vel, local_acc):
+            out_ref[3 + c, rows, :] = vel_ref[c, rows, :] + KICK * (ref[c, near, :] + pull)
+        return carry
+
+    lax.fori_loop(0, early // 8, functools.partial(finish, local0_ref, 0), 0)
+    lax.fori_loop(0, (groups - early) // 8, functools.partial(finish, local1_ref, early), 0)
+
+
+def remote_pull(export_group, export_count, recv, pos, vel, near0, near1):
     groups = pos.shape[1]
     peers = export_count.shape[0]
     slots = export_group.shape[0]
@@ -285,7 +305,7 @@
     return pl.pallas_call(
         remote_kernel,
         out_shape=jax.ShapeDtypeStruct((6, groups, LANES), f32),
-        in_specs=[smem, smem] + [vmem] * 5,
+        in_specs=[smem, smem] + [vmem] * 7,
         out_specs=vmem,
         scratch_shapes=[
             pltpu.SMEM((peers * slots + 8,), jnp.int32),
@@ -297,7 +317,7 @@
         ],
         compiler_params=pltpu.CompilerParams(vmem_limit_bytes=40 << 20),
         name="remote_pull",
-    )(export_group, export_count, recv, xt, pos, vel, local_acc)
+    )(export_group, export_count, recv, near0[1], near1[1], pos, vel, near0[0], near1[0])
 
 
 def shifted(value, axis, steps):
@@ -320,31 +340,38 @@
 ):
     peers = export_group.shape[1]
     groups = group_pos.shape[0]
-    before = shifted(move_count, AXES, 1)
-    ids = lax.all_to_all(
-        export_leaf[0].reshape(peers, 16), AXES, split_axis=0, concat_axis=0, tiled=True
-    )
+    early = groups * 3 // 16
+    asked = jnp.concatenate(
+        [export_leaf[0].reshape(peers, 16), jnp.broadcast_to(move_count[:, None], (peers, 1))], axis=1
+    )
+    got = lax.all_to_all(asked, AXES, split_axis=0, concat_axis=0, tiled=True)
     pos = jnp.transpose(group_pos, (1, 0, 2))
     vel = jnp.transpose(group_vel, (1, 0, 2))
-    opened = open_leaves(ids, jnp.transpose(leaf_pos, (1, 0, 2)), leaf_mass)
+    mass = node_mass[None, :]
+    near0 = local_pull(pos, node_pos, mass, group_nodes, 0, early)
+    got, near0 = lax.optimization_barrier((got, near0))
+    opened = open_leaves(got, jnp.transpose(leaf_pos, (1, 0, 2)), leaf_mass)
+    opened, mass = lax.optimization_barrier((opened, mass))
     recv = lax.all_to_all(opened, AXES, split_axis=0, concat_axis=0, tiled=True)
-    local_acc, xt = local_pull(pos, node_pos, node_mass[None, :], group_nodes)
+    near1 = local_pull(pos, node_pos, mass, group_nodes, early, groups)
     kicked = remote_pull(
         jnp.transpose(export_group[0]),
         export_count[0],
         recv.reshape(peers * 64, LANES),
-        xt,
         pos,
         vel,
-        local_acc,
-    )
+        near0,
+        near1,
+    )
+    me = lax.axis_index(AXES)
+    before = jnp.where(me > 0, got[jnp.maximum(me - 1, 0), 16], 0)
     leaving = move_count[0]
     arrived = shifted(kicked[:, groups - MOVE_MAX :], AXES, 1)
     keep = (jnp.arange(groups) < groups - leaving).astype(f32)
     stacked = jnp.concatenate(
         [arrived, kicked * keep[None, :, None], jnp.zeros((6, MOVE_MAX, LANES), f32)], axis=1
     )
-    moved = lax.dynamic_slice_in_dim(stacked, MOVE_MAX - before[0], groups + MOVE_MAX, 1)
+    moved = lax.dynamic_slice_in_dim(stacked, MOVE_MAX - before, groups + MOVE_MAX, 1)
     return jnp.transpose(moved, (1, 0, 2))
 
 

time: 183 us -> 146 us (0.80)
  the two profiles are of different devices: /device:TPU:14 before, /device:TPU:1 now
where the time goes in v2:
time: 146 us; the launch traced here: 147 us
  Pallas kernels  93.1 us (64%)
  starting transfers between devices  23.6 us (16%)
  waiting for transfers between devices  18.7 us (13%)
  local copies, waits for them, and re-layouts  8.57 us (6%)
  between operations  1.46 us (1%)
    pallas_call x2, Pallas kernels, local_pull(): pl.pallas_call(functools.partial(local_kernel, begin), out_shape=(jax.Sha...  46.4 us
    pallas_call x1, Pallas kernels, remote_pull(): pl.pallas_call(remote_kernel, out_shape=jax.ShapeDtypeStruct((6, groups,...  41.8 us
    all_to_all x1, waiting for transfers between devices, per_device(): recv = lax.all_to_all(opened, AXES, split_axis=0, concat_axis=0, tiled=True)  12.1 us
    all_to_all x1, starting transfers between devices, per_device(): got = lax.all_to_all(asked, AXES, split_axis=0, concat_axis=0, tiled=True)  11.5 us
    all_to_all x1, starting transfers between devices, per_device(): recv = lax.all_to_all(opened, AXES, split_axis=0, concat_axis=0, tiled=True)  10.2 us
    ppermute x1, waiting for transfers between devices, shifted(): lax.ppermute(value, axis, [(source, source + steps) for source in range(c...  6.67 us
    unnamed x28, local copies, waits for them, and re-layouts  6.45 us
    pallas_call x1, Pallas kernels, open_leaves(): pl.pallas_call(open_kernel, out_shape=jax.ShapeDtypeStruct((peers, 64, LA...  4.95 us
  transfers between devices with their start and end apart: 3, of which 2 were waited for; matrix products, arithmetic and copies ran while one was open for 1% of the time, Pallas kernels for 32%

profile of v2, /device:TPU:1, one launch (start us, length us, event | category | flops | bytes accessed | tf_op | source)
XLA Modules:
  0.0 146.7 jit_solution(7136604065384649423)
XLA Ops:
  0.7 0.7 pad_bitcast_fusion
  1.4 0.7 copy.14
  2.1 11.5 %all-to-all-start = ((s32[128,1,17]{2,1,0:T(1,128)}), s32[128,1,17]{2,1,0:T(1,128)S(1)}, u32[]{:S(2)}, u32[]{:S(2)}) async-start(s32[128,1,17]{2,1,0:T(1,128)} %copy.14), calls=%async_computation | async-start | bytes 131072 | tf_op jit(solution)/shard_map/all_to_all | solution.py:347
  13.6 0.0 copy-start.2
  13.6 1.0 copy-done.2
  14.6 0.0 copy-start.8
  14.6 1.0 copy-done.8
  15.6 0.0 copy-start.10
  15.6 0.7 copy-done.10
  16.3 0.0 copy-start.12
  16.3 0.7 copy-done.12
  17.0 0.0 copy-start.1
  17.0 0.0 copy-start.5
  17.0 8.8 %local_pull.2 = (f32[3,48,128]{2,1,0:T(8,128)S(1)}, bf16[12,128,128]{2,1,0:T(8,128)(2,1)S(1)}) custom-call(f32[3,256,128]{2,1,0:T(8,128)S(1)} %bitcast.20, f32[3,512]{1,0:T(4,128)S(1)} %copy-done.10, f32[1,512]{1,0:T(1,128)S(1)} %bitcast.28, s32[256,512]{1,0:T(8,128)S(1)} %copy-done.8), custom_call_target="tpu_custom_call" | custom-call | flops 6291456000 | bytes 4194304 | tf_op jit(solution)/shard_map/local_pull/pallas_call | solution.py:177
  25.8 0.0 all-to-all-done
  25.8 0.0 copy-done.1
  25.8 0.0 copy-done.5
  25.9 4.9 %open_leaves.1 = f32[128,64,128]{2,1,0:T(8,128)S(1)} custom-call(s32[128,17]{1,0:T(8,128)S(1)} %bitcast.24, f32[3,512,128]{2,1,0:T(8,128)S(1)} %bitcast.19, f32[512,128]{1,0:T(8,128)S(1)} %copy-done.5), custom_call_target="tpu_custom_call" | custom-call | tf_op jit(solution)/shard_map/open_leaves/pallas_call | solution.py:96
  30.8 0.0 copy-start
  30.8 2.0 %copy-done = f32[128,64,128]{2,1,0:T(8,128)} copy-done((f32[128,64,128]{2,1,0:T(8,128)}, f32[128,64,128]{2,1,0:T(8,128)S(1)}, u32[]{:S(2)}) %copy-start) | copy-done | bytes 4194328
  32.8 0.0 copy-start.3
  32.8 0.0 copy-start.11
  32.8 0.0 copy-start.13
  32.8 10.2 %all-to-all-start.1 = ((f32[128,64,128]{2,1,0:T(8,128)}), f32[128,64,128]{2,1,0:T(8,128)}, u32[]{:S(2)}, u32[]{:S(2)}) async-start(f32[128,64,128]{2,1,0:T(8,128)} %copy-done), calls=%async_computation.1 | async-start | bytes 8388608 | tf_op jit(solution)/shard_map/all_to_all | solution.py:355
  43.0 0.6 constant_dynamic-slice_fusion
  44.3 0.1 pad_dynamic-slice_fusion.2
  44.4 0.0 copy-done.3
  44.4 0.0 copy-done.11
  44.4 0.0 copy-done.13
  44.4 0.0 copy-start.9
  44.4 1.0 copy-done.9
  45.4 0.0 copy-start.4
  45.4 0.0 copy-start.6
  45.4 0.0 copy-start.7
  45.4 37.6 %local_pull.3 = (f32[3,208,128]{2,1,0:T(8,128)S(1)}, bf16[52,128,128]{2,1,0:T(8,128)(2,1)S(1)}) custom-call(f32[3,256,128]{2,1,0:T(8,128)S(1)} %bitcast.21, f32[3,512]{1,0:T(4,128)S(1)} %copy-done.11, f32[1,512]{1,0:T(1,128)S(1)} %bitcast.29, s32[256,512]{1,0:T(8,128)S(1)} %copy-done.9), custom_call_target="tpu_custom_call" | custom-call | flops 27262976000 | bytes 4194304 | tf_op jit(solution)/shard_map/local_pull/pallas_call | solution.py:177
  83.0 12.1 %all-to-all-done.1 = f32[128,64,128]{2,1,0:T(8,128)} async-done(((f32[128,64,128]{2,1,0:T(8,128)}), f32[128,64,128]{2,1,0:T(8,128)}, u32[]{:S(2)}, u32[]{:S(2)}) %all-to-all-start.1) | async-done | bytes 4194336 | tf_op jit(solution)/shard_map/all_to_all | solution.py:355
  95.1 0.0 copy-done.4
  95.1 0.0 copy-done.6
  95.1 0.0 copy-done.7
  95.1 41.8 %remote_pull.1 = f32[6,256,128]{2,1,0:T(8,128)S(1)} custom-call(s32[8,128]{1,0:T(8,128)S(1)} %bitcast.26, s32[128]{0:T(128)S(1)} %bitcast.27, f32[8192,128]{1,0:T(8,128)} %bitcast.10.recv_ref, bf16[12,128,128]{2,1,0:T(8,128)(2,1)S(1)} %get-tuple-element.18.xt0_ref, bf16[52,128,128]{2,1,0:T(8,128)(2,1)S(1)} %get-tuple-element.20.xt1_ref, ...), custom_call_target="tpu_custom_call" | custom-call | tf_op jit(solution)/shard_map/remote_pull/pallas_call | solution.py:305
  137.0 1.9 %collective-permute-start = (f32[6,16,128]{2,1,0:T(8,128)S(1)}, f32[6,16,128]{2,1,0:T(8,128)S(1)}, u32[]{:S(2)}, u32[]{:S(2)}) collective-permute-start(f32[6,16,128]{2,1,0:T(8,128)S(1)} %slice.4), channel_id=1, source_target_pairs={{0,1},{1,2},{2,3},{3,4},{4,5},{5,6},{6,7},{7,8},{8,9},{9,10},{10,1... | collective-permute-start | bytes 147464 | tf_op jit(solution)/shard_map/ppermute | solution.py:325
  138.9 0.1 broadcast_multiply_fusion
  139.0 6.7 %collective-permute-done = f32[6,16,128]{2,1,0:T(8,128)S(1)} collective-permute-done((f32[6,16,128]{2,1,0:T(8,128)S(1)}, f32[6,16,128]{2,1,0:T(8,128)S(1)}, u32[]{:S(2)}, u32[]{:S(2)}) %collective-permute-start) | collective-permute-done | bytes 49184 | tf_op jit(solution)/shard_map/ppermute | solution.py:325
  145.7 1.0 fusion.2
  (3 shorter events, 0.0 us)
Async XLA Ops:
  2.1 23.7 %all-to-all-start = ((s32[128,1,17]{2,1,0:T(1,128)}), s32[128,1,17]{2,1,0:T(1,128)S(1)}, u32[]{:S(2)}, u32[]{:S(2)}) async-start(s32[128,1,17]{2,1,0:T(1,128)} %copy.14), calls=%async_computation | async-start | bytes 131072 | tf_op jit(solution)/shard_map/all_to_all | solution.py:347
  13.6 1.0 copy-start.2
  14.6 1.0 copy-start.8
  15.6 0.7 copy-start.10
  16.3 0.7 copy-start.12
  17.0 8.8 %copy-start.1 = (f32[512,3,128]{2,0,1:T(8,128)S(1)}, f32[512,3,128]{2,0,1:T(8,128)}, u32[]{:S(2)}) copy-start(f32[512,3,128]{2,0,1:T(8,128)} %param.13) | copy-start | bytes 2359300
  17.0 8.8 %copy-start.5 = (f32[512,128]{1,0:T(8,128)S(1)}, f32[512,128]{1,0:T(8,128)}, u32[]{:S(2)}) copy-start(f32[512,128]{1,0:T(8,128)} %mass_ref.1) | copy-start | bytes 786436
  30.8 2.0 %copy-start = (f32[128,64,128]{2,1,0:T(8,128)}, f32[128,64,128]{2,1,0:T(8,128)S(1)}, u32[]{:S(2)}) copy-start(f32[128,64,128]{2,1,0:T(8,128)S(1)} %open_leaves.1) | copy-start | bytes 12582916
  32.8 11.6 %copy-start.3 = (f32[256,3,128]{2,0,1:T(8,128)S(1)}, f32[256,3,128]{2,0,1:T(8,128)}, u32[]{:S(2)}) copy-start(f32[256,3,128]{2,0,1:T(8,128)} %param.11) | copy-start | bytes 1179652
  32.8 11.6 %copy-start.11 = (f32[3,512]{1,0:T(4,128)S(1)}, f32[3,512]{1,0:T(4,128)}, u32[]{:S(2)}) copy-start(f32[3,512]{1,0:T(4,128)} %node_ref.3) | copy-start | bytes 18436
  32.8 11.6 %copy-start.13 = (f32[512]{0:T(512)S(1)}, f32[512]{0:T(512)}, u32[]{:S(2)}) copy-start(f32[512]{0:T(512)} %param.16) | copy-start | bytes 6148
  32.8 62.3 %all-to-all-start.1 = ((f32[128,64,128]{2,1,0:T(8,128)}), f32[128,64,128]{2,1,0:T(8,128)}, u32[]{:S(2)}, u32[]{:S(2)}) async-start(f32[128,64,128]{2,1,0:T(8,128)} %copy-done), calls=%async_computation.1 | async-start | bytes 8388608 | tf_op jit(solution)/shard_map/all_to_all | solution.py:355
  44.4 1.0 copy-start.9
  45.4 49.7 %copy-start.4 = (f32[256,3,128]{2,0,1:T(8,128)S(1)}, f32[256,3,128]{2,0,1:T(8,128)}, u32[]{:S(2)}) copy-start(f32[256,3,128]{2,0,1:T(8,128)} %param.12) | copy-start | bytes 1179652
  45.4 49.7 %copy-start.6 = (s32[1,128,8]{1,2,0:T(8,128)S(1)}, s32[1,128,8]{1,2,0:T(8,128)}, u32[]{:S(2)}) copy-start(s32[1,128,8]{1,2,0:T(8,128)} %param.18) | copy-start | bytes 12292
  45.4 49.7 %copy-start.7 = (s32[1,128]{1,0:T(1,128)S(1)}, s32[1,128]{1,0:T(1,128)}, u32[]{:S(2)}) copy-start(s32[1,128]{1,0:T(1,128)} %param.20) | copy-start | bytes 1540
  137.0 8.7 %collective-permute-start = (f32[6,16,128]{2,1,0:T(8,128)S(1)}, f32[6,16,128]{2,1,0:T(8,128)S(1)}, u32[]{:S(2)}, u32[]{:S(2)}) collective-permute-start(f32[6,16,128]{2,1,0:T(8,128)S(1)} %slice.4), channel_id=1, source_target_pairs={{0,1},{1,2},{2,3},{3,4},{4,5},{5,6},{6,7},{7,8},{8,9},{9,10},{10,1... | collective-permute-start | bytes 147464 | tf_op jit(solution)/shard_map/ppermute | solution.py:325

commit v3 on v2

--- a/solution.py
+++ b/solution.py
@@ -14,6 +14,7 @@
 MID = 0.5
 LANES = 128
 ROWS = 32
+SPAN = 4
 
 f32 = jnp.float32
 bf16 = jnp.bfloat16
@@ -65,7 +66,7 @@
     return rs * rs * rs
 
 
-def open_kernel(ids_ref, pos_ref, mass_ref, out_ref, table):
+def open_kernel(base, ids_ref, pos_ref, mass_ref, out_ref, table):
     leaf_count = pos_ref.shape[1]
 
     def build(b, carry):
@@ -76,26 +77,26 @@
             table[pl.ds(first * 8 + 4 + c, 8, stride=8), :] = v
         return carry
 
-    lax.fori_loop(0, leaf_count // 8, build, 0)
+    lax.fori_loop(0, leaf_count // 8, build, 0, unroll=4)
     upper = lax.broadcasted_iota(jnp.int32, (8, LANES), 0) < 4
 
     def one_peer(p, carry):
-        for s in range(8):
-            i0 = pl.multiple_of(ids_ref[p, 2 * s] * 8, 8)
-            i1 = pl.multiple_of(ids_ref[p, 2 * s + 1] * 8, 8)
+        for s in range(SPAN):
+            i0 = pl.multiple_of(ids_ref[p, 2 * (base + s)] * 8, 8)
+            i1 = pl.multiple_of(ids_ref[p, 2 * (base + s) + 1] * 8, 8)
             out_ref[p, pl.ds(s * 8, 8), :] = jnp.where(
                 upper, table[pl.ds(i0, 8), :], table[pl.ds(i1, 8), :]
             )
         return carry
 
-    lax.fori_loop(0, out_ref.shape[0], one_peer, 0)
-
-
-def open_leaves(ids, leaf_pos, leaf_mass):
+    lax.fori_loop(0, out_ref.shape[0], one_peer, 0, unroll=4)
+
+
+def open_leaves(ids, leaf_pos, leaf_mass, base):
     peers = ids.shape[0]
     return pl.pallas_call(
-        open_kernel,
-        out_shape=jax.ShapeDtypeStruct((peers, 64, LANES), f32),
+        functools.partial(open_kernel, base),
+        out_shape=jax.ShapeDtypeStruct((peers, SPAN * 8, LANES), f32),
         in_specs=[
             pl.BlockSpec(memory_space=pltpu.SMEM),
             pl.BlockSpec(memory_space=pltpu.VMEM),
@@ -103,12 +104,14 @@
         ],
         out_specs=pl.BlockSpec(memory_space=pltpu.VMEM),
         scratch_shapes=[pltpu.VMEM((leaf_pos.shape[1] * 8, LANES), f32)],
-        compiler_params=pltpu.CompilerParams(vmem_limit_bytes=24 << 20),
+        compiler_params=pltpu.CompilerParams(vmem_limit_bytes=12 << 20),
         name="open_leaves",
     )(ids, leaf_pos, leaf_mass)
 
 
-def local_kernel(begin, pos_ref, node_ref, mass_ref, list_ref, acc_ref, xt_ref, ynt, xk, raw):
+def local_kernel(begin, emit, pos_ref, node_ref, mass_ref, list_ref, acc_ref, *rest):
+    xt_ref = rest[0] if emit else None
+    ynt, xk, raw = rest[-3:]
     nodes = node_ref.shape[1]
     y = [node_ref[c : c + 1, :] - MID for c in range(3)]
     mass = mass_ref[...]
@@ -119,19 +122,29 @@
     xk[...] = jnp.zeros_like(xk)
     row128 = lax.broadcasted_iota(jnp.int32, (LANES, nodes), 0)
     row16 = lax.broadcasted_iota(jnp.int32, (16, nodes), 0)
-    eye = (
-        lax.broadcasted_iota(jnp.int32, (LANES, LANES), 0)
-        == lax.broadcasted_iota(jnp.int32, (LANES, LANES), 1)
-    ).astype(f32).astype(bf16)
     upper = lax.broadcasted_iota(jnp.int32, (8, LANES), 0) < 4
     raw[...] = jnp.zeros_like(raw)
+
+    def stage(place):
+        x = [pos_ref[c, pl.ds(place, 8), :] - MID for c in range(3)]
+        for r, v in enumerate(target_rows(x)):
+            xk[pl.ds(r, 8, stride=ROWS), :] = v
+        if emit:
+            for g in range(8):
+                xt_ref[place + g] = jnp.transpose(xk[pl.ds(g * ROWS, ROWS), :]).astype(bf16)
+        return x
+
+    def only_stage(b, carry):
+        stage(pl.multiple_of(b * 8, 8))
+        return carry
+
+    if emit:
+        lax.fori_loop(0, begin // 8, only_stage, 0)
 
     def one_block(b, carry):
         first = pl.multiple_of(b * 8, 8)
         place = pl.multiple_of(begin + b * 8, 8)
-        x = [pos_ref[c, pl.ds(place, 8), :] - MID for c in range(3)]
-        for r, v in enumerate(target_rows(x)):
-            xk[pl.ds(r, 8, stride=ROWS), :] = v
+        x = stage(place)
         lists = list_ref[pl.ds(place, 8), :]
         counts = []
         for g in range(8):
@@ -153,35 +166,37 @@
             rhs = jnp.concatenate([xa, xb], axis=1).astype(bf16)
             total = jnp.zeros((32, 2 * LANES), f32)
             for h in range(nodes // 256):
-                hi, lo = split2(inv_cube(dot(ynt[pl.ds(h * 256, 256), :], rhs)))
+                his, los = [], []
+                for k in range(256 // 128):
+                    rows = pl.ds(h * 256 + k * 128, 128)
+                    a, d = split2(inv_cube(dot(ynt[rows, :], rhs)))
+                    his.append(a)
+                    los.append(d)
                 part = weights[:, h * 256 : (h + 1) * 256]
-                total = total + dot(part, hi) + dot(part, lo)
+                total = total + dot(part, jnp.concatenate(his, axis=0)) + dot(part, jnp.concatenate(los, axis=0))
             total = total[0:8] + total[8:16] + total[16:24]
             raw[pl.ds(2 * p * 8, 4), :] = total[0:4, :LANES]
             raw[pl.ds((2 * p + 1) * 8, 4), :] = total[4:8, LANES:]
         weight = raw[pl.ds(3, 8, stride=8), :]
         for c in range(3):
             acc_ref[c, pl.ds(first, 8), :] = raw[pl.ds(c, 8, stride=8), :] - x[c] * weight
-        xt = dot_t(eye, xk[...].astype(bf16)).astype(bf16)
-        xt_ref[2 * b] = xt[:, :LANES]
-        xt_ref[2 * b + 1] = xt[:, LANES:]
         return carry
 
     lax.fori_loop(0, acc_ref.shape[1] // 8, one_block, 0)
 
 
-def local_pull(pos, node_pos, node_mass, lists, begin, end):
+def local_pull(pos, node_pos, node_mass, lists, begin, end, emit):
     groups = end - begin
     nodes = node_pos.shape[1]
     pairs = groups * LANES * nodes
+    out_shape = [jax.ShapeDtypeStruct((3, groups, LANES), f32)]
+    if emit:
+        out_shape.append(jax.ShapeDtypeStruct((pos.shape[1], LANES, ROWS), bf16))
     return pl.pallas_call(
-        functools.partial(local_kernel, begin),
-        out_shape=(
-            jax.ShapeDtypeStruct((3, groups, LANES), f32),
-            jax.ShapeDtypeStruct((groups // 4, LANES, LANES), bf16),
-        ),
+        functools.partial(local_kernel, begin, emit),
+        out_shape=out_shape,
         in_specs=[pl.BlockSpec(memory_space=pltpu.VMEM)] * 4,
-        out_specs=[pl.BlockSpec(memory_space=pltpu.VMEM)] * 2,
+        out_specs=[pl.BlockSpec(memory_space=pltpu.VMEM)] * len(out_shape),
         scratch_shapes=[
             pltpu.VMEM((nodes, ROWS), bf16),
             pltpu.VMEM((8 * ROWS, LANES), f32),
@@ -195,52 +210,16 @@
     )(pos, node_pos, node_mass, lists)
 
 
-def remote_kernel(
-    eg_ref,
-    ec_ref,
-    recv_ref,
-    xt0_ref,
-    xt1_ref,
-    pos_ref,
-    vel_ref,
-    local0_ref,
-    local1_ref,
-    out_ref,
-    todo,
-    xt,
-    tile,
-    yk,
-    tk,
-    acc,
-):
-    peers = ec_ref.shape[0]
-    groups = pos_ref.shape[1]
-
-    def unpack(ref, base, q, carry):
-        for i in range(4):
-            v = ref[4 * q + i]
-            for j in range(4):
-                xt[base + 16 * q + 4 * i + j] = v[:, j * ROWS : (j + 1) * ROWS]
-        return carry
-
-    early = local0_ref.shape[1]
-    lax.fori_loop(0, early // 16, functools.partial(unpack, xt0_ref, 0), 0)
-    lax.fori_loop(0, (groups - early) // 16, functools.partial(unpack, xt1_ref, early), 0)
-
-    def clear(i, carry):
-        acc[pl.ds(pl.multiple_of(i * 64, 64), 64), :] = jnp.zeros((64, LANES), f32)
-        return carry
-
-    lax.fori_loop(0, groups * 16 // 64, clear, 0)
+def exported_pull(base, eg_ref, ec_ref, recv_ref, xt_ref, acc, todo, tile, yk, tk):
     yk[...] = jnp.zeros_like(yk)
     tk[...] = jnp.zeros_like(tk)
 
     def enlist(p, count):
-        for s in range(8):
-            todo[count + s] = p * 8 + s
-        return count + ec_ref[p]
-
-    count = lax.fori_loop(0, peers, enlist, 0)
+        for s in range(SPAN):
+            todo[count + s] = p * SPAN + s
+        return count + jnp.clip(ec_ref[p] - base, 0, SPAN)
+
+    count = lax.fori_loop(0, ec_ref.shape[0], enlist, 0, unroll=4)
     for s in range(8):
         todo[count + s] = 0
 
@@ -265,9 +244,9 @@
                 for j, part in enumerate(split3(v)):
                     tk[pl.ds(h * 128 + 4 * j + c, 8, stride=16), :] = part
         for s in range(8):
-            g = eg_ref[slots[s] & 7, slots[s] >> 3]
+            g = eg_ref[base + lax.rem(slots[s], SPAN), lax.div(slots[s], SPAN)]
             rhs = [yk[pl.ds((h * 8 + s) * ROWS, ROWS), :] for h in range(2)]
-            r2 = dot(xt[g], jnp.concatenate(rhs, axis=1).astype(bf16))
+            r2 = dot(xt_ref[g], jnp.concatenate(rhs, axis=1).astype(bf16))
             part = [tk[pl.ds((h * 8 + s) * 16, 16), :] for h in range(2)]
             part = jnp.concatenate(part, axis=1).astype(bf16)
             rows = pl.ds(pl.multiple_of(g * 16, 16), 16)
@@ -275,6 +254,37 @@
         return carry
 
     lax.fori_loop(0, (count + 7) // 8, one_block, 0)
+
+
+def first_kernel(eg_ref, ec_ref, recv_ref, xt_ref, acc_ref, todo, tile, yk, tk):
+    def clear(i, carry):
+        acc_ref[pl.ds(pl.multiple_of(i * 64, 64), 64), :] = jnp.zeros((64, LANES), f32)
+        return carry
+
+    lax.fori_loop(0, acc_ref.shape[0] // 64, clear, 0)
+    exported_pull(0, eg_ref, ec_ref, recv_ref, xt_ref, acc_ref, todo, tile, yk, tk)
+
+
+def last_kernel(
+    eg_ref,
+    ec_ref,
+    recv_ref,
+    xt_ref,
+    old_ref,
+    pos_ref,
+    vel_ref,
+    local0_ref,
+    local1_ref,
+    out_ref,
+    acc_ref,
+    todo,
+    tile,
+    yk,
+    tk,
+):
+    exported_pull(SPAN, eg_ref, ec_ref, recv_ref, xt_ref, acc_ref, todo, tile, yk, tk)
+    groups = pos_ref.shape[1]
+    early = local0_ref.shape[1]
 
     def finish(ref, base, b, carry):
         first = pl.multiple_of(base + b * 8, 8)
@@ -282,9 +292,9 @@
         near = pl.ds(pl.multiple_of(b * 8, 8), 8)
         total = []
         for c in range(4):
-            v = acc[pl.ds(first * 16 + c, 8, stride=16), :]
-            v = v + acc[pl.ds(first * 16 + 4 + c, 8, stride=16), :]
-            total.append(v + acc[pl.ds(first * 16 + 8 + c, 8, stride=16), :])
+            v = acc_ref[pl.ds(first * 16 + c, 8, stride=16), :]
+            v = v + acc_ref[pl.ds(first * 16 + 4 + c, 8, stride=16), :]
+            total.append(v + acc_ref[pl.ds(first * 16 + 8 + c, 8, stride=16), :])
         for c in range(3):
             x = pos_ref[c, rows, :]
             pull = total[c] - (x - MID) * total[3]
@@ -296,28 +306,50 @@
     lax.fori_loop(0, (groups - early) // 8, functools.partial(finish, local1_ref, early), 0)
 
 
-def remote_pull(export_group, export_count, recv, pos, vel, near0, near1):
-    groups = pos.shape[1]
-    peers = export_count.shape[0]
-    slots = export_group.shape[0]
-    smem = pl.BlockSpec(memory_space=pltpu.SMEM)
-    vmem = pl.BlockSpec(memory_space=pltpu.VMEM)
+def exported_scratch(slots):
+    return [
+        pltpu.SMEM((slots + 8,), jnp.int32),
+        pltpu.VMEM((64, LANES), f32),
+        pltpu.VMEM((2 * 8 * ROWS, LANES), f32),
+        pltpu.VMEM((2 * 8 * 16, LANES), f32),
+    ]
+
+
+SMEM_SPEC = pl.BlockSpec(memory_space=pltpu.SMEM)
+VMEM_SPEC = pl.BlockSpec(memory_space=pltpu.VMEM)
+
+
+def first_pull(export_group, export_count, recv, xt):
+    slots, peers = export_group.shape
     return pl.pallas_call(
-        remote_kernel,
-        out_shape=jax.ShapeDtypeStruct((6, groups, LANES), f32),
-        in_specs=[smem, smem] + [vmem] * 7,
-        out_specs=vmem,
-        scratch_shapes=[
-            pltpu.SMEM((peers * slots + 8,), jnp.int32),
-            pltpu.VMEM((groups, LANES, ROWS), bf16),
-            pltpu.VMEM((64, LANES), f32),
-            pltpu.VMEM((2 * 8 * ROWS, LANES), f32),
-            pltpu.VMEM((2 * 8 * 16, LANES), f32),
-            pltpu.VMEM((groups * 16, LANES), f32),
-        ],
-        compiler_params=pltpu.CompilerParams(vmem_limit_bytes=40 << 20),
-        name="remote_pull",
-    )(export_group, export_count, recv, near0[1], near1[1], pos, vel, near0[0], near1[0])
+        first_kernel,
+        out_shape=jax.ShapeDtypeStruct((xt.shape[0] * 16, LANES), f32),
+        in_specs=[SMEM_SPEC] * 2 + [VMEM_SPEC] * 2,
+        out_specs=VMEM_SPEC,
+        scratch_shapes=exported_scratch(peers * SPAN),
+        compiler_params=pltpu.CompilerParams(vmem_limit_bytes=24 << 20),
+        cost_estimate=pl.CostEstimate(
+            flops=peers * SPAN * 65536000, bytes_accessed=4 << 20, transcendentals=0
+        ),
+        name="first_pull",
+    )(export_group, export_count, recv, xt)
+
+
+def last_pull(export_group, export_count, recv, xt, acc, pos, vel, local0, local1):
+    slots, peers = export_group.shape
+    return pl.pallas_call(
+        last_kernel,
+        out_shape=(
+            jax.ShapeDtypeStruct((6,) + pos.shape[1:], f32),
+            jax.ShapeDtypeStruct(acc.shape, f32),
+        ),
+        in_specs=[SMEM_SPEC] * 2 + [VMEM_SPEC] * 7,
+        out_specs=[VMEM_SPEC] * 2,
+        scratch_shapes=exported_scratch(peers * SPAN),
+        input_output_aliases={4: 1},
+        compiler_params=pltpu.CompilerParams(vmem_limit_bytes=24 << 20),
+        name="last_pull",
+    )(export_group, export_count, recv, xt, acc, pos, vel, local0, local1)[0]
 
 
 def shifted(value, axis, steps):
@@ -348,20 +380,21 @@
     pos = jnp.transpose(group_pos, (1, 0, 2))
     vel = jnp.transpose(group_vel, (1, 0, 2))
     mass = node_mass[None, :]
-    near0 = local_pull(pos, node_pos, mass, group_nodes, 0, early)
-    got, near0 = lax.optimization_barrier((got, near0))
-    opened = open_leaves(got, jnp.transpose(leaf_pos, (1, 0, 2)), leaf_mass)
+    (local0,) = local_pull(pos, node_pos, mass, group_nodes, 0, early, False)
+    got, local0 = lax.optimization_barrier((got, local0))
+    leaf = jnp.transpose(leaf_pos, (1, 0, 2))
+    opened = open_leaves(got, leaf, leaf_mass, 0)
     opened, mass = lax.optimization_barrier((opened, mass))
     recv = lax.all_to_all(opened, AXES, split_axis=0, concat_axis=0, tiled=True)
-    near1 = local_pull(pos, node_pos, mass, group_nodes, early, groups)
-    kicked = remote_pull(
-        jnp.transpose(export_group[0]),
-        export_count[0],
-        recv.reshape(peers * 64, LANES),
-        pos,
-        vel,
-        near0,
-        near1,
+    local1, xt = local_pull(pos, node_pos, mass, group_nodes, early, groups, True)
+    got2, recv, local1, xt = lax.optimization_barrier((got, recv, local1, xt))
+    opened2 = open_leaves(got2, leaf, leaf_mass, SPAN)
+    opened2, recv = lax.optimization_barrier((opened2, recv))
+    recv2 = lax.all_to_all(opened2, AXES, split_axis=0, concat_axis=0, tiled=True)
+    exported = jnp.transpose(export_group[0])
+    acc = first_pull(exported, export_count[0], recv.reshape(-1, LANES), xt)
+    kicked = last_pull(
+        exported, export_count[0], recv2.reshape(-1, LANES), xt, acc, pos, vel, local0, local1
     )
     me = lax.axis_index(AXES)
     before = jnp.where(me > 0, got[jnp.maximum(me - 1, 0), 16], 0)

time: 146 us -> 152 us (1.041); the launches traced: 147 us -> 150 us
  local copies, waits for them, and re-layouts: 8.57 us -> 24.2 us
  waiting for transfers between devices: 18.7 us -> 5.8 us
  starting transfers between devices: 23.6 us -> 34.4 us
  Pallas kernels: 93.1 us -> 82.7 us
    unnamed x28 -> x48, local copies, waits for them, and re-layouts: 6.45 us -> 22 us
    all_to_all x1, waiting for transfers between devices: 12.1 us -> 0.01 us  [per_device(): recv = lax.all_to_all(opened, AXES, split_axis=0, concat_axis=0, tiled=True)]
    pallas_call x4 -> x6, Pallas kernels: 93.1 us -> 82.7 us  [the longest x2 43 us: local_pull(): pl.pallas_call(functools.partial(local_kernel, begin, emit), out_shape=ou...]
    all_to_all x0 -> x1, starting transfers between devices: none -> 9.75 us  [per_device(): lax.all_to_all(opened2, AXES, split_axis=0, concat_axis=0, tiled=True)]
  transfers between devices with their start and end apart: 3 -> 4, of which waited for: 2 -> 1; matrix products, arithmetic and copies ran while one was open for 1% -> 0% of each run, Pallas kernels for 32% -> 45%
where the time goes in v3:
time: 152 us; the launch traced here: 150 us
  Pallas kernels  82.7 us (54%)
  starting transfers between devices  34.4 us (23%)
  local copies, waits for them, and re-layouts  24.2 us (16%)
  waiting for transfers between devices  5.8 us (4%)
    pallas_call x2, Pallas kernels, local_pull(): pl.pallas_call(functools.partial(local_kernel, begin, emit), out_shape=ou...  43 us
    pallas_call x1, Pallas kernels, first_pull(): pl.pallas_call(first_kernel, out_shape=jax.ShapeDtypeStruct((xt.shape[0]...  24.5 us
    unnamed x48, local copies, waits for them, and re-layouts  22 us
    all_to_all x1, starting transfers between devices, per_device(): got = lax.all_to_all(asked, AXES, split_axis=0, concat_axis=0, tiled=True)  11.5 us
    all_to_all x1, starting transfers between devices, per_device(): recv = lax.all_to_all(opened, AXES, split_axis=0, concat_axis=0, tiled=True)  9.76 us
    all_to_all x1, starting transfers between devices, per_device(): lax.all_to_all(opened2, AXES, split_axis=0, concat_axis=0, tiled=True)  9.75 us
    pallas_call x2, Pallas kernels, open_leaves(): pl.pallas_call(functools.partial(open_kernel, base), out_shape=jax.ShapeD...  7.79 us
    pallas_call x1, Pallas kernels, last_pull(): pl.pallas_call(last_kernel, out_shape=(jax.ShapeDtypeStruct((6,) + pos.sh...  7.44 us
  transfers between devices with their start and end apart: 4, of which 1 were waited for; matrix products, arithmetic and copies ran while one was open for 0% of the time, Pallas kernels for 45%

profile of v3, /device:TPU:1, one launch (start us, length us, event | category | flops | bytes accessed | tf_op | source)
XLA Modules:
  0.0 149.6 jit_solution(18055053364993373411)
XLA Ops:
  0.7 0.7 pad_bitcast_fusion
  1.4 0.7 copy.15
  2.1 11.5 %all-to-all-start = ((s32[128,1,17]{2,1,0:T(1,128)}), s32[128,1,17]{2,1,0:T(1,128)S(1)}, u32[]{:S(2)}, u32[]{:S(2)}) async-start(s32[128,1,17]{2,1,0:T(1,128)} %copy.15), calls=%async_computation | async-start | bytes 131072 | tf_op jit(solution)/shard_map/all_to_all | solution.py:379
  13.6 0.0 copy-start.10
  13.6 1.0 copy-done.10
  14.6 0.0 copy-start.18
  14.6 1.0 copy-done.18
  15.6 0.0 copy-start.20
  15.6 0.7 copy-done.20
  16.3 0.0 copy-start.22
  16.3 0.7 copy-done.22
  17.0 0.0 copy-start.4
  17.0 0.0 copy-start.9
  17.0 7.9 %local_pull.2.local0_ref = f32[3,48,128]{2,1,0:T(8,128)S(1)} custom-call(f32[3,256,128]{2,1,0:T(8,128)S(1)} %bitcast.27, f32[3,512]{1,0:T(4,128)S(1)} %copy-done.20, f32[1,512]{1,0:T(1,128)S(1)} %bitcast.35, s32[256,512]{1,0:T(8,128)S(1)} %copy-done.18), custom_call_target="tpu_custom_call" | custom-call | flops 6291456000 | bytes 4194304 | tf_op jit(solution)/shard_map/local_pull/pallas_call | solution.py:195
  25.0 0.0 copy-start.14
  25.0 0.6 copy-done.14
  25.6 0.0 all-to-all-done
  25.6 0.6 constant_dynamic-slice_fusion
  26.8 0.0 copy-done.4
  26.8 0.0 copy-done.9
  26.8 4.6 %open_leaves.2 = f32[128,32,128]{2,1,0:T(8,128)} custom-call(s32[128,17]{1,0:T(8,128)S(1)} %bitcast.25, f32[3,512,128]{2,1,0:T(8,128)S(1)} %bitcast.21, f32[512,128]{1,0:T(8,128)S(1)} %copy-done.9), custom_call_target="tpu_custom_call" | custom-call | tf_op jit(solution)/shard_map/open_leaves/pallas_call | solution.py:97
  31.3 0.0 copy-start.21
  31.3 0.0 copy-start.23
  31.3 9.8 %all-to-all-start.1 = ((f32[128,32,128]{2,1,0:T(8,128)}), f32[128,32,128]{2,1,0:T(8,128)S(1)}, u32[]{:S(2)}, u32[]{:S(2)}) async-start(f32[128,32,128]{2,1,0:T(8,128)} %open_leaves.2), calls=%async_computation.1 | async-start | bytes 4194304 | tf_op jit(solution)/shard_map/all_to_all | solution.py:388
  41.1 0.1 pad_dynamic-slice_fusion.2
  41.2 0.0 copy-done.21
  41.2 0.0 copy-done.23
  41.2 0.0 copy-start.11
  41.2 1.0 copy-done.11
  42.2 0.0 copy-start.19
  42.2 1.0 copy-done.19
  43.3 35.0 %local_pull.3 = (f32[3,208,128]{2,1,0:T(8,128)S(1)}, bf16[256,128,32]{2,1,0:T(8,128)(2,1)S(1)}) custom-call(f32[3,256,128]{2,1,0:T(8,128)S(1)} %bitcast.28, f32[3,512]{1,0:T(4,128)S(1)} %copy-done.21, f32[1,512]{1,0:T(1,128)S(1)} %bitcast.36, s32[256,512]{1,0:T(8,128)S(1)} %copy-done.19), custom_call_target="tpu_custom_call" | custom-call | flops 27262976000 | bytes 4194304 | tf_op jit(solution)/shard_map/local_pull/pallas_call | solution.py:195
  78.3 0.0 copy-start
  78.3 3.3 %copy-done = bf16[256,128,32]{2,1,0:T(8,128)(2,1)} copy-done((bf16[256,128,32]{2,1,0:T(8,128)(2,1)}, bf16[256,128,32]{2,1,0:T(8,128)(2,1)S(1)}, u32[]{:S(2)}) %copy-start) | copy-done | bytes 2097176
  81.6 0.0 all-to-all-done.1
  81.6 0.0 copy-start.7
  81.6 3.2 %open_leaves.3 = f32[128,32,128]{2,1,0:T(8,128)S(1)} custom-call(s32[128,17]{1,0:T(8,128)S(1)} %bitcast.26, f32[3,512,128]{2,1,0:T(8,128)S(1)} %bitcast.22, f32[512,128]{1,0:T(8,128)S(1)} %copy-done.9), custom_call_target="tpu_custom_call" | custom-call | tf_op jit(solution)/shard_map/open_leaves/pallas_call | solution.py:97
  84.8 0.0 copy-start.3
  84.8 1.4 copy-done.3
  86.2 0.0 copy-start.16
  86.2 0.0 copy-start.17
  86.2 0.0 copy-done.7
  86.2 9.8 %all-to-all-start.2 = ((f32[128,32,128]{2,1,0:T(8,128)}), f32[128,32,128]{2,1,0:T(8,128)S(1)}, u32[]{:S(2)}, u32[]{:S(2)}) async-start(f32[128,32,128]{2,1,0:T(8,128)} %copy-done.3), calls=%async_computation.2 | async-start | bytes 4194304 | tf_op jit(solution)/shard_map/all_to_all | solution.py:393
  96.0 0.0 copy-done.16
  96.0 0.0 copy-done.17
  96.0 0.0 copy-start.1
  96.0 3.4 %copy-done.1 = bf16[256,128,32]{2,1,0:T(8,128)(2,1)S(1)} copy-done((bf16[256,128,32]{2,1,0:T(8,128)(2,1)S(1)}, bf16[256,128,32]{2,1,0:T(8,128)(2,1)}, u32[]{:S(2)}) %copy-start.1) | copy-done | bytes 2097176
  99.4 0.0 copy-start.8
  99.4 1.6 %copy-done.8 = f32[128,32,128]{2,1,0:T(8,128)S(1)} copy-done((f32[128,32,128]{2,1,0:T(8,128)S(1)}, f32[128,32,128]{2,1,0:T(8,128)}, u32[]{:S(2)}) %copy-start.8) | copy-done | bytes 2097176
  101.0 0.0 copy-start.12
  101.0 24.5 %first_pull.1.old_ref = f32[4096,128]{1,0:T(8,128)S(1)} custom-call(s32[8,128]{1,0:T(8,128)S(1)} %bitcast.31, s32[128]{0:T(128)S(1)} %bitcast.33, f32[4096,128]{1,0:T(8,128)S(1)} %bitcast.23, bf16[256,128,32]{2,1,0:T(8,128)(2,1)S(1)} %copy-done.1), custom_call_target="tpu_custom_call" | custom-call | flops 33554432000 | bytes 4194304 | tf_op jit(solution)/shard_map/first_pull/pallas_call | solution.py:324
  125.4 1.4 copy-done.5
  126.8 0.0 all-to-all-done.2
  126.8 0.0 copy-done.12
  126.8 0.0 copy-done.13
  126.8 0.0 copy-done.15
  126.8 0.0 copy-start.2
  126.8 3.4 %copy-done.2 = bf16[256,128,32]{2,1,0:T(8,128)(2,1)S(1)} copy-done((bf16[256,128,32]{2,1,0:T(8,128)(2,1)S(1)}, bf16[256,128,32]{2,1,0:T(8,128)(2,1)}, u32[]{:S(2)}) %copy-start.2) | copy-done | bytes 2097176
  130.2 1.6 %copy-done.6 = f32[4096,128]{1,0:T(8,128)S(1)} copy-done((f32[4096,128]{1,0:T(8,128)S(1)}, f32[4096,128]{1,0:T(8,128)}, u32[]{:S(2)}) %copy-start.6) | copy-done | bytes 2097176
  131.8 7.4 %last_pull.1 = (f32[6,256,128]{2,1,0:T(8,128)S(1)}, f32[4096,128]{1,0:T(8,128)S(1)}) custom-call(s32[8,128]{1,0:T(8,128)S(1)} %bitcast.32, s32[128]{0:T(128)S(1)} %bitcast.34, f32[4096,128]{1,0:T(8,128)S(1)} %bitcast.20, bf16[256,128,32]{2,1,0:T(8,128)(2,1)S(1)} %copy-done.2, f32[4096,128]{1,0:T(8,128)S(1)} %copy-done.6, ...), custom_call_target="tpu_custom_call", output_to_operand_aliasing={{1}: (4, {})} | custom-call | tf_op jit(solution)/shard_map/last_pull/pallas_call | solution.py:340
  139.3 3.4 %collective-permute-start = (f32[6,16,128]{2,1,0:T(8,128)S(1)}, f32[6,16,128]{2,1,0:T(8,128)S(1)}, u32[]{:S(2)}, u32[]{:S(2)}) collective-permute-start(f32[6,16,128]{2,1,0:T(8,128)S(1)} %slice.3), channel_id=1, source_target_pairs={{0,1},{1,2},{2,3},{3,4},{4,5},{5,6},{6,7},{7,8},{8,9},{9,10},{10,1... | collective-permute-start | bytes 147464 | tf_op jit(solution)/shard_map/ppermute | solution.py:357
  142.7 0.1 broadcast_multiply_fusion
  142.8 5.8 %collective-permute-done = f32[6,16,128]{2,1,0:T(8,128)S(1)} collective-permute-done((f32[6,16,128]{2,1,0:T(8,128)S(1)}, f32[6,16,128]{2,1,0:T(8,128)S(1)}, u32[]{:S(2)}, u32[]{:S(2)}) %collective-permute-start) | collective-permute-done | bytes 49184 | tf_op jit(solution)/shard_map/ppermute | solution.py:357
  148.6 1.0 fusion.2
  (7 shorter events, 0.0 us)
Async XLA Ops:
  2.1 23.5 %all-to-all-start = ((s32[128,1,17]{2,1,0:T(1,128)}), s32[128,1,17]{2,1,0:T(1,128)S(1)}, u32[]{:S(2)}, u32[]{:S(2)}) async-start(s32[128,1,17]{2,1,0:T(1,128)} %copy.15), calls=%async_computation | async-start | bytes 131072 | tf_op jit(solution)/shard_map/all_to_all | solution.py:379
  13.6 1.0 copy-start.10
  14.6 1.0 copy-start.18
  15.6 0.7 copy-start.20
  16.3 0.7 copy-start.22
  17.0 9.7 %copy-start.4 = (f32[512,3,128]{2,0,1:T(8,128)S(1)}, f32[512,3,128]{2,0,1:T(8,128)}, u32[]{:S(2)}) copy-start(f32[512,3,128]{2,0,1:T(8,128)} %param.13) | copy-start | bytes 2359300
  17.0 9.7 %copy-start.9 = (f32[512,128]{1,0:T(8,128)S(1)}, f32[512,128]{1,0:T(8,128)}, u32[]{:S(2)}) copy-start(f32[512,128]{1,0:T(8,128)} %mass_ref.3) | copy-start | bytes 786436
  25.0 0.6 copy-start.14
  31.3 9.9 %copy-start.21 = (f32[3,512]{1,0:T(4,128)S(1)}, f32[3,512]{1,0:T(4,128)}, u32[]{:S(2)}) copy-start(f32[3,512]{1,0:T(4,128)} %node_ref.3) | copy-start | bytes 18436
  31.3 9.9 %copy-start.23 = (f32[512]{0:T(512)S(1)}, f32[512]{0:T(512)}, u32[]{:S(2)}) copy-start(f32[512]{0:T(512)} %param.16) | copy-start | bytes 6148
  31.3 50.2 %all-to-all-start.1 = ((f32[128,32,128]{2,1,0:T(8,128)}), f32[128,32,128]{2,1,0:T(8,128)S(1)}, u32[]{:S(2)}, u32[]{:S(2)}) async-start(f32[128,32,128]{2,1,0:T(8,128)} %open_leaves.2), calls=%async_computation.1 | async-start | bytes 4194304 | tf_op jit(solution)/shard_map/all_to_all | solution.py:388
  41.2 1.0 copy-start.11
  42.2 1.0 copy-start.19
  78.3 3.3 %copy-start = (bf16[256,128,32]{2,1,0:T(8,128)(2,1)}, bf16[256,128,32]{2,1,0:T(8,128)(2,1)S(1)}, u32[]{:S(2)}) copy-start(bf16[256,128,32]{2,1,0:T(8,128)(2,1)S(1)} %get-tuple-element.26.xt_ref) | copy-start | bytes 6291460
  81.6 4.6 %copy-start.7 = (f32[128,32,128]{2,1,0:T(8,128)}, f32[128,32,128]{2,1,0:T(8,128)S(1)}, u32[]{:S(2)}) copy-start(f32[128,32,128]{2,1,0:T(8,128)S(1)} %all-to-all-done.1) | copy-start | bytes 6291460
  84.8 1.4 copy-start.3
  86.2 9.8 %copy-start.16 = (s32[1,128,8]{1,2,0:T(8,128)S(1)}, s32[1,128,8]{1,2,0:T(8,128)}, u32[]{:S(2)}) copy-start(s32[1,128,8]{1,2,0:T(8,128)} %param.18) | copy-start | bytes 12292
  86.2 9.8 %copy-start.17 = (s32[1,128]{1,0:T(1,128)S(1)}, s32[1,128]{1,0:T(1,128)}, u32[]{:S(2)}) copy-start(s32[1,128]{1,0:T(1,128)} %param.20) | copy-start | bytes 1540
  86.2 40.6 %all-to-all-start.2 = ((f32[128,32,128]{2,1,0:T(8,128)}), f32[128,32,128]{2,1,0:T(8,128)S(1)}, u32[]{:S(2)}, u32[]{:S(2)}) async-start(f32[128,32,128]{2,1,0:T(8,128)} %copy-done.3), calls=%async_computation.2 | async-start | bytes 4194304 | tf_op jit(solution)/shard_map/all_to_all | solution.py:393
  96.0 3.4 %copy-start.1 = (bf16[256,128,32]{2,1,0:T(8,128)(2,1)S(1)}, bf16[256,128,32]{2,1,0:T(8,128)(2,1)}, u32[]{:S(2)}) copy-start(bf16[256,128,32]{2,1,0:T(8,128)(2,1)} %copy-done) | copy-start | bytes 6291460
  99.4 1.6 %copy-start.8 = (f32[128,32,128]{2,1,0:T(8,128)S(1)}, f32[128,32,128]{2,1,0:T(8,128)}, u32[]{:S(2)}) copy-start(f32[128,32,128]{2,1,0:T(8,128)} %copy-done.7) | copy-start | bytes 6291460
  101.0 25.8 %copy-start.12 = (f32[256,3,128]{2,0,1:T(8,128)S(1)}, f32[256,3,128]{2,0,1:T(8,128)}, u32[]{:S(2)}) copy-start(f32[256,3,128]{2,0,1:T(8,128)} %param.11) | copy-start | bytes 1179652
  101.0 25.8 %copy-start.13 = (f32[256,3,128]{2,0,1:T(8,128)S(1)}, f32[256,3,128]{2,0,1:T(8,128)}, u32[]{:S(2)}) copy-start(f32[256,3,128]{2,0,1:T(8,128)} %param.12) | copy-start | bytes 1179652
  101.0 25.9 %copy-start.15 = (f32[3,48,128]{2,1,0:T(8,128)S(1)}, f32[3,48,128]{2,1,0:T(8,128)}, u32[]{:S(2)}) copy-start(f32[3,48,128]{2,1,0:T(8,128)} %copy-done.14) | copy-start | bytes 221188
  125.4 1.4 copy-start.5
  126.8 3.4 %copy-start.2 = (bf16[256,128,32]{2,1,0:T(8,128)(2,1)S(1)}, bf16[256,128,32]{2,1,0:T(8,128)(2,1)}, u32[]{:S(2)}) copy-start(bf16[256,128,32]{2,1,0:T(8,128)(2,1)} %copy-done) | copy-start | bytes 6291460
  130.2 1.6 %copy-start.6 = (f32[4096,128]{1,0:T(8,128)S(1)}, f32[4096,128]{1,0:T(8,128)}, u32[]{:S(2)}) copy-start(f32[4096,128]{1,0:T(8,128)} %copy-done.5) | copy-start | bytes 6291460
  139.3 9.3 %collective-permute-start = (f32[6,16,128]{2,1,0:T(8,128)S(1)}, f32[6,16,128]{2,1,0:T(8,128)S(1)}, u32[]{:S(2)}, u32[]{:S(2)}) collective-permute-start(f32[6,16,128]{2,1,0:T(8,128)S(1)} %slice.3), channel_id=1, source_target_pairs={{0,1},{1,2},{2,3},{3,4},{4,5},{5,6},{6,7},{7,8},{8,9},{9,10},{10,1... | collective-permute-start | bytes 147464 | tf_op jit(solution)/shard_map/ppermute | solution.py:357

commit v4 on v1

v4 whole, which is shorter than its diff:
```python
import functools

import jax
import jax.numpy as jnp
from jax import lax
from jax.experimental import pallas as pl
from jax.experimental.pallas import tpu as pltpu
from jax.sharding import PartitionSpec as P

AXES = ("dom", "bulk")
MOVE_MAX = 16
SOFT_SQ = 0.001
KICK = 0.5
MID = 0.5
LANES = 128
ROWS = 32
SLOTS = 8
BATCH = 32

SMEM_SPEC = pl.BlockSpec(memory_space=pltpu.SMEM)
VMEM_SPEC = pl.BlockSpec(memory_space=pltpu.VMEM)

f32 = jnp.float32
bf16 = jnp.bfloat16


def dot(a, b):
    return lax.dot_general(a, b, (((1,), (0,)), ((), ())), preferred_element_type=f32)


def dot_t(a, b):
    return lax.dot_general(a, b, (((1,), (1,)), ((), ())), preferred_element_type=f32)


def split3(v):
    a = v.astype(bf16).astype(f32)
    r = v - a
    b = r.astype(bf16).astype(f32)
    return a, b, r - b


def split2(w):
    hi = w.astype(bf16)
    return hi, (w - hi.astype(f32)).astype(bf16)


def target_rows(x):
    rows = []
    for c in range(3):
        a, b, d = split3(x[c])
        rows += [a, a, b, b, a, d]
    rows += list(split3(x[0] * x[0] + x[1] * x[1] + x[2] * x[2]))
    one = jnp.ones_like(x[0])
    return rows + [one, one, one]


def source_rows(y, scale):
    rows = []
    for c in range(3):
        a, b, d = split3(y[c] * (-2.0 * scale))
        rows += [a, b, a, b, d, a]
    one = jnp.ones_like(y[0]) * scale
    rows += [one, one, one]
    rows += list(split3((y[0] * y[0] + y[1] * y[1] + y[2] * y[2] + SOFT_SQ) * scale))
    return rows


def inv_cube(r2):
    rs = lax.rsqrt(r2)
    return rs * rs * rs


def open_kernel(ids_ref, pos_hbm, mass_hbm, out_hbm, pos, mass, table, out, in_sem, out_sem):
    leaf_count = pos.shape[1]
    peers = out.shape[0]
    loads = [
        pltpu.make_async_copy(pos_hbm, pos, in_sem.at[0]),
        pltpu.make_async_copy(mass_hbm, mass, in_sem.at[1]),
    ]
    for load in loads:
        load.start()
    for load in loads:
        load.wait()

    def build(b, carry):
        first = pl.multiple_of(b * 8, 8)
        for c in range(4):
            v = pos[c, pl.ds(first, 8), :] if c < 3 else mass[pl.ds(first, 8), :]
            table[pl.ds(first * 8 + c, 8, stride=8), :] = v
            table[pl.ds(first * 8 + 4 + c, 8, stride=8), :] = v
        return carry

    lax.fori_loop(0, leaf_count // 8, build, 0, unroll=4)
    upper = lax.broadcasted_iota(jnp.int32, (8, LANES), 0) < 4

    def one_peer(p, carry):
        for s in range(SLOTS):
            i0 = pl.multiple_of(ids_ref[p, 2 * s] * 8, 8)
            i1 = pl.multiple_of(ids_ref[p, 2 * s + 1] * 8, 8)
            out[p, pl.ds(s * 8, 8), :] = jnp.where(
                upper, table[pl.ds(i0, 8), :], table[pl.ds(i1, 8), :]
            )
        return carry

    stores = []
    step = peers // 4
    for q in range(4):
        lax.fori_loop(q * step, (q + 1) * step, one_peer, 0, unroll=2)
        rows = pl.ds(q * step, step)
        stores.append(pltpu.make_async_copy(out.at[rows], out_hbm.at[rows], out_sem.at[q]))
        stores[-1].start()
    for store in stores:
        store.wait()


def open_leaves(ids, leaf_pos, leaf_mass):
    peers = ids.shape[0]
    shape = (peers, SLOTS * 8, LANES)
    return pl.pallas_call(
        open_kernel,
        out_shape=jax.ShapeDtypeStruct(shape, f32),
        in_specs=[
            pl.BlockSpec(memory_space=pltpu.SMEM),
            pl.BlockSpec(memory_space=pltpu.HBM),
            pl.BlockSpec(memory_space=pltpu.HBM),
        ],
        out_specs=pl.BlockSpec(memory_space=pltpu.HBM),
        scratch_shapes=[
            pltpu.VMEM(leaf_pos.shape, f32),
            pltpu.VMEM(leaf_mass.shape, f32),
            pltpu.VMEM((leaf_pos.shape[1] * 8, LANES), f32),
            pltpu.VMEM(shape, f32),
            pltpu.SemaphoreType.DMA((2,)),
            pltpu.SemaphoreType.DMA((4,)),
        ],
        compiler_params=pltpu.CompilerParams(vmem_limit_bytes=24 << 20),
        name="open_leaves",
    )(ids, leaf_pos, leaf_mass)


def local_kernel(
    eg_ref, ec_ref, pos_ref, node_ref, mass_ref, list_ref, acc_ref, todo_ref, ynt, xk, raw
):
    peers = ec_ref.shape[0]

    def enlist(p, count):
        for s in range(SLOTS):
            todo_ref[count + s] = (p * SLOTS + s) * 256 + eg_ref[s, p]
        return count + ec_ref[p]

    count = lax.fori_loop(0, peers, enlist, 0)
    for s in range(BATCH):
        todo_ref[count + s] = 0
    todo_ref[todo_ref.shape[0] - 1] = count

    nodes = node_ref.shape[1]
    y = [node_ref[c : c + 1, :] - MID for c in range(3)]
    mass = mass_ref[...]
    yk = jnp.concatenate(source_rows(y, 1.0) + [jnp.zeros((8, nodes), f32)], axis=0)
    ynt[...] = jnp.transpose(yk).astype(bf16)
    tab = jnp.concatenate([mass * y[0], mass * y[1], mass * y[2], mass], axis=0)
    tab = jnp.concatenate([tab, tab], axis=0)
    xk[...] = jnp.zeros_like(xk)
    row128 = lax.broadcasted_iota(jnp.int32, (LANES, nodes), 0)
    row16 = lax.broadcasted_iota(jnp.int32, (16, nodes), 0)
    upper = lax.broadcasted_iota(jnp.int32, (8, LANES), 0) < 4
    raw[...] = jnp.zeros_like(raw)

    def one_block(b, carry):
        first = pl.multiple_of(b * 8, 8)
        x = [pos_ref[c, pl.ds(first, 8), :] - MID for c in range(3)]
        for r, v in enumerate(target_rows(x)):
            xk[pl.ds(r, 8, stride=ROWS), :] = v
        lists = list_ref[pl.ds(first, 8), :]
        counts = []
        for g in range(8):
            wanted = lists[g : g + 1, :]
            low = jnp.where(row128 == (wanted & 127), 1.0, 0.0).astype(bf16)
            high = jnp.where(row16 == (wanted >> 7), 1.0, 0.0).astype(bf16)
            counts.append(dot_t(high, low))
        for p in range(4):
            parts = []
            for h in range(nodes // LANES):
                both = jnp.where(
                    upper, counts[2 * p][h : h + 1, :], counts[2 * p + 1][h : h + 1, :]
                )
                parts.append(tab[:, h * LANES : (h + 1) * LANES] * both)
            a, d, e = split3(jnp.concatenate(parts, axis=1))
            weights = jnp.concatenate([a, d, e, jnp.zeros_like(a)], axis=0).astype(bf16)
            xa = xk[pl.ds(2 * p * ROWS, ROWS), :]
            xb = xk[pl.ds((2 * p + 1) * ROWS, ROWS), :]
            rhs = jnp.concatenate([xa, xb], axis=1).astype(bf16)
            total = jnp.zeros((32, 2 * LANES), f32)
            for h in range(nodes // 256):
                his, los = [], []
                for k in range(256 // 128):
                    rows = pl.ds(h * 256 + k * 128, 128)
                    a, d = split2(inv_cube(dot(ynt[rows, :], rhs)))
                    his.append(a)
                    los.append(d)
                part = weights[:, h * 256 : (h + 1) * 256]
                total = total + dot(part, jnp.concatenate(his, axis=0)) + dot(part, jnp.concatenate(los, axis=0))
            total = total[0:8] + total[8:16] + total[16:24]
            raw[pl.ds(2 * p * 8, 4), :] = total[0:4, :LANES]
            raw[pl.ds((2 * p + 1) * 8, 4), :] = total[4:8, LANES:]
        weight = raw[pl.ds(3, 8, stride=8), :]
        for c in range(3):
            acc_ref[c, pl.ds(first, 8), :] = raw[pl.ds(c, 8, stride=8), :] - x[c] * weight
        return carry

    lax.fori_loop(0, acc_ref.shape[1] // 8, one_block, 0)


def local_pull(export_group, export_count, pos, node_pos, node_mass, lists):
    groups = pos.shape[1]
    nodes = node_pos.shape[1]
    entries = export_group.shape[0] * export_group.shape[1] + 2 * BATCH
    pairs = groups * LANES * nodes
    return pl.pallas_call(
        local_kernel,
        out_shape=(
            jax.ShapeDtypeStruct((3, groups, LANES), f32),
            jax.ShapeDtypeStruct((entries,), jnp.int32),
        ),
        in_specs=[SMEM_SPEC] * 2 + [VMEM_SPEC] * 4,
        out_specs=[VMEM_SPEC, SMEM_SPEC],
        scratch_shapes=[
            pltpu.VMEM((nodes, ROWS), bf16),
            pltpu.VMEM((8 * ROWS, LANES), f32),
            pltpu.VMEM((64, LANES), f32),
        ],
        compiler_params=pltpu.CompilerParams(vmem_limit_bytes=16 << 20),
        cost_estimate=pl.CostEstimate(
            flops=pairs * 2000, bytes_accessed=4 << 20, transcendentals=pairs
        ),
        name="local_pull",
    )(export_group, export_count, pos, node_pos, node_mass, lists)


def remote_kernel(
    todo, recv_ref, pos_ref, vel_ref, local_ref, out_ref, tile, place, xk, yk, tk, acc
):
    groups = pos_ref.shape[1]
    count = todo[todo.shape[0] - 1]
    xk[...] = jnp.zeros_like(xk)
    yk[...] = jnp.zeros_like(yk)
    tk[...] = jnp.zeros_like(tk)

    def clear(i, carry):
        acc[pl.ds(pl.multiple_of(i * 64, 64), 64), :] = jnp.zeros((64, LANES), f32)
        return carry

    lax.fori_loop(0, groups * 8 // 64, clear, 0)
    lane = lax.broadcasted_iota(jnp.int32, (8, LANES), 1).astype(f32)
    scale = 1.0 + lane * (1.0 / LANES)
    lift = scale * jnp.sqrt(scale)

    def one_block(b, carry):
        owners = []
        for s in range(BATCH):
            entry = todo[b * BATCH + s]
            g = entry & 255
            owners.append(g)
            tile[pl.ds(s * 8, 8), :] = recv_ref[pl.ds(pl.multiple_of((entry >> 8) * 8, 8), 8), :]
            for c in range(3):
                place[c, pl.ds(s, 1), :] = pos_ref[c, pl.ds(g, 1), :]
        for q in range(BATCH // 8):
            first = q * 8
            rank = lax.broadcasted_iota(jnp.int32, (8, LANES), 0) + (b * BATCH + first)
            x = [place[c, pl.ds(first, 8), :] - MID for c in range(3)]
            for r, v in enumerate(target_rows(x)):
                xk[pl.ds(first * ROWS + r, 8, stride=ROWS), :] = v
            for h in range(2):
                y = [tile[pl.ds(first * 8 + 4 * h + c, 8, stride=8), :] - MID for c in range(3)]
                m = tile[pl.ds(first * 8 + 4 * h + 3, 8, stride=8), :]
                m = jnp.where(rank < count, m * lift, 0.0)
                base = h * BATCH + first
                for r, v in enumerate(source_rows(y, scale)):
                    yk[pl.ds(base * ROWS + r, 8, stride=ROWS), :] = v
                for c, v in enumerate([m * y[0], m * y[1], m * y[2], m]):
                    for j, part in enumerate(split3(v)):
                        tk[pl.ds(base * 16 + 4 * j + c, 8, stride=16), :] = part
        for s in range(BATCH):
            xt = jnp.transpose(xk[pl.ds(s * ROWS, ROWS), :]).astype(bf16)
            rhs = [yk[pl.ds((h * BATCH + s) * ROWS, ROWS), :] for h in range(2)]
            r2 = dot(xt, jnp.concatenate(rhs, axis=1).astype(bf16))
            part = [tk[pl.ds((h * BATCH + s) * 16, 16), :] for h in range(2)]
            part = jnp.concatenate(part, axis=1).astype(bf16)
            total = dot_t(part, inv_cube(r2).astype(bf16))
            rows = pl.ds(pl.multiple_of(owners[s] * 8, 8), 8)
            acc[rows, :] += total[0:8] + total[8:16]
        return carry

    lax.fori_loop(0, (count + BATCH - 1) // BATCH, one_block, 0)

    def finish(b, carry):
        first = pl.multiple_of(b * 8, 8)
        rows = pl.ds(first, 8)
        total = []
        for c in range(4):
            v = acc[pl.ds(first * 8 + c, 8, stride=8), :]
            total.append(v + acc[pl.ds(first * 8 + 4 + c, 8, stride=8), :])
        for c in range(3):
            x = pos_ref[c, rows, :]
            pull = local_ref[c, rows, :] + total[c] - (x - MID) * total[3]
            out_ref[c, rows, :] = x
            out_ref[3 + c, rows, :] = vel_ref[c, rows, :] + KICK * pull
        return carry

    lax.fori_loop(0, groups // 8, finish, 0, unroll=2)


def remote_pull(todo, recv, pos, vel, local_acc):
    groups = pos.shape[1]
    return pl.pallas_call(
        remote_kernel,
        out_shape=jax.ShapeDtypeStruct((6, groups, LANES), f32),
        in_specs=[SMEM_SPEC] + [VMEM_SPEC] * 4,
        out_specs=VMEM_SPEC,
        scratch_shapes=[
            pltpu.VMEM((BATCH * 8, LANES), f32),
            pltpu.VMEM((3, BATCH, LANES), f32),
            pltpu.VMEM((BATCH * ROWS, LANES), f32),
            pltpu.VMEM((2 * BATCH * ROWS, LANES), f32),
            pltpu.VMEM((2 * BATCH * 16, LANES), f32),
            pltpu.VMEM((groups * 8, LANES), f32),
        ],
        compiler_params=pltpu.CompilerParams(vmem_limit_bytes=24 << 20),
        name="remote_pull",
    )(todo, recv, pos, vel, local_acc)


def shifted(value, axis, steps):
    count = lax.axis_size(axis)
    return lax.ppermute(value, axis, [(source, source + steps) for source in range(count - steps)])


def per_device(
    group_pos,
    group_vel,
    leaf_pos,
    leaf_mass,
    node_pos,
    node_mass,
    group_nodes,
    export_group,
    export_leaf,
    export_count,
    move_count,
):
    peers = export_group.shape[1]
    groups = group_pos.shape[0]
    asked = jnp.concatenate(
        [export_leaf[0].reshape(peers, 16), jnp.broadcast_to(move_count[:, None], (peers, 1))], axis=1
    )
    got = lax.all_to_all(asked, AXES, split_axis=0, concat_axis=0, tiled=True)
    pos = jnp.transpose(group_pos, (1, 0, 2))
    vel = jnp.transpose(group_vel, (1, 0, 2))
    mass = node_mass[None, :]
    exported = jnp.transpose(export_group[0])
    opened = open_leaves(got, jnp.transpose(leaf_pos, (1, 0, 2)), leaf_mass)
    opened, mass = lax.optimization_barrier((opened, mass))
    recv = lax.all_to_all(opened, AXES, split_axis=0, concat_axis=0, tiled=True)
    local_acc, todo = local_pull(exported, export_count[0], pos, node_pos, mass, group_nodes)
    kicked = remote_pull(todo, recv.reshape(-1, LANES), pos, vel, local_acc)
    me = lax.axis_index(AXES)
    before = jnp.where(me > 0, got[jnp.maximum(me - 1, 0), 16], 0)
    leaving = move_count[0]
    arrived = shifted(kicked[:, groups - MOVE_MAX :], AXES, 1)
    keep = (jnp.arange(groups) < groups - leaving).astype(f32)
    stacked = jnp.concatenate(
        [arrived, kicked * keep[None, :, None], jnp.zeros((6, MOVE_MAX, LANES), f32)], axis=1
    )
    moved = lax.dynamic_slice_in_dim(stacked, MOVE_MAX - before, groups + MOVE_MAX, 1)
    return jnp.transpose(moved, (1, 0, 2))


def solution(mesh):
    in_specs = (
        P(AXES, None, None),
        P(AXES, None, None),
        P(AXES, None, None),
        P(AXES, None),
        P(None, AXES),
        P(AXES),
        P(AXES, None),
        P(AXES, None, None),
        P(AXES, None, None, None),
        P(AXES, None),
        P(AXES),
    )
    return jax.shard_map(
        per_device,
        mesh=mesh,
        in_specs=in_specs,
        out_specs=P(AXES, None, None),
        check_vma=False,
    )
```

time: 183 us -> 125 us (0.68)
  the two profiles are of different devices: /device:TPU:14 before, /device:TPU:1 now
where the time goes in v4:
time: 125 us; the launch traced here: 124 us
  Pallas kernels  74.1 us (59%)
  blocking collectives  20.8 us (17%)
  waiting for transfers between devices  12.8 us (10%)
  starting transfers between devices  7.86 us (6%)
  local copies, waits for them, and re-layouts  5.57 us (4%)
  between operations  1.46 us (1%)
    pallas_call x1, Pallas kernels, local_pull(): pl.pallas_call(local_kernel, out_shape=(jax.ShapeDtypeStruct((3, groups,...  44.8 us
    pallas_call x1, Pallas kernels, remote_pull(): pl.pallas_call(remote_kernel, out_shape=jax.ShapeDtypeStruct((6, groups,...  24.5 us
    all_to_all x1, blocking collectives, per_device(): got = lax.all_to_all(asked, AXES, split_axis=0, concat_axis=0, tiled=True)  20.8 us
    ppermute x1, waiting for transfers between devices, shifted(): lax.ppermute(value, axis, [(source, source + steps) for source in range(c...  6.78 us
    all_to_all x1, waiting for transfers between devices, per_device(): recv = lax.all_to_all(opened, AXES, split_axis=0, concat_axis=0, tiled=True)  6.06 us
    all_to_all x1, starting transfers between devices, per_device(): recv = lax.all_to_all(opened, AXES, split_axis=0, concat_axis=0, tiled=True)  5.72 us
    pallas_call x1, Pallas kernels, open_leaves(): pl.pallas_call(open_kernel, out_shape=jax.ShapeDtypeStruct(shape, f32), i...  4.88 us
    unnamed x20, local copies, waits for them, and re-layouts  4.08 us
  transfers between devices with their start and end apart: 2, of which 2 were waited for; matrix products, arithmetic and copies ran while one was open for 1% of the time, Pallas kernels for 36%

profile of v4, /device:TPU:1, one launch (start us, length us, event | category | flops | bytes accessed | tf_op | source)
XLA Modules:
  0.0 123.8 jit_solution(15804583522111854032)
XLA Ops:
  0.7 0.7 pad_bitcast_fusion
  1.4 0.1 copy.14
  1.5 20.8 %all_to_all.16 = s32[128,1,17]{2,1,0:T(1,128)S(1)} all-to-all(s32[128,1,17]{2,1,0:T(1,128)S(1)} %copy.14), channel_id=1, replica_groups=mesh['dom'=8,'bulk'=16] {'dom','bulk'}, dimensions={0} | all-to-all | bytes 17408 | tf_op jit(solution)/shard_map/all_to_all | solution.py:356
  22.3 0.0 copy-start.1
  22.3 1.1 copy-done.1
  23.4 0.0 copy-start.4
  23.4 0.9 copy-done.4
  24.4 4.9 %open_leaves.1 = f32[128,64,128]{2,1,0:T(8,128)S(1)} custom-call(s32[128,17]{1,0:T(8,128)S(1)} %bitcast.23, f32[3,512,128]{2,1,0:T(8,128)S(1)} %bitcast.19, f32[512,128]{1,0:T(8,128)S(1)} %copy-done.4), custom_call_target="tpu_custom_call" | custom-call | tf_op jit(solution)/shard_map/open_leaves/pallas_call | solution.py:119
  29.3 0.0 copy-start
  29.3 2.0 %copy-done = f32[128,64,128]{2,1,0:T(8,128)} copy-done((f32[128,64,128]{2,1,0:T(8,128)}, f32[128,64,128]{2,1,0:T(8,128)S(1)}, u32[]{:S(2)}) %copy-start) | copy-done | bytes 4194328
  31.2 0.0 copy-start.2
  31.2 0.0 copy-start.5
  31.2 0.0 copy-start.6
  31.3 0.0 copy-start.7
  31.3 0.0 copy-start.8
  31.3 0.0 copy-start.9
  31.3 5.7 %all-to-all-start.1 = ((f32[128,64,128]{2,1,0:T(8,128)}), f32[128,64,128]{2,1,0:T(8,128)}, u32[]{:S(2)}, u32[]{:S(2)}) async-start(f32[128,64,128]{2,1,0:T(8,128)} %copy-done), calls=%async_computation.1 | async-start | bytes 8388608 | tf_op jit(solution)/shard_map/all_to_all | solution.py:363
  37.0 0.6 constant_dynamic-slice_fusion
  38.3 0.1 pad_dynamic-slice_fusion.2
  38.4 0.0 copy-done.2
  38.4 0.0 copy-done.5
  38.4 0.0 copy-done.6
  38.4 0.0 copy-done.7
  38.4 0.0 copy-done.8
  38.4 0.0 copy-done.9
  38.4 0.0 copy-start.3
  38.4 44.8 %local_pull.1 = (f32[3,256,128]{2,1,0:T(8,128)S(1)}, s32[1088]{0:T(1024)S(1)}) custom-call(s32[8,128]{1,0:T(8,128)S(1)} %bitcast.24, s32[128]{0:T(128)S(1)} %bitcast.26, f32[3,256,128]{2,1,0:T(8,128)S(1)} %bitcast.20, f32[3,512]{1,0:T(4,128)S(1)} %copy-done.6, f32[1,512]{1,0:T(1,128)S(1)} %bitcast.25, s32[256,512]{1,0:T(8,128)S(1)} %copy-done.5), custom_call_target="tpu_custom_call" | custom-call | flops 33554432000 | bytes 4194304 | tf_op jit(solution)/shard_map/local_pull/pallas_call | solution.py:219
  83.2 6.1 %all-to-all-done.1 = f32[128,64,128]{2,1,0:T(8,128)} async-done(((f32[128,64,128]{2,1,0:T(8,128)}), f32[128,64,128]{2,1,0:T(8,128)}, u32[]{:S(2)}, u32[]{:S(2)}) %all-to-all-start.1) | async-done | bytes 4194336 | tf_op jit(solution)/shard_map/all_to_all | solution.py:363
  89.3 0.0 copy-done.3
  89.3 24.5 %remote_pull.1 = f32[6,256,128]{2,1,0:T(8,128)S(1)} custom-call(s32[1088]{0:T(1024)S(1)} %get-tuple-element.10.todo, f32[8192,128]{1,0:T(8,128)} %bitcast.10.recv_ref, f32[3,256,128]{2,1,0:T(8,128)S(1)} %bitcast.21, f32[3,256,128]{2,1,0:T(8,128)S(1)} %bitcast.22, f32[3,256,128]{2,1,0:T(8,128)S(1)} %get-tuple-element.12.local_ref), custom_call_target="tpu_custom_call" | custom-call | tf_op jit(solution)/shard_map/remote_pull/pallas_call | solution.py:315
  113.8 2.1 %collective-permute-start = (f32[6,16,128]{2,1,0:T(8,128)S(1)}, f32[6,16,128]{2,1,0:T(8,128)S(1)}, u32[]{:S(2)}, u32[]{:S(2)}) collective-permute-start(f32[6,16,128]{2,1,0:T(8,128)S(1)} %slice.4), channel_id=1, source_target_pairs={{0,1},{1,2},{2,3},{3,4},{4,5},{5,6},{6,7},{7,8},{8,9},{9,10},{10,1... | collective-permute-start | bytes 147464 | tf_op jit(solution)/shard_map/ppermute | solution.py:335
  115.9 0.1 broadcast_multiply_fusion
  116.0 6.8 %collective-permute-done = f32[6,16,128]{2,1,0:T(8,128)S(1)} collective-permute-done((f32[6,16,128]{2,1,0:T(8,128)S(1)}, f32[6,16,128]{2,1,0:T(8,128)S(1)}, u32[]{:S(2)}, u32[]{:S(2)}) %collective-permute-start) | collective-permute-done | bytes 49184 | tf_op jit(solution)/shard_map/ppermute | solution.py:335
  122.8 1.0 fusion.2
  (3 shorter events, 0.0 us)
Async XLA Ops:
  22.3 1.1 copy-start.1
  23.4 0.9 copy-start.4
  29.3 2.0 %copy-start = (f32[128,64,128]{2,1,0:T(8,128)}, f32[128,64,128]{2,1,0:T(8,128)S(1)}, u32[]{:S(2)}) copy-start(f32[128,64,128]{2,1,0:T(8,128)S(1)} %open_leaves.1) | copy-start | bytes 12582916
  31.2 7.1 %copy-start.2 = (f32[256,3,128]{2,0,1:T(8,128)S(1)}, f32[256,3,128]{2,0,1:T(8,128)}, u32[]{:S(2)}) copy-start(f32[256,3,128]{2,0,1:T(8,128)} %param.11) | copy-start | bytes 1179652
  31.2 7.1 %copy-start.5 = (s32[256,512]{1,0:T(8,128)S(1)}, s32[256,512]{1,0:T(8,128)}, u32[]{:S(2)}) copy-start(s32[256,512]{1,0:T(8,128)} %list_ref.1) | copy-start | bytes 1572868
  31.2 7.1 %copy-start.6 = (f32[3,512]{1,0:T(4,128)S(1)}, f32[3,512]{1,0:T(4,128)}, u32[]{:S(2)}) copy-start(f32[3,512]{1,0:T(4,128)} %node_ref.1) | copy-start | bytes 18436
  31.3 7.1 %copy-start.7 = (s32[1,128,8]{1,2,0:T(8,128)S(1)}, s32[1,128,8]{1,2,0:T(8,128)}, u32[]{:S(2)}) copy-start(s32[1,128,8]{1,2,0:T(8,128)} %param.18) | copy-start | bytes 12292
  31.3 7.1 %copy-start.8 = (f32[512]{0:T(512)S(1)}, f32[512]{0:T(512)}, u32[]{:S(2)}) copy-start(f32[512]{0:T(512)} %param.16) | copy-start | bytes 6148
  31.3 7.1 %copy-start.9 = (s32[1,128]{1,0:T(1,128)S(1)}, s32[1,128]{1,0:T(1,128)}, u32[]{:S(2)}) copy-start(s32[1,128]{1,0:T(1,128)} %param.20) | copy-start | bytes 1540
  31.3 58.0 %all-to-all-start.1 = ((f32[128,64,128]{2,1,0:T(8,128)}), f32[128,64,128]{2,1,0:T(8,128)}, u32[]{:S(2)}, u32[]{:S(2)}) async-start(f32[128,64,128]{2,1,0:T(8,128)} %copy-done), calls=%async_computation.1 | async-start | bytes 8388608 | tf_op jit(solution)/shard_map/all_to_all | solution.py:363
  38.4 50.8 %copy-start.3 = (f32[256,3,128]{2,0,1:T(8,128)S(1)}, f32[256,3,128]{2,0,1:T(8,128)}, u32[]{:S(2)}) copy-start(f32[256,3,128]{2,0,1:T(8,128)} %param.12) | copy-start | bytes 1179652
  113.8 9.1 %collective-permute-start = (f32[6,16,128]{2,1,0:T(8,128)S(1)}, f32[6,16,128]{2,1,0:T(8,128)S(1)}, u32[]{:S(2)}, u32[]{:S(2)}) collective-permute-start(f32[6,16,128]{2,1,0:T(8,128)S(1)} %slice.4), channel_id=1, source_target_pairs={{0,1},{1,2},{2,3},{3,4},{4,5},{5,6},{6,7},{7,8},{8,9},{9,10},{10,1... | collective-permute-start | bytes 147464 | tf_op jit(solution)/shard_map/ppermute | solution.py:335

commit v5 on v4

--- a/solution.py
+++ b/solution.py
@@ -73,10 +73,13 @@
 def open_kernel(ids_ref, pos_hbm, mass_hbm, out_hbm, pos, mass, table, out, in_sem, out_sem):
     leaf_count = pos.shape[1]
     peers = out.shape[0]
-    loads = [
-        pltpu.make_async_copy(pos_hbm, pos, in_sem.at[0]),
-        pltpu.make_async_copy(mass_hbm, mass, in_sem.at[1]),
-    ]
+    loads = []
+    part = leaf_count // 1
+    for q in range(1):
+        rows = pl.ds(q * part, part)
+        loads.append(pltpu.make_async_copy(mass_hbm.at[rows], mass.at[rows], in_sem.at[4 * q + 3]))
+        for c in range(3):
+            loads.append(pltpu.make_async_copy(pos_hbm.at[c, rows], pos.at[c, rows], in_sem.at[4 * q + c]))
     for load in loads:
         load.start()
     for load in loads:
@@ -90,7 +93,7 @@
             table[pl.ds(first * 8 + 4 + c, 8, stride=8), :] = v
         return carry
 
-    lax.fori_loop(0, leaf_count // 8, build, 0, unroll=4)
+    lax.fori_loop(0, leaf_count // 8, build, 0, unroll=8)
     upper = lax.broadcasted_iota(jnp.int32, (8, LANES), 0) < 4
 
     def one_peer(p, carry):
@@ -103,9 +106,9 @@
         return carry
 
     stores = []
-    step = peers // 4
-    for q in range(4):
-        lax.fori_loop(q * step, (q + 1) * step, one_peer, 0, unroll=2)
+    step = peers // 32
+    for q in range(32):
+        lax.fori_loop(q * step, (q + 1) * step, one_peer, 0, unroll=4)
         rows = pl.ds(q * step, step)
         stores.append(pltpu.make_async_copy(out.at[rows], out_hbm.at[rows], out_sem.at[q]))
         stores[-1].start()
@@ -130,10 +133,10 @@
             pltpu.VMEM(leaf_mass.shape, f32),
             pltpu.VMEM((leaf_pos.shape[1] * 8, LANES), f32),
             pltpu.VMEM(shape, f32),
-            pltpu.SemaphoreType.DMA((2,)),
             pltpu.SemaphoreType.DMA((4,)),
+            pltpu.SemaphoreType.DMA((32,)),
         ],
-        compiler_params=pltpu.CompilerParams(vmem_limit_bytes=24 << 20),
+        compiler_params=pltpu.CompilerParams(vmem_limit_bytes=60 << 20),
         name="open_leaves",
     )(ids, leaf_pos, leaf_mass)
 

time: 125 us -> 123 us (0.984)
  local copies, waits for them, and re-layouts: 5.57 us -> 2.14 us
  Pallas kernels: 74.1 us -> 77.1 us
    unnamed x20 -> x14, local copies, waits for them, and re-layouts: 4.08 us -> 0.04 us
    pallas_call x1, Pallas kernels: 24.5 us -> 26.4 us  [remote_pull(): pl.pallas_call(remote_kernel, out_shape=jax.ShapeDtypeStruct((6, groups,...]
where the time goes in v5:
time: 123 us
  Pallas kernels  77.1 us (63%)
  blocking collectives  21.1 us (17%)
  waiting for transfers between devices  11.9 us (10%)
  starting transfers between devices  7.92 us (6%)
  local copies, waits for them, and re-layouts  2.14 us (2%)
  between operations  1.47 us (1%)
    pallas_call x1, Pallas kernels, local_pull(): pl.pallas_call(local_kernel, out_shape=(jax.ShapeDtypeStruct((3, groups,...  44.8 us
    pallas_call x1, Pallas kernels, remote_pull(): pl.pallas_call(remote_kernel, out_shape=jax.ShapeDtypeStruct((6, groups,...  26.4 us
    all_to_all x1, blocking collectives, per_device(): got = lax.all_to_all(asked, AXES, split_axis=0, concat_axis=0, tiled=True)  21.1 us
    ppermute x1, waiting for transfers between devices, shifted(): lax.ppermute(value, axis, [(source, source + steps) for source in range(c...  6.44 us
    pallas_call x1, Pallas kernels, open_leaves(): pl.pallas_call(open_kernel, out_shape=jax.ShapeDtypeStruct(shape, f32), i...  5.93 us
    all_to_all x1, starting transfers between devices, per_device(): recv = lax.all_to_all(opened, AXES, split_axis=0, concat_axis=0, tiled=True)  5.76 us
    all_to_all x1, waiting for transfers between devices, per_device(): recv = lax.all_to_all(opened, AXES, split_axis=0, concat_axis=0, tiled=True)  5.46 us
  transfers between devices with their start and end apart: 2, of which 2 were waited for; matrix products, arithmetic and copies ran while one was open for 1% of the time, Pallas kernels for 36%

profile of v5, /device:TPU:1, one launch (start us, length us, event | category | flops | bytes accessed | tf_op | source)
XLA Modules:
  0.0 122.8 jit_solution(17730168124755748475)
XLA Ops:
  0.7 0.7 pad_bitcast_fusion
  1.4 0.1 copy.14
  1.5 21.1 %all_to_all.16 = s32[128,1,17]{2,1,0:T(1,128)} all-to-all(s32[128,1,17]{2,1,0:T(1,128)S(1)} %copy.14), channel_id=1, replica_groups=mesh['dom'=8,'bulk'=16] {'dom','bulk'}, dimensions={0} | all-to-all | bytes 17408 | tf_op jit(solution)/shard_map/all_to_all | solution.py:359
  22.6 5.9 %open_leaves.1 = f32[128,64,128]{2,1,0:T(8,128)} custom-call(s32[128,17]{1,0:T(8,128)} %bitcast.26, f32[3,512,128]{2,1,0:T(8,128)} %bitcast.25, f32[512,128]{1,0:T(8,128)} %mass_hbm.1), custom_call_target="tpu_custom_call" | custom-call | tf_op jit(solution)/shard_map/open_leaves/pallas_call | solution.py:122
  28.5 0.0 copy-start
  28.5 0.0 copy-start.2
  28.6 0.0 copy-start.3
  28.6 0.0 copy-start.4
  28.6 0.0 copy-start.5
  28.6 0.0 copy-start.6
  28.6 5.8 %all-to-all-start.1 = ((f32[128,64,128]{2,1,0:T(8,128)}), f32[128,64,128]{2,1,0:T(8,128)}, u32[]{:S(2)}, u32[]{:S(2)}) async-start(f32[128,64,128]{2,1,0:T(8,128)} %open_leaves.1), calls=%async_computation.1 | async-start | bytes 8388608 | tf_op jit(solution)/shard_map/all_to_all | solution.py:366
  34.4 1.2 constant_dynamic-slice_fusion
  36.3 0.1 pad_dynamic-slice_fusion.2
  36.3 0.0 copy-done
  36.3 0.0 copy-done.2
  36.4 0.0 copy-done.3
  36.4 0.0 copy-done.4
  36.4 0.0 copy-done.5
  36.4 0.0 copy-done.6
  36.4 0.0 copy-start.1
  36.4 44.8 %local_pull.1 = (f32[3,256,128]{2,1,0:T(8,128)S(1)}, s32[1088]{0:T(1024)S(1)}) custom-call(s32[8,128]{1,0:T(8,128)S(1)} %bitcast.22, s32[128]{0:T(128)S(1)} %bitcast.24, f32[3,256,128]{2,1,0:T(8,128)S(1)} %bitcast.19, f32[3,512]{1,0:T(4,128)S(1)} %copy-done.3, f32[1,512]{1,0:T(1,128)S(1)} %bitcast.23, s32[256,512]{1,0:T(8,128)S(1)} %copy-done.2), custom_call_target="tpu_custom_call" | custom-call | flops 33554432000 | bytes 4194304 | tf_op jit(solution)/shard_map/local_pull/pallas_call | solution.py:222
  81.2 5.5 %all-to-all-done.1 = f32[128,64,128]{2,1,0:T(8,128)} async-done(((f32[128,64,128]{2,1,0:T(8,128)}), f32[128,64,128]{2,1,0:T(8,128)}, u32[]{:S(2)}, u32[]{:S(2)}) %all-to-all-start.1) | async-done | bytes 4194336 | tf_op jit(solution)/shard_map/all_to_all | solution.py:366
  86.6 0.0 copy-done.1
  86.6 26.4 %remote_pull.1 = f32[6,256,128]{2,1,0:T(8,128)S(1)} custom-call(s32[1088]{0:T(1024)S(1)} %get-tuple-element.10.todo, f32[8192,128]{1,0:T(8,128)} %bitcast.10.recv_ref, f32[3,256,128]{2,1,0:T(8,128)S(1)} %bitcast.20, f32[3,256,128]{2,1,0:T(8,128)S(1)} %bitcast.21, f32[3,256,128]{2,1,0:T(8,128)S(1)} %get-tuple-element.12.local_ref), custom_call_target="tpu_custom_call" | custom-call | tf_op jit(solution)/shard_map/remote_pull/pallas_call | solution.py:318
  113.1 2.2 %collective-permute-start = (f32[6,16,128]{2,1,0:T(8,128)S(1)}, f32[6,16,128]{2,1,0:T(8,128)S(1)}, u32[]{:S(2)}, u32[]{:S(2)}) collective-permute-start(f32[6,16,128]{2,1,0:T(8,128)S(1)} %slice.4), channel_id=1, source_target_pairs={{0,1},{1,2},{2,3},{3,4},{4,5},{5,6},{6,7},{7,8},{8,9},{9,10},{10,1... | collective-permute-start | bytes 147464 | tf_op jit(solution)/shard_map/ppermute | solution.py:338
  115.2 0.1 broadcast_multiply_fusion
  115.4 6.4 %collective-permute-done = f32[6,16,128]{2,1,0:T(8,128)S(1)} collective-permute-done((f32[6,16,128]{2,1,0:T(8,128)S(1)}, f32[6,16,128]{2,1,0:T(8,128)S(1)}, u32[]{:S(2)}, u32[]{:S(2)}) %collective-permute-start) | collective-permute-done | bytes 49184 | tf_op jit(solution)/shard_map/ppermute | solution.py:338
  121.8 1.0 fusion.2
  (3 shorter events, 0.0 us)
Async XLA Ops:
  28.5 7.8 %copy-start = (f32[256,3,128]{2,0,1:T(8,128)S(1)}, f32[256,3,128]{2,0,1:T(8,128)}, u32[]{:S(2)}) copy-start(f32[256,3,128]{2,0,1:T(8,128)} %param.11) | copy-start | bytes 1179652
  28.5 7.8 %copy-start.2 = (s32[256,512]{1,0:T(8,128)S(1)}, s32[256,512]{1,0:T(8,128)}, u32[]{:S(2)}) copy-start(s32[256,512]{1,0:T(8,128)} %list_ref.1) | copy-start | bytes 1572868
  28.6 7.8 %copy-start.3 = (f32[3,512]{1,0:T(4,128)S(1)}, f32[3,512]{1,0:T(4,128)}, u32[]{:S(2)}) copy-start(f32[3,512]{1,0:T(4,128)} %node_ref.1) | copy-start | bytes 18436
  28.6 7.8 %copy-start.4 = (s32[1,128,8]{1,2,0:T(8,128)S(1)}, s32[1,128,8]{1,2,0:T(8,128)}, u32[]{:S(2)}) copy-start(s32[1,128,8]{1,2,0:T(8,128)} %param.18) | copy-start | bytes 12292
  28.6 7.8 %copy-start.5 = (f32[512]{0:T(512)S(1)}, f32[512]{0:T(512)}, u32[]{:S(2)}) copy-start(f32[512]{0:T(512)} %param.16) | copy-start | bytes 6148
  28.6 7.8 %copy-start.6 = (s32[1,128]{1,0:T(1,128)S(1)}, s32[1,128]{1,0:T(1,128)}, u32[]{:S(2)}) copy-start(s32[1,128]{1,0:T(1,128)} %param.20) | copy-start | bytes 1540
  28.6 58.0 %all-to-all-start.1 = ((f32[128,64,128]{2,1,0:T(8,128)}), f32[128,64,128]{2,1,0:T(8,128)}, u32[]{:S(2)}, u32[]{:S(2)}) async-start(f32[128,64,128]{2,1,0:T(8,128)} %open_leaves.1), calls=%async_computation.1 | async-start | bytes 8388608 | tf_op jit(solution)/shard_map/all_to_all | solution.py:366
  36.4 50.2 %copy-start.1 = (f32[256,3,128]{2,0,1:T(8,128)S(1)}, f32[256,3,128]{2,0,1:T(8,128)}, u32[]{:S(2)}) copy-start(f32[256,3,128]{2,0,1:T(8,128)} %param.12) | copy-start | bytes 1179652
  113.1 8.7 %collective-permute-start = (f32[6,16,128]{2,1,0:T(8,128)S(1)}, f32[6,16,128]{2,1,0:T(8,128)S(1)}, u32[]{:S(2)}, u32[]{:S(2)}) collective-permute-start(f32[6,16,128]{2,1,0:T(8,128)S(1)} %slice.4), channel_id=1, source_target_pairs={{0,1},{1,2},{2,3},{3,4},{4,5},{5,6},{6,7},{7,8},{8,9},{9,10},{10,1... | collective-permute-start | bytes 147464 | tf_op jit(solution)/shard_map/ppermute | solution.py:338

commit v6 on v5

--- a/solution.py
+++ b/solution.py
@@ -15,7 +15,9 @@
 LANES = 128
 ROWS = 32
 SLOTS = 8
-BATCH = 32
+TOGETHER = 32
+BATCH = 64
+TAIL = 16
 
 SMEM_SPEC = pl.BlockSpec(memory_space=pltpu.SMEM)
 VMEM_SPEC = pl.BlockSpec(memory_space=pltpu.VMEM)
@@ -170,18 +172,21 @@
     raw[...] = jnp.zeros_like(raw)
 
     def one_block(b, carry):
-        first = pl.multiple_of(b * 8, 8)
-        x = [pos_ref[c, pl.ds(first, 8), :] - MID for c in range(3)]
-        for r, v in enumerate(target_rows(x)):
-            xk[pl.ds(r, 8, stride=ROWS), :] = v
-        lists = list_ref[pl.ds(first, 8), :]
+        first = pl.multiple_of(b * TOGETHER, TOGETHER)
+        places = []
+        for q in range(TOGETHER // 8):
+            x = [pos_ref[c, pl.ds(first + q * 8, 8), :] - MID for c in range(3)]
+            places.append(x)
+            for r, v in enumerate(target_rows(x)):
+                xk[pl.ds(q * 8 * ROWS + r, 8, stride=ROWS), :] = v
+        lists = list_ref[pl.ds(first, TOGETHER), :]
         counts = []
-        for g in range(8):
+        for g in range(TOGETHER):
             wanted = lists[g : g + 1, :]
             low = jnp.where(row128 == (wanted & 127), 1.0, 0.0).astype(bf16)
             high = jnp.where(row16 == (wanted >> 7), 1.0, 0.0).astype(bf16)
             counts.append(dot_t(high, low))
-        for p in range(4):
+        for p in range(TOGETHER // 2):
             parts = []
             for h in range(nodes // LANES):
                 both = jnp.where(
@@ -206,12 +211,14 @@
             total = total[0:8] + total[8:16] + total[16:24]
             raw[pl.ds(2 * p * 8, 4), :] = total[0:4, :LANES]
             raw[pl.ds((2 * p + 1) * 8, 4), :] = total[4:8, LANES:]
-        weight = raw[pl.ds(3, 8, stride=8), :]
-        for c in range(3):
-            acc_ref[c, pl.ds(first, 8), :] = raw[pl.ds(c, 8, stride=8), :] - x[c] * weight
-        return carry
-
-    lax.fori_loop(0, acc_ref.shape[1] // 8, one_block, 0)
+        for q, x in enumerate(places):
+            weight = raw[pl.ds(q * 64 + 3, 8, stride=8), :]
+            for c in range(3):
+                pull = raw[pl.ds(q * 64 + c, 8, stride=8), :] - x[c] * weight
+                acc_ref[c, pl.ds(first + q * 8, 8), :] = pull
+        return carry
+
+    lax.fori_loop(0, acc_ref.shape[1] // TOGETHER, one_block, 0)
 
 
 def local_pull(export_group, export_count, pos, node_pos, node_mass, lists):
@@ -229,8 +236,8 @@
         out_specs=[VMEM_SPEC, SMEM_SPEC],
         scratch_shapes=[
             pltpu.VMEM((nodes, ROWS), bf16),
-            pltpu.VMEM((8 * ROWS, LANES), f32),
-            pltpu.VMEM((64, LANES), f32),
+            pltpu.VMEM((TOGETHER * ROWS, LANES), f32),
+            pltpu.VMEM((TOGETHER * 8, LANES), f32),
         ],
         compiler_params=pltpu.CompilerParams(vmem_limit_bytes=16 << 20),
         cost_estimate=pl.CostEstimate(
@@ -258,18 +265,18 @@
     scale = 1.0 + lane * (1.0 / LANES)
     lift = scale * jnp.sqrt(scale)
 
-    def one_block(b, carry):
+    def one_batch(size, start, b, carry):
         owners = []
-        for s in range(BATCH):
-            entry = todo[b * BATCH + s]
+        for s in range(size):
+            entry = todo[start + b * size + s]
             g = entry & 255
             owners.append(g)
             tile[pl.ds(s * 8, 8), :] = recv_ref[pl.ds(pl.multiple_of((entry >> 8) * 8, 8), 8), :]
             for c in range(3):
                 place[c, pl.ds(s, 1), :] = pos_ref[c, pl.ds(g, 1), :]
-        for q in range(BATCH // 8):
+        for q in range(size // 8):
             first = q * 8
-            rank = lax.broadcasted_iota(jnp.int32, (8, LANES), 0) + (b * BATCH + first)
+            rank = lax.broadcasted_iota(jnp.int32, (8, LANES), 0) + (start + b * size + first)
             x = [place[c, pl.ds(first, 8), :] - MID for c in range(3)]
             for r, v in enumerate(target_rows(x)):
                 xk[pl.ds(first * ROWS + r, 8, stride=ROWS), :] = v
@@ -283,7 +290,7 @@
                 for c, v in enumerate([m * y[0], m * y[1], m * y[2], m]):
                     for j, part in enumerate(split3(v)):
                         tk[pl.ds(base * 16 + 4 * j + c, 8, stride=16), :] = part
-        for s in range(BATCH):
+        for s in range(size):
             xt = jnp.transpose(xk[pl.ds(s * ROWS, ROWS), :]).astype(bf16)
             rhs = [yk[pl.ds((h * BATCH + s) * ROWS, ROWS), :] for h in range(2)]
             r2 = dot(xt, jnp.concatenate(rhs, axis=1).astype(bf16))
@@ -294,7 +301,10 @@
             acc[rows, :] += total[0:8] + total[8:16]
         return carry
 
-    lax.fori_loop(0, (count + BATCH - 1) // BATCH, one_block, 0)
+    whole = count // BATCH
+    lax.fori_loop(0, whole, functools.partial(one_batch, BATCH, 0), 0)
+    rest = count - whole * BATCH
+    lax.fori_loop(0, (rest + TAIL - 1) // TAIL, functools.partial(one_batch, TAIL, whole * BATCH), 0)
 
     def finish(b, carry):
         first = pl.multiple_of(b * 8, 8)

time: 123 us -> 121 us (0.984)
  Pallas kernels: 77.1 us -> 64.8 us
  waiting for transfers between devices: 11.9 us -> 22.4 us
    all_to_all x1, waiting for transfers between devices: 5.46 us -> 15.8 us  [per_device(): recv = lax.all_to_all(opened, AXES, split_axis=0, concat_axis=0, tiled=True)]
    pallas_call x1, Pallas kernels: 44.8 us -> 34.5 us  [local_pull(): pl.pallas_call(local_kernel, out_shape=(jax.ShapeDtypeStruct((3, groups,...]
    pallas_call x1, Pallas kernels: 26.4 us -> 24.4 us  [remote_pull(): pl.pallas_call(remote_kernel, out_shape=jax.ShapeDtypeStruct((6, groups,...]
  transfers between devices with their start and end apart: 2 -> 2, of which waited for: 2 -> 2; matrix products, arithmetic and copies ran while one was open for 1% -> 1% of each run, Pallas kernels for 36% -> 29%
where the time goes in v6:
time: 121 us
  Pallas kernels  64.8 us (54%)
  waiting for transfers between devices  22.4 us (19%)
  blocking collectives  21.1 us (17%)
  starting transfers between devices  7.69 us (6%)
  local copies, waits for them, and re-layouts  2.14 us (2%)
  between operations  1.47 us (1%)
    pallas_call x1, Pallas kernels, local_pull(): pl.pallas_call(local_kernel, out_shape=(jax.ShapeDtypeStruct((3, groups,...  34.5 us
    pallas_call x1, Pallas kernels, remote_pull(): pl.pallas_call(remote_kernel, out_shape=jax.ShapeDtypeStruct((6, groups,...  24.4 us
    all_to_all x1, blocking collectives, per_device(): got = lax.all_to_all(asked, AXES, split_axis=0, concat_axis=0, tiled=True)  21.1 us
    all_to_all x1, waiting for transfers between devices, per_device(): recv = lax.all_to_all(opened, AXES, split_axis=0, concat_axis=0, tiled=True)  15.8 us
    ppermute x1, waiting for transfers between devices, shifted(): lax.ppermute(value, axis, [(source, source + steps) for source in range(c...  6.67 us
    pallas_call x1, Pallas kernels, open_leaves(): pl.pallas_call(open_kernel, out_shape=jax.ShapeDtypeStruct(shape, f32), i...  5.93 us
    all_to_all x1, starting transfers between devices, per_device(): recv = lax.all_to_all(opened, AXES, split_axis=0, concat_axis=0, tiled=True)  5.76 us
  transfers between devices with their start and end apart: 2, of which 2 were waited for; matrix products, arithmetic and copies ran while one was open for 1% of the time, Pallas kernels for 29%

profile of v6, /device:TPU:1, one launch (start us, length us, event | category | flops | bytes accessed | tf_op | source)
XLA Modules:
  0.0 120.8 jit_solution(8586822377494619917)
XLA Ops:
  0.7 0.7 pad_bitcast_fusion
  1.4 0.1 copy.14
  1.5 21.1 %all_to_all.16 = s32[128,1,17]{2,1,0:T(1,128)} all-to-all(s32[128,1,17]{2,1,0:T(1,128)S(1)} %copy.14), channel_id=1, replica_groups=mesh['dom'=8,'bulk'=16] {'dom','bulk'}, dimensions={0} | all-to-all | bytes 17408 | tf_op jit(solution)/shard_map/all_to_all | solution.py:369
  22.6 5.9 %open_leaves.1 = f32[128,64,128]{2,1,0:T(8,128)} custom-call(s32[128,17]{1,0:T(8,128)} %bitcast.26, f32[3,512,128]{2,1,0:T(8,128)} %bitcast.25, f32[512,128]{1,0:T(8,128)} %mass_hbm.1), custom_call_target="tpu_custom_call" | custom-call | tf_op jit(solution)/shard_map/open_leaves/pallas_call | solution.py:124
  28.5 0.0 copy-start
  28.5 0.0 copy-start.2
  28.6 0.0 copy-start.3
  28.6 0.0 copy-start.4
  28.6 0.0 copy-start.5
  28.6 0.0 copy-start.6
  28.6 5.8 %all-to-all-start.1 = ((f32[128,64,128]{2,1,0:T(8,128)}), f32[128,64,128]{2,1,0:T(8,128)}, u32[]{:S(2)}, u32[]{:S(2)}) async-start(f32[128,64,128]{2,1,0:T(8,128)} %open_leaves.1), calls=%async_computation.1 | async-start | bytes 8388608 | tf_op jit(solution)/shard_map/all_to_all | solution.py:376
  34.4 1.2 constant_dynamic-slice_fusion
  36.3 0.1 pad_dynamic-slice_fusion.2
  36.3 0.0 copy-done
  36.3 0.0 copy-done.2
  36.4 0.0 copy-done.3
  36.4 0.0 copy-done.4
  36.4 0.0 copy-done.5
  36.4 0.0 copy-done.6
  36.4 0.0 copy-start.1
  36.4 34.5 %local_pull.1 = (f32[3,256,128]{2,1,0:T(8,128)S(1)}, s32[1152]{0:T(1024)S(1)}) custom-call(s32[8,128]{1,0:T(8,128)S(1)} %bitcast.22, s32[128]{0:T(128)S(1)} %bitcast.24, f32[3,256,128]{2,1,0:T(8,128)S(1)} %bitcast.19, f32[3,512]{1,0:T(4,128)S(1)} %copy-done.3, f32[1,512]{1,0:T(1,128)S(1)} %bitcast.23, s32[256,512]{1,0:T(8,128)S(1)} %copy-done.2), custom_call_target="tpu_custom_call" | custom-call | flops 33554432000 | bytes 4194304 | tf_op jit(solution)/shard_map/local_pull/pallas_call | solution.py:229
  70.9 15.8 %all-to-all-done.1 = f32[128,64,128]{2,1,0:T(8,128)} async-done(((f32[128,64,128]{2,1,0:T(8,128)}), f32[128,64,128]{2,1,0:T(8,128)}, u32[]{:S(2)}, u32[]{:S(2)}) %all-to-all-start.1) | async-done | bytes 4194336 | tf_op jit(solution)/shard_map/all_to_all | solution.py:376
  86.6 0.0 copy-done.1
  86.6 24.4 %remote_pull.1 = f32[6,256,128]{2,1,0:T(8,128)S(1)} custom-call(s32[1152]{0:T(1024)S(1)} %get-tuple-element.10.todo, f32[8192,128]{1,0:T(8,128)} %bitcast.10.recv_ref, f32[3,256,128]{2,1,0:T(8,128)S(1)} %bitcast.20, f32[3,256,128]{2,1,0:T(8,128)S(1)} %bitcast.21, f32[3,256,128]{2,1,0:T(8,128)S(1)} %get-tuple-element.12.local_ref), custom_call_target="tpu_custom_call" | custom-call | tf_op jit(solution)/shard_map/remote_pull/pallas_call | solution.py:328
  111.0 1.9 %collective-permute-start = (f32[6,16,128]{2,1,0:T(8,128)S(1)}, f32[6,16,128]{2,1,0:T(8,128)S(1)}, u32[]{:S(2)}, u32[]{:S(2)}) collective-permute-start(f32[6,16,128]{2,1,0:T(8,128)S(1)} %slice.4), channel_id=1, source_target_pairs={{0,1},{1,2},{2,3},{3,4},{4,5},{5,6},{6,7},{7,8},{8,9},{9,10},{10,1... | collective-permute-start | bytes 147464 | tf_op jit(solution)/shard_map/ppermute | solution.py:348
  113.0 0.1 broadcast_multiply_fusion
  113.1 6.7 %collective-permute-done = f32[6,16,128]{2,1,0:T(8,128)S(1)} collective-permute-done((f32[6,16,128]{2,1,0:T(8,128)S(1)}, f32[6,16,128]{2,1,0:T(8,128)S(1)}, u32[]{:S(2)}, u32[]{:S(2)}) %collective-permute-start) | collective-permute-done | bytes 49184 | tf_op jit(solution)/shard_map/ppermute | solution.py:348
  119.8 1.0 fusion.2
  (3 shorter events, 0.0 us)
Async XLA Ops:
  28.5 7.8 %copy-start = (f32[256,3,128]{2,0,1:T(8,128)S(1)}, f32[256,3,128]{2,0,1:T(8,128)}, u32[]{:S(2)}) copy-start(f32[256,3,128]{2,0,1:T(8,128)} %param.11) | copy-start | bytes 1179652
  28.5 7.8 %copy-start.2 = (s32[256,512]{1,0:T(8,128)S(1)}, s32[256,512]{1,0:T(8,128)}, u32[]{:S(2)}) copy-start(s32[256,512]{1,0:T(8,128)} %list_ref.1) | copy-start | bytes 1572868
  28.6 7.8 %copy-start.3 = (f32[3,512]{1,0:T(4,128)S(1)}, f32[3,512]{1,0:T(4,128)}, u32[]{:S(2)}) copy-start(f32[3,512]{1,0:T(4,128)} %node_ref.1) | copy-start | bytes 18436
  28.6 7.8 %copy-start.4 = (s32[1,128,8]{1,2,0:T(8,128)S(1)}, s32[1,128,8]{1,2,0:T(8,128)}, u32[]{:S(2)}) copy-start(s32[1,128,8]{1,2,0:T(8,128)} %param.18) | copy-start | bytes 12292
  28.6 7.8 %copy-start.5 = (f32[512]{0:T(512)S(1)}, f32[512]{0:T(512)}, u32[]{:S(2)}) copy-start(f32[512]{0:T(512)} %param.16) | copy-start | bytes 6148
  28.6 7.8 %copy-start.6 = (s32[1,128]{1,0:T(1,128)S(1)}, s32[1,128]{1,0:T(1,128)}, u32[]{:S(2)}) copy-start(s32[1,128]{1,0:T(1,128)} %param.20) | copy-start | bytes 1540
  28.6 58.0 %all-to-all-start.1 = ((f32[128,64,128]{2,1,0:T(8,128)}), f32[128,64,128]{2,1,0:T(8,128)}, u32[]{:S(2)}, u32[]{:S(2)}) async-start(f32[128,64,128]{2,1,0:T(8,128)} %open_leaves.1), calls=%async_computation.1 | async-start | bytes 8388608 | tf_op jit(solution)/shard_map/all_to_all | solution.py:376
  36.4 50.2 %copy-start.1 = (f32[256,3,128]{2,0,1:T(8,128)S(1)}, f32[256,3,128]{2,0,1:T(8,128)}, u32[]{:S(2)}) copy-start(f32[256,3,128]{2,0,1:T(8,128)} %param.12) | copy-start | bytes 1179652
  111.0 8.7 %collective-permute-start = (f32[6,16,128]{2,1,0:T(8,128)S(1)}, f32[6,16,128]{2,1,0:T(8,128)S(1)}, u32[]{:S(2)}, u32[]{:S(2)}) collective-permute-start(f32[6,16,128]{2,1,0:T(8,128)S(1)} %slice.4), channel_id=1, source_target_pairs={{0,1},{1,2},{2,3},{3,4},{4,5},{5,6},{6,7},{7,8},{8,9},{9,10},{10,1... | collective-permute-start | bytes 147464 | tf_op jit(solution)/shard_map/ppermute | solution.py:348

commit v7 on v6

--- a/solution.py
+++ b/solution.py
@@ -72,7 +72,11 @@
     return rs * rs * rs
 
 
-def open_kernel(ids_ref, pos_hbm, mass_hbm, out_hbm, pos, mass, table, out, in_sem, out_sem):
+def open_kernel(
+    ids_any, pos_hbm, mass_hbm, out_hbm, ids_ref, pos, mass, table, out, ids_sem, in_sem, out_sem
+):
+    fetch = pltpu.make_async_copy(ids_any, ids_ref, ids_sem)
+    fetch.start()
     leaf_count = pos.shape[1]
     peers = out.shape[0]
     loads = []
@@ -107,6 +111,7 @@
             )
         return carry
 
+    fetch.wait()
     stores = []
     step = peers // 32
     for q in range(32):
@@ -125,16 +130,18 @@
         open_kernel,
         out_shape=jax.ShapeDtypeStruct(shape, f32),
         in_specs=[
-            pl.BlockSpec(memory_space=pltpu.SMEM),
+            pl.BlockSpec(memory_space=pl.ANY),
             pl.BlockSpec(memory_space=pltpu.HBM),
             pl.BlockSpec(memory_space=pltpu.HBM),
         ],
         out_specs=pl.BlockSpec(memory_space=pltpu.HBM),
         scratch_shapes=[
+            pltpu.SMEM(ids.shape, jnp.int32),
             pltpu.VMEM(leaf_pos.shape, f32),
             pltpu.VMEM(leaf_mass.shape, f32),
             pltpu.VMEM((leaf_pos.shape[1] * 8, LANES), f32),
             pltpu.VMEM(shape, f32),
+            pltpu.SemaphoreType.DMA,
             pltpu.SemaphoreType.DMA((4,)),
             pltpu.SemaphoreType.DMA((32,)),
         ],
@@ -248,19 +255,25 @@
 
 
 def remote_kernel(
-    todo, recv_ref, pos_ref, vel_ref, local_ref, out_ref, tile, place, xk, yk, tk, acc
+    todo_ref, recv_ref, pos_ref, vel_ref, local_ref, out_ref, todo, tile, place, xk, yk, tk, acc, sem
 ):
     groups = pos_ref.shape[1]
-    count = todo[todo.shape[0] - 1]
-    xk[...] = jnp.zeros_like(xk)
-    yk[...] = jnp.zeros_like(yk)
-    tk[...] = jnp.zeros_like(tk)
+    fetch = pltpu.make_async_copy(todo_ref, todo, sem)
+    fetch.start()
+    blank = jnp.zeros((8, LANES), f32)
+    for s in range(BATCH):
+        xk[pl.ds(s * ROWS + 24, 8), :] = blank
+    for s in range(2 * BATCH):
+        yk[pl.ds(s * ROWS + 24, 8), :] = blank
+        tk[pl.ds(s * 16 + 8, 8), :] = blank
 
     def clear(i, carry):
         acc[pl.ds(pl.multiple_of(i * 64, 64), 64), :] = jnp.zeros((64, LANES), f32)
         return carry
 
     lax.fori_loop(0, groups * 8 // 64, clear, 0)
+    fetch.wait()
+    count = todo[todo.shape[0] - 1]
     lane = lax.broadcasted_iota(jnp.int32, (8, LANES), 1).astype(f32)
     scale = 1.0 + lane * (1.0 / LANES)
     lift = scale * jnp.sqrt(scale)
@@ -328,15 +341,17 @@
     return pl.pallas_call(
         remote_kernel,
         out_shape=jax.ShapeDtypeStruct((6, groups, LANES), f32),
-        in_specs=[SMEM_SPEC] + [VMEM_SPEC] * 4,
+        in_specs=[pl.BlockSpec(memory_space=pl.ANY)] + [VMEM_SPEC] * 4,
         out_specs=VMEM_SPEC,
         scratch_shapes=[
+            pltpu.SMEM(todo.shape, jnp.int32),
             pltpu.VMEM((BATCH * 8, LANES), f32),
             pltpu.VMEM((3, BATCH, LANES), f32),
             pltpu.VMEM((BATCH * ROWS, LANES), f32),
             pltpu.VMEM((2 * BATCH * ROWS, LANES), f32),
             pltpu.VMEM((2 * BATCH * 16, LANES), f32),
             pltpu.VMEM((groups * 8, LANES), f32),
+            pltpu.SemaphoreType.DMA,
         ],
         compiler_params=pltpu.CompilerParams(vmem_limit_bytes=24 << 20),
         name="remote_pull",

time: 121 us -> 121 us (level); the launches traced: 121 us -> 118 us
  Pallas kernels: 64.8 us -> 62.4 us
  starting transfers between devices: 7.69 us -> 9.07 us
  waiting for transfers between devices: 22.4 us -> 21.1 us
    ppermute x1, starting transfers between devices: 1.92 us -> 3.31 us  [shifted(): lax.ppermute(value, axis, [(source, source + steps) for source in range(c...]
    ppermute x1, waiting for transfers between devices: 6.67 us -> 5.29 us  [shifted(): lax.ppermute(value, axis, [(source, source + steps) for source in range(c...]
    pallas_call x1, Pallas kernels: 5.93 us -> 4.55 us  [open_leaves(): pl.pallas_call(open_kernel, out_shape=jax.ShapeDtypeStruct(shape, f32), i...]
where the time goes in v7:
time: 121 us; the launch traced here: 118 us
  Pallas kernels  62.4 us (52%)
  blocking collectives  21.1 us (17%)
  waiting for transfers between devices  21.1 us (17%)
  starting transfers between devices  9.07 us (7%)
  local copies, waits for them, and re-layouts  2.14 us (2%)
  between operations  1.47 us (1%)
    pallas_call x1, Pallas kernels, local_pull(): pl.pallas_call(local_kernel, out_shape=(jax.ShapeDtypeStruct((3, groups,...  34.5 us
    pallas_call x1, Pallas kernels, remote_pull(): pl.pallas_call(remote_kernel, out_shape=jax.ShapeDtypeStruct((6, groups,...  23.4 us
    all_to_all x1, blocking collectives, per_device(): got = lax.all_to_all(asked, AXES, split_axis=0, concat_axis=0, tiled=True)  21.1 us
    all_to_all x1, waiting for transfers between devices, per_device(): recv = lax.all_to_all(opened, AXES, split_axis=0, concat_axis=0, tiled=True)  15.8 us
    all_to_all x1, starting transfers between devices, per_device(): recv = lax.all_to_all(opened, AXES, split_axis=0, concat_axis=0, tiled=True)  5.76 us
    ppermute x1, waiting for transfers between devices, shifted(): lax.ppermute(value, axis, [(source, source + steps) for source in range(c...  5.29 us
    pallas_call x1, Pallas kernels, open_leaves(): pl.pallas_call(open_kernel, out_shape=jax.ShapeDtypeStruct(shape, f32), i...  4.55 us
    ppermute x1, starting transfers between devices, shifted(): lax.ppermute(value, axis, [(source, source + steps) for source in range(c...  3.31 us
  transfers between devices with their start and end apart: 2, of which 2 were waited for; matrix products, arithmetic and copies ran while one was open for 1% of the time, Pallas kernels for 29%

profile of v7, /device:TPU:1, one launch (start us, length us, event | category | flops | bytes accessed | tf_op | source)
XLA Modules:
  0.0 118.4 jit_solution(18389501374278871521)
XLA Ops:
  0.7 0.7 pad_bitcast_fusion
  1.4 0.1 copy.14
  1.5 21.1 %all_to_all.16 = s32[128,1,17]{2,1,0:T(1,128)} all-to-all(s32[128,1,17]{2,1,0:T(1,128)S(1)} %copy.14), channel_id=1, replica_groups=mesh['dom'=8,'bulk'=16] {'dom','bulk'}, dimensions={0} | all-to-all | bytes 17408 | tf_op jit(solution)/shard_map/all_to_all | solution.py:384
  22.6 4.6 %open_leaves.1 = f32[128,64,128]{2,1,0:T(8,128)} custom-call(s32[128,17]{1,0:T(8,128)} %bitcast.26, f32[3,512,128]{2,1,0:T(8,128)} %bitcast.25, f32[512,128]{1,0:T(8,128)} %mass_hbm.1), custom_call_target="tpu_custom_call" | custom-call | tf_op jit(solution)/shard_map/open_leaves/pallas_call | solution.py:129
  27.2 0.0 copy-start
  27.2 0.0 copy-start.2
  27.2 0.0 copy-start.3
  27.2 0.0 copy-start.4
  27.2 0.0 copy-start.5
  27.2 0.0 copy-start.6
  27.2 5.8 %all-to-all-start.1 = ((f32[128,64,128]{2,1,0:T(8,128)}), f32[128,64,128]{2,1,0:T(8,128)}, u32[]{:S(2)}, u32[]{:S(2)}) async-start(f32[128,64,128]{2,1,0:T(8,128)} %open_leaves.1), calls=%async_computation.1 | async-start | bytes 8388608 | tf_op jit(solution)/shard_map/all_to_all | solution.py:391
  33.0 1.2 %constant_dynamic-slice_fusion = s32[1,1,1]{2,1,0:T(1,128)} fusion(s32[128,1,17]{2,1,0:T(1,128)} %all_to_all.16, s32[]{:T(128)S(6)} %max.3), kind=kLoop, calls=%fused_computation.9 | loop fusion | bytes 12 | tf_op jit(solution)/shard_map/dynamic_slice | solution.py:395
  34.9 0.1 pad_dynamic-slice_fusion.2
  35.0 0.0 copy-done
  35.0 0.0 copy-done.2
  35.0 0.0 copy-done.3
  35.0 0.0 copy-done.4
  35.0 0.0 copy-done.5
  35.0 0.0 copy-done.6
  35.0 0.0 copy-start.1
  35.0 34.5 %local_pull.1 = (f32[3,256,128]{2,1,0:T(8,128)S(1)}, s32[1152]{0:T(1024)S(1)}) custom-call(s32[8,128]{1,0:T(8,128)S(1)} %bitcast.22, s32[128]{0:T(128)S(1)} %bitcast.24, f32[3,256,128]{2,1,0:T(8,128)S(1)} %bitcast.19, f32[3,512]{1,0:T(4,128)S(1)} %copy-done.3, f32[1,512]{1,0:T(1,128)S(1)} %bitcast.23, s32[256,512]{1,0:T(8,128)S(1)} %copy-done.2), custom_call_target="tpu_custom_call" | custom-call | flops 33554432000 | bytes 4194304 | tf_op jit(solution)/shard_map/local_pull/pallas_call | solution.py:236
  69.5 15.8 %all-to-all-done.1 = f32[128,64,128]{2,1,0:T(8,128)} async-done(((f32[128,64,128]{2,1,0:T(8,128)}), f32[128,64,128]{2,1,0:T(8,128)}, u32[]{:S(2)}, u32[]{:S(2)}) %all-to-all-start.1) | async-done | bytes 4194336 | tf_op jit(solution)/shard_map/all_to_all | solution.py:391
  85.2 0.0 copy-done.1
  85.2 23.4 %remote_pull.1 = f32[6,256,128]{2,1,0:T(8,128)S(1)} custom-call(s32[1152]{0:T(1024)S(1)} %get-tuple-element.10.todo_ref, f32[8192,128]{1,0:T(8,128)} %bitcast.10.recv_ref, f32[3,256,128]{2,1,0:T(8,128)S(1)} %bitcast.20, f32[3,256,128]{2,1,0:T(8,128)S(1)} %bitcast.21, f32[3,256,128]{2,1,0:T(8,128)S(1)} %get-tuple-element.12.local_ref), custom_call_target="tpu_custom_call" | custom-call | tf_op jit(solution)/shard_map/remote_pull/pallas_call | solution.py:341
  108.6 3.3 %collective-permute-start = (f32[6,16,128]{2,1,0:T(8,128)S(1)}, f32[6,16,128]{2,1,0:T(8,128)S(1)}, u32[]{:S(2)}, u32[]{:S(2)}) collective-permute-start(f32[6,16,128]{2,1,0:T(8,128)S(1)} %slice.4), channel_id=1, source_target_pairs={{0,1},{1,2},{2,3},{3,4},{4,5},{5,6},{6,7},{7,8},{8,9},{9,10},{10,1... | collective-permute-start | bytes 147464 | tf_op jit(solution)/shard_map/ppermute | solution.py:363
  111.9 0.1 broadcast_multiply_fusion
  112.1 5.3 %collective-permute-done = f32[6,16,128]{2,1,0:T(8,128)S(1)} collective-permute-done((f32[6,16,128]{2,1,0:T(8,128)S(1)}, f32[6,16,128]{2,1,0:T(8,128)S(1)}, u32[]{:S(2)}, u32[]{:S(2)}) %collective-permute-start) | collective-permute-done | bytes 49184 | tf_op jit(solution)/shard_map/ppermute | solution.py:363
  117.4 1.0 fusion.2
  (3 shorter events, 0.0 us)
Async XLA Ops:
  27.2 7.8 %copy-start = (f32[256,3,128]{2,0,1:T(8,128)S(1)}, f32[256,3,128]{2,0,1:T(8,128)}, u32[]{:S(2)}) copy-start(f32[256,3,128]{2,0,1:T(8,128)} %param.11) | copy-start | bytes 1179652
  27.2 7.8 %copy-start.2 = (s32[256,512]{1,0:T(8,128)S(1)}, s32[256,512]{1,0:T(8,128)}, u32[]{:S(2)}) copy-start(s32[256,512]{1,0:T(8,128)} %list_ref.1) | copy-start | bytes 1572868
  27.2 7.8 %copy-start.3 = (f32[3,512]{1,0:T(4,128)S(1)}, f32[3,512]{1,0:T(4,128)}, u32[]{:S(2)}) copy-start(f32[3,512]{1,0:T(4,128)} %node_ref.1) | copy-start | bytes 18436
  27.2 7.8 %copy-start.4 = (s32[1,128,8]{1,2,0:T(8,128)S(1)}, s32[1,128,8]{1,2,0:T(8,128)}, u32[]{:S(2)}) copy-start(s32[1,128,8]{1,2,0:T(8,128)} %param.18) | copy-start | bytes 12292
  27.2 7.8 %copy-start.5 = (f32[512]{0:T(512)S(1)}, f32[512]{0:T(512)}, u32[]{:S(2)}) copy-start(f32[512]{0:T(512)} %param.16) | copy-start | bytes 6148
  27.2 7.8 %copy-start.6 = (s32[1,128]{1,0:T(1,128)S(1)}, s32[1,128]{1,0:T(1,128)}, u32[]{:S(2)}) copy-start(s32[1,128]{1,0:T(1,128)} %param.20) | copy-start | bytes 1540
  27.2 58.0 %all-to-all-start.1 = ((f32[128,64,128]{2,1,0:T(8,128)}), f32[128,64,128]{2,1,0:T(8,128)}, u32[]{:S(2)}, u32[]{:S(2)}) async-start(f32[128,64,128]{2,1,0:T(8,128)} %open_leaves.1), calls=%async_computation.1 | async-start | bytes 8388608 | tf_op jit(solution)/shard_map/all_to_all | solution.py:391
  35.0 50.2 %copy-start.1 = (f32[256,3,128]{2,0,1:T(8,128)S(1)}, f32[256,3,128]{2,0,1:T(8,128)}, u32[]{:S(2)}) copy-start(f32[256,3,128]{2,0,1:T(8,128)} %param.12) | copy-start | bytes 1179652
  108.6 8.7 %collective-permute-start = (f32[6,16,128]{2,1,0:T(8,128)S(1)}, f32[6,16,128]{2,1,0:T(8,128)S(1)}, u32[]{:S(2)}, u32[]{:S(2)}) collective-permute-start(f32[6,16,128]{2,1,0:T(8,128)S(1)} %slice.4), channel_id=1, source_target_pairs={{0,1},{1,2},{2,3},{3,4},{4,5},{5,6},{6,7},{7,8},{8,9},{9,10},{10,1... | collective-permute-start | bytes 147464 | tf_op jit(solution)/shard_map/ppermute | solution.py:363

commit v8 on v7

--- a/solution.py
+++ b/solution.py
@@ -271,7 +271,7 @@
         acc[pl.ds(pl.multiple_of(i * 64, 64), 64), :] = jnp.zeros((64, LANES), f32)
         return carry
 
-    lax.fori_loop(0, groups * 8 // 64, clear, 0)
+    lax.fori_loop(0, groups * 8 // 64, clear, 0, unroll=4)
     fetch.wait()
     count = todo[todo.shape[0] - 1]
     lane = lax.broadcasted_iota(jnp.int32, (8, LANES), 1).astype(f32)
@@ -333,7 +333,7 @@
             out_ref[3 + c, rows, :] = vel_ref[c, rows, :] + KICK * pull
         return carry
 
-    lax.fori_loop(0, groups // 8, finish, 0, unroll=2)
+    lax.fori_loop(0, groups // 8, finish, 0, unroll=8)
 
 
 def remote_pull(todo, recv, pos, vel, local_acc):

time: 121 us -> 119 us (0.983); the launches traced: 118 us -> 121 us
  Pallas kernels: 62.4 us -> 64.6 us
  starting transfers between devices: 9.07 us -> 7.69 us
  waiting for transfers between devices: 21.1 us -> 22.4 us
    pallas_call x1, Pallas kernels: 23.4 us -> 25.6 us  [remote_pull(): pl.pallas_call(remote_kernel, out_shape=jax.ShapeDtypeStruct((6, groups,...]
    ppermute x1, starting transfers between devices: 3.31 us -> 1.92 us  [shifted(): lax.ppermute(value, axis, [(source, source + steps) for source in range(c...]
    ppermute x1, waiting for transfers between devices: 5.29 us -> 6.67 us  [shifted(): lax.ppermute(value, axis, [(source, source + steps) for source in range(c...]
where the time goes in v8:
time: 119 us; the launch traced here: 121 us
  Pallas kernels  64.6 us (54%)
  waiting for transfers between devices  22.4 us (19%)
  blocking collectives  21.1 us (18%)
  starting transfers between devices  7.69 us (6%)
  local copies, waits for them, and re-layouts  2.14 us (2%)
  between operations  1.47 us (1%)
    pallas_call x1, Pallas kernels, local_pull(): pl.pallas_call(local_kernel, out_shape=(jax.ShapeDtypeStruct((3, groups,...  34.5 us
    pallas_call x1, Pallas kernels, remote_pull(): pl.pallas_call(remote_kernel, out_shape=jax.ShapeDtypeStruct((6, groups,...  25.6 us
    all_to_all x1, blocking collectives, per_device(): got = lax.all_to_all(asked, AXES, split_axis=0, concat_axis=0, tiled=True)  21.1 us
    all_to_all x1, waiting for transfers between devices, per_device(): recv = lax.all_to_all(opened, AXES, split_axis=0, concat_axis=0, tiled=True)  15.8 us
    ppermute x1, waiting for transfers between devices, shifted(): lax.ppermute(value, axis, [(source, source + steps) for source in range(c...  6.67 us
    all_to_all x1, starting transfers between devices, per_device(): recv = lax.all_to_all(opened, AXES, split_axis=0, concat_axis=0, tiled=True)  5.76 us
    pallas_call x1, Pallas kernels, open_leaves(): pl.pallas_call(open_kernel, out_shape=jax.ShapeDtypeStruct(shape, f32), i...  4.55 us
  transfers between devices with their start and end apart: 2, of which 2 were waited for; matrix products, arithmetic and copies ran while one was open for 1% of the time, Pallas kernels for 29%

profile of v8, /device:TPU:1, one launch (start us, length us, event | category | flops | bytes accessed | tf_op | source)
XLA Modules:
  0.0 120.6 jit_solution(8145695205369402746)
XLA Ops:
  0.7 0.7 pad_bitcast_fusion
  1.4 0.1 copy.14
  1.5 21.1 %all_to_all.16 = s32[128,1,17]{2,1,0:T(1,128)} all-to-all(s32[128,1,17]{2,1,0:T(1,128)S(1)} %copy.14), channel_id=1, replica_groups=mesh['dom'=8,'bulk'=16] {'dom','bulk'}, dimensions={0} | all-to-all | bytes 17408 | tf_op jit(solution)/shard_map/all_to_all | solution.py:384
  22.6 4.6 %open_leaves.1 = f32[128,64,128]{2,1,0:T(8,128)} custom-call(s32[128,17]{1,0:T(8,128)} %bitcast.26, f32[3,512,128]{2,1,0:T(8,128)} %bitcast.25, f32[512,128]{1,0:T(8,128)} %mass_hbm.1), custom_call_target="tpu_custom_call" | custom-call | tf_op jit(solution)/shard_map/open_leaves/pallas_call | solution.py:129
  27.2 0.0 copy-start
  27.2 0.0 copy-start.2
  27.2 0.0 copy-start.3
  27.2 0.0 copy-start.4
  27.2 0.0 copy-start.5
  27.2 0.0 copy-start.6
  27.2 5.8 %all-to-all-start.1 = ((f32[128,64,128]{2,1,0:T(8,128)}), f32[128,64,128]{2,1,0:T(8,128)}, u32[]{:S(2)}, u32[]{:S(2)}) async-start(f32[128,64,128]{2,1,0:T(8,128)} %open_leaves.1), calls=%async_computation.1 | async-start | bytes 8388608 | tf_op jit(solution)/shard_map/all_to_all | solution.py:391
  33.0 1.2 constant_dynamic-slice_fusion
  34.9 0.1 pad_dynamic-slice_fusion.2
  35.0 0.0 copy-done
  35.0 0.0 copy-done.2
  35.0 0.0 copy-done.3
  35.0 0.0 copy-done.4
  35.0 0.0 copy-done.5
  35.0 0.0 copy-done.6
  35.0 0.0 copy-start.1
  35.0 34.5 %local_pull.1 = (f32[3,256,128]{2,1,0:T(8,128)S(1)}, s32[1152]{0:T(1024)S(1)}) custom-call(s32[8,128]{1,0:T(8,128)S(1)} %bitcast.22, s32[128]{0:T(128)S(1)} %bitcast.24, f32[3,256,128]{2,1,0:T(8,128)S(1)} %bitcast.19, f32[3,512]{1,0:T(4,128)S(1)} %copy-done.3, f32[1,512]{1,0:T(1,128)S(1)} %bitcast.23, s32[256,512]{1,0:T(8,128)S(1)} %copy-done.2), custom_call_target="tpu_custom_call" | custom-call | flops 33554432000 | bytes 4194304 | tf_op jit(solution)/shard_map/local_pull/pallas_call | solution.py:236
  69.5 15.8 %all-to-all-done.1 = f32[128,64,128]{2,1,0:T(8,128)} async-done(((f32[128,64,128]{2,1,0:T(8,128)}), f32[128,64,128]{2,1,0:T(8,128)}, u32[]{:S(2)}, u32[]{:S(2)}) %all-to-all-start.1) | async-done | bytes 4194336 | tf_op jit(solution)/shard_map/all_to_all | solution.py:391
  85.2 0.0 copy-done.1
  85.2 25.6 %remote_pull.1 = f32[6,256,128]{2,1,0:T(8,128)S(1)} custom-call(s32[1152]{0:T(1024)S(1)} %get-tuple-element.10.todo_ref, f32[8192,128]{1,0:T(8,128)} %bitcast.10.recv_ref, f32[3,256,128]{2,1,0:T(8,128)S(1)} %bitcast.20, f32[3,256,128]{2,1,0:T(8,128)S(1)} %bitcast.21, f32[3,256,128]{2,1,0:T(8,128)S(1)} %get-tuple-element.12.local_ref), custom_call_target="tpu_custom_call" | custom-call | tf_op jit(solution)/shard_map/remote_pull/pallas_call | solution.py:341
  110.8 1.9 %collective-permute-start = (f32[6,16,128]{2,1,0:T(8,128)S(1)}, f32[6,16,128]{2,1,0:T(8,128)S(1)}, u32[]{:S(2)}, u32[]{:S(2)}) collective-permute-start(f32[6,16,128]{2,1,0:T(8,128)S(1)} %slice.4), channel_id=1, source_target_pairs={{0,1},{1,2},{2,3},{3,4},{4,5},{5,6},{6,7},{7,8},{8,9},{9,10},{10,1... | collective-permute-start | bytes 147464 | tf_op jit(solution)/shard_map/ppermute | solution.py:363
  112.8 0.1 broadcast_multiply_fusion
  112.9 6.7 %collective-permute-done = f32[6,16,128]{2,1,0:T(8,128)S(1)} collective-permute-done((f32[6,16,128]{2,1,0:T(8,128)S(1)}, f32[6,16,128]{2,1,0:T(8,128)S(1)}, u32[]{:S(2)}, u32[]{:S(2)}) %collective-permute-start) | collective-permute-done | bytes 49184 | tf_op jit(solution)/shard_map/ppermute | solution.py:363
  119.6 1.0 fusion.2
  (3 shorter events, 0.0 us)
Async XLA Ops:
  27.2 7.8 %copy-start = (f32[256,3,128]{2,0,1:T(8,128)S(1)}, f32[256,3,128]{2,0,1:T(8,128)}, u32[]{:S(2)}) copy-start(f32[256,3,128]{2,0,1:T(8,128)} %param.11) | copy-start | bytes 1179652
  27.2 7.8 %copy-start.2 = (s32[256,512]{1,0:T(8,128)S(1)}, s32[256,512]{1,0:T(8,128)}, u32[]{:S(2)}) copy-start(s32[256,512]{1,0:T(8,128)} %list_ref.1) | copy-start | bytes 1572868
  27.2 7.8 %copy-start.3 = (f32[3,512]{1,0:T(4,128)S(1)}, f32[3,512]{1,0:T(4,128)}, u32[]{:S(2)}) copy-start(f32[3,512]{1,0:T(4,128)} %node_ref.1) | copy-start | bytes 18436
  27.2 7.8 %copy-start.4 = (s32[1,128,8]{1,2,0:T(8,128)S(1)}, s32[1,128,8]{1,2,0:T(8,128)}, u32[]{:S(2)}) copy-start(s32[1,128,8]{1,2,0:T(8,128)} %param.18) | copy-start | bytes 12292
  27.2 7.8 %copy-start.5 = (f32[512]{0:T(512)S(1)}, f32[512]{0:T(512)}, u32[]{:S(2)}) copy-start(f32[512]{0:T(512)} %param.16) | copy-start | bytes 6148
  27.2 7.8 %copy-start.6 = (s32[1,128]{1,0:T(1,128)S(1)}, s32[1,128]{1,0:T(1,128)}, u32[]{:S(2)}) copy-start(s32[1,128]{1,0:T(1,128)} %param.20) | copy-start | bytes 1540
  27.2 58.0 %all-to-all-start.1 = ((f32[128,64,128]{2,1,0:T(8,128)}), f32[128,64,128]{2,1,0:T(8,128)}, u32[]{:S(2)}, u32[]{:S(2)}) async-start(f32[128,64,128]{2,1,0:T(8,128)} %open_leaves.1), calls=%async_computation.1 | async-start | bytes 8388608 | tf_op jit(solution)/shard_map/all_to_all | solution.py:391
  35.0 50.2 %copy-start.1 = (f32[256,3,128]{2,0,1:T(8,128)S(1)}, f32[256,3,128]{2,0,1:T(8,128)}, u32[]{:S(2)}) copy-start(f32[256,3,128]{2,0,1:T(8,128)} %param.12) | copy-start | bytes 1179652
  110.8 8.7 %collective-permute-start = (f32[6,16,128]{2,1,0:T(8,128)S(1)}, f32[6,16,128]{2,1,0:T(8,128)S(1)}, u32[]{:S(2)}, u32[]{:S(2)}) collective-permute-start(f32[6,16,128]{2,1,0:T(8,128)S(1)} %slice.4), channel_id=1, source_target_pairs={{0,1},{1,2},{2,3},{3,4},{4,5},{5,6},{6,7},{7,8},{8,9},{9,10},{10,1... | collective-permute-start | bytes 147464 | tf_op jit(solution)/shard_map/ppermute | solution.py:363
